TPU v7x, 32 devices: a whole 2x2x4 slice. The times are simulated.
32 devices in a mesh: grp: 2 (over y), dp: 8 (over z, x), head: 2 (over core).
Axes of the slice: x: 2, y: 2, z: 4, core: 2. Of those that a mesh axis runs over, the one named last changes fastest.
Arguments:
- tokens: bfloat16 [2, 896, 4096], P(None, ('grp', 'dp'), 'head'), parts along dimension 1, may hold values from -6 to 6
- inner_weight: bfloat16 [4096, 256], P(None, 'head'), may hold values from -0.09375 to 0.09375
- gate_weight: bfloat16 [4096, 256], P(None, 'head'), may hold values from -0.09375 to 0.09375
- group_weight: bfloat16 [4096, 128], P(None, 'head'), may hold values from -0.09375 to 0.09375
- delta_weight: bfloat16 [4096, 2], P(None, 'head'), may hold values from -0.09375 to 0.09375
- inner_taps: float32 [4, 256], P(None, 'head'), may hold values from -1 to 1
- inner_offset: float32 [256], P('head'), may hold values from -0.5 to 0.5
- group_taps: float32 [4, 128], P(None, 'head'), may hold values from -1 to 1
- group_offset: float32 [128], P('head'), may hold values from -0.5 to 0.5
- decay_log: float32 [2], P('head'), may hold values from -2.3 to 0.5
- delta_bias: float32 [2], P('head'), may hold values from -1 to 1
- skip_gain: float32 [2], P('head'), may hold values from 0.5 to 2
- inner_window: bfloat16 [896, 3, 256], P(('grp', 'dp'), None, 'head'), parts along dimension 0, may hold values from -6 to 6
- group_window: bfloat16 [896, 3, 128], P(('grp', 'dp'), None, 'head'), parts along dimension 0, may hold values from -6 to 6
- scan_state: bfloat16 [896, 256, 64], P(('grp', 'dp'), 'head'), parts along dimension 0, may hold values from -6 to 6
- send_list: int32 [16, 56], P(('grp', 'dp')), parts along dimension 0, may hold values from -1 to 55, as said below
- receive_list: int32 [16, 56], P(('grp', 'dp')), parts along dimension 0, may hold values from -1 to 55, as said below
- live_count: int32 [16], P(('grp', 'dp')), parts along dimension 0, may hold values from 1 to 56, as said below
Outputs:
- gated_output: bfloat16 [2, 896, 256], P(None, ('grp', 'dp'), 'head'), parts along dimension 1
- inner_next: bfloat16 [896, 3, 256], P(('grp', 'dp'), None, 'head'), parts along dimension 0
- group_next: bfloat16 [896, 3, 128], P(('grp', 'dp'), None, 'head'), parts along dimension 0
- scan_next: bfloat16 [896, 256, 64], P(('grp', 'dp'), 'head'), parts along dimension 0
There are 2 independent parts, one for each index of `grp`. A program takes and returns all parts, laid end to end along the dimension named above; an argument that names none is the same for every part. Nothing has to cross between parts.
Inputs may be any that keep to these rules, and one draw needn't show every extreme that they name: `send_list`: row s lists, at position d * 7 + c, the local slot of old replica s whose states become the c-th arrival at replica d, or -1; each replica sends exactly 28 distinct slots, exactly 7 to each of 4 other replicas and none to itself. `receive_list`: entry d, k is -1 when new slot k of replica d keeps the state of old slot k of the same replica, else s * 7 * 7 + c (7 = 1) where the c-th state that replica s sends to replica d is the one it takes; a slot takes an arrival exactly when replica d sends its own old slot k away; it agrees with send_list. `live_count`: some replica is full and some holds a single live request.
All inputs are finite; a program needn't handle non-finite values.
Results may differ from a plain program's by a relative error of at most 0.008.
Values may be sent and summed in bfloat16 or wider, within the bound.
No kernel may reach another device: no remote copies, remote signals or barrier semaphores. Data moves between devices by JAX's collectives and lax.ppermute only.
A program may use at most 64 MiB of HBM per device.

v0:
```python
import jax
import jax.numpy as jnp
from jax import lax
from jax.sharding import PartitionSpec as P

P_SIZE = 128


def convolve(carried, incoming, taps, offset):
    tap_count = taps.shape[0]
    step_count = incoming.shape[0]
    joined = jnp.concatenate([carried, jnp.transpose(incoming, (1, 0, 2))], axis=1)
    widened = joined.astype(jnp.float32)
    outputs = []
    for position in range(step_count):
        window = widened[:, position : position + tap_count]
        summed = jnp.sum(window * taps[None], axis=1) + offset[None]
        outputs.append(jax.nn.silu(summed).astype(jnp.bfloat16))
    return (jnp.stack(outputs), joined[:, step_count:])


def recurrence(inner_conv, gate_raw, group_conv, delta_rate, decay_rate, carried, skip_value):
    state_width = group_conv.shape[2] // 2
    hidden = carried.astype(jnp.float32)
    rounded = carried
    outputs = []
    for position in range(inner_conv.shape[0]):
        inner_now = inner_conv[position].astype(jnp.float32)
        input_map = group_conv[position, :, :state_width].astype(jnp.float32)
        output_map = group_conv[position, :, state_width:].astype(jnp.float32)
        hidden = (
            decay_rate[position][:, :, None] * hidden
            + (delta_rate[position] * inner_now)[:, :, None] * input_map[:, None, :]
        )
        output = jnp.sum(hidden * output_map[:, None, :], axis=2) + skip_value[None, :] * inner_now
        outputs.append(
            (output * jax.nn.silu(gate_raw[position].astype(jnp.float32))).astype(jnp.bfloat16)
        )
        rounded = hidden.astype(jnp.bfloat16)
        hidden = lax.optimization_barrier(rounded).astype(jnp.float32)
    return (jnp.stack(outputs), rounded)


def advance(
    inner_raw, gate_raw, group_raw, delta_raw, inner_carried, group_carried, scan_carried, params
):
    inner_taps, inner_offset, group_taps, group_offset, decay_log, delta_bias, skip_gain = params
    inner_conv, inner_carry = convolve(inner_carried, inner_raw, inner_taps, inner_offset)
    group_half, group_carry = convolve(group_carried, group_raw, group_taps, group_offset)
    group_conv = lax.all_gather(group_half, "head", axis=2, tiled=True)
    delta_head = jax.nn.softplus(delta_raw.astype(jnp.float32) + delta_bias)
    decay_head = jnp.exp(-delta_head * jnp.exp(decay_log))
    delta_rate = jnp.repeat(delta_head, P_SIZE, axis=-1)
    decay_rate = jnp.repeat(decay_head, P_SIZE, axis=-1)
    skip_value = jnp.repeat(skip_gain, P_SIZE)
    gated, scan_carry = recurrence(
        inner_conv, gate_raw, group_conv, delta_rate, decay_rate, scan_carried, skip_value
    )
    return (gated, inner_carry, group_carry, scan_carry)


def pick_rows(member, send_index, occupied):
    clipped = jnp.where(occupied, send_index, 0)
    expand = (occupied.shape[0],) + (1,) * (member.ndim - 1)
    return jnp.where(occupied.reshape(expand), member[clipped], jnp.zeros((), member.dtype))


def settle(arrived, own, moved, clipped):
    expand = (moved.shape[0],) + (1,) * (own.ndim - 1)
    return jnp.where(moved.reshape(expand), arrived[clipped], own)


def per_device(
    tokens,
    inner_weight,
    gate_weight,
    group_weight,
    delta_weight,
    inner_taps,
    inner_offset,
    group_taps,
    group_offset,
    decay_log,
    delta_bias,
    skip_gain,
    inner_window,
    group_window,
    scan_state,
    send_list,
    receive_list,
    live_count,
):
    step_count, slot_count, half_width = tokens.shape
    token_rows = tokens.reshape(step_count * slot_count, half_width)
    weights = (inner_weight, gate_weight, group_weight, delta_weight)
    block_rows = lax.all_gather(token_rows, "head", axis=1, tiled=True)
    projected = tuple(
        (jnp.dot(block_rows, weight, preferred_element_type=jnp.float32) for weight in weights)
    )
    inner_raw, gate_raw, group_raw, delta_raw = (
        column_block.astype(jnp.bfloat16).reshape(step_count, slot_count, -1)
        for column_block in projected
    )
    send_index = send_list[0]
    occupied = send_index >= 0
    receive_index = receive_list[0]
    moved = receive_index >= 0
    clipped = jnp.where(moved, receive_index, 0)
    living = jnp.arange(slot_count) < live_count[0]
    params = (inner_taps, inner_offset, group_taps, group_offset, decay_log, delta_bias, skip_gain)
    arrived = (
        lax.all_to_all(
            pick_rows(inner_window, send_index, occupied),
            "dp",
            split_axis=0,
            concat_axis=0,
            tiled=True,
        ),
        lax.all_to_all(
            pick_rows(group_window, send_index, occupied),
            "dp",
            split_axis=0,
            concat_axis=0,
            tiled=True,
        ),
        lax.all_to_all(
            pick_rows(scan_state, send_index, occupied),
            "dp",
            split_axis=0,
            concat_axis=0,
            tiled=True,
        ),
    )
    inner_here = settle(arrived[0], inner_window, moved, clipped)
    group_here = settle(arrived[1], group_window, moved, clipped)
    scan_here = settle(arrived[2], scan_state, moved, clipped)
    gated, inner_carry, group_carry, scan_carry = advance(
        inner_raw, gate_raw, group_raw, delta_raw, inner_here, group_here, scan_here, params
    )
    zero = jnp.zeros((), jnp.bfloat16)
    gated_output = jnp.where(living[None, :, None], gated, zero)
    inner_next = jnp.where(living[:, None, None], inner_carry, zero)
    group_next = jnp.where(living[:, None, None], group_carry, zero)
    scan_next = jnp.where(living[:, None, None], scan_carry, zero)
    return (gated_output, inner_next, group_next, scan_next)


def solution(mesh):
    in_specs = (
        P(None, ("grp", "dp"), "head"),
        P(None, "head"),
        P(None, "head"),
        P(None, "head"),
        P(None, "head"),
        P(None, "head"),
        P("head"),
        P(None, "head"),
        P("head"),
        P("head"),
        P("head"),
        P("head"),
        P(("grp", "dp"), None, "head"),
        P(("grp", "dp"), None, "head"),
        P(("grp", "dp"), "head", None),
        P(("grp", "dp"), None),
        P(("grp", "dp"), None),
        P(("grp", "dp")),
    )
    out_specs = (
        P(None, ("grp", "dp"), "head"),
        P(("grp", "dp"), None, "head"),
        P(("grp", "dp"), None, "head"),
        P(("grp", "dp"), "head", None),
    )
    return jax.shard_map(
        per_device, mesh=mesh, in_specs=in_specs, out_specs=out_specs, check_vma=False
    )
```

profile of v0, /device:TPU:0, one launch (start us, length us, event | category | flops | bytes accessed | tf_op | source)
XLA Modules:
  0.0 72.5 jit_solution(15879744960141586794)
XLA Ops:
  0.6 0.0 copy-start
  0.7 0.8 %compare_bitcast_fusion = pred[56]{0:T(512)(128)(4,1)S(1)} fusion(s32[1,56]{1,0:T(1,128)} %param.33), kind=kLoop, calls=%fused_computation.87 | loop fusion | flops 56 | bytes 280 | tf_op jit(solution)/shard_map/ge | solution.py:105
  1.5 0.7 fusion.30
  2.1 1.6 %gather_fusion.4 = bf16[56,3,64]{2,0,1:T(8,128)(2,1)S(1)} fusion(bf16[56,3,64]{2,0,1:T(8,128)(2,1)} %param.31, s32[1024]{0:T(1024)S(1)} %pad_clamp_fusion.1), kind=kCustom, calls=%fused_computation.4 | custom fusion | bytes 43232 | tf_op jit(solution)/shard_map/gather | solution.py:65
  3.7 0.1 broadcast_select_fusion.2
  3.8 0.7 reshape.469
  4.5 7.3 %all-to-all-start.2 = ((bf16[8,2,672]{2,1,0:T(2,128)(2,1)}), bf16[8,2,672]{2,1,0:T(2,128)(2,1)}, u32[]{:S(2)}, u32[]{:S(2)}) async-start(bf16[8,2,672]{2,1,0:T(2,128)(2,1)} %reshape.469), calls=%async_computation.2 | async-start | bytes 49152 | tf_op jit(solution)/shard_map/all_to_all | solution.py:119
  11.8 0.7 compare_bitcast_fusion.1
  12.5 0.7 fusion.31
  15.1 0.8 %gather_fusion.2 = bf16[56,3,128]{2,0,1:T(8,128)(2,1)S(1)} fusion(bf16[56,3,128]{2,0,1:T(8,128)(2,1)S(1)} %copy-done.3, s32[1024]{0:T(1024)S(1)} %pad_clamp_fusion.1), kind=kCustom, calls=%fused_computation.2 | custom fusion | bytes 86240 | tf_op jit(solution)/shard_map/gather | solution.py:65
  15.9 0.1 broadcast_select_fusion.3
  16.0 0.7 gather_fusion
  16.7 0.0 copy-start.6
  16.7 1.1 %broadcast_select_fusion = bf16[56,128,64]{1,2,0:T(8,128)(2,1)} fusion(bf16[56,128,64]{1,2,0:T(8,128)(2,1)S(1)} %gather_fusion, pred[56]{0:T(512)(128)(4,1)S(1)} %compare_bitcast_fusion), kind=kLoop, calls=%fused_computation.20 | loop fusion | flops 458752 | bytes 1835064 | tf_op jit(solution)/shard_map/jit(_where)/select_n | solution.py:65
  17.8 2.6 %all_gather.6 = bf16[112,4096]{1,0:T(8,128)(2,1)S(1)} all-gather(bf16[112,2048]{1,0:T(8,128)(2,1)S(1)} %bitcast.66), channel_id=1, replica_groups=mesh['grp'=2,'dp'=8,'head'=2] {'head'}, dimensions={1}, use_global_device_ids=true | all-gather | bytes 1376256 | tf_op jit(solution)/shard_map/all_gather | solution.py:96
  20.4 0.3 fusion.4
  20.7 0.1 add.174
  20.8 1.1 %convolution_convert_fusion.2 = bf16[112,64]{0,1:T(8,128)(2,1)} fusion(bf16[112,4096]{1,0:T(8,128)(2,1)S(1)} %all_gather.6, bf16[4096,64]{0,1:T(8,128)(2,1)S(1)} %copy-done.5), kind=kOutput, calls=%fused_computation.14 | convolution fusion | flops 58727424 | bytes 1456128 | tf_op jit(solution)/shard_map/dot_general | solution.py:98
  21.9 0.4 convolution_convert_fusion
  22.3 0.8 %copy-done.4 = bf16[4096,128]{1,0:T(8,128)(2,1)S(1)} copy-done((bf16[4096,128]{1,0:T(8,128)(2,1)S(1)}, bf16[4096,128]{1,0:T(8,128)(2,1)}, u32[]{:S(2)}) %copy-start.4) | copy-done | bytes 1048600
  23.1 0.4 convolution_convert_fusion.1
  24.2 0.6 copy.37
  24.9 0.1 copy.47
  25.0 6.0 %all-to-all-start.1 = ((bf16[56,3,128]{2,1,0:T(4,128)(2,1)}), bf16[56,3,128]{2,1,0:T(4,128)(2,1)S(1)}, u32[]{:S(2)}, u32[]{:S(2)}) async-start(bf16[56,3,128]{2,1,0:T(4,128)(2,1)} %copy.37), calls=%async_computation.1 | async-start | bytes 114688 | tf_op jit(solution)/shard_map/all_to_all | solution.py:112
  31.0 0.9 %reshape.470 = bf16[56,3,64]{2,1,0:T(4,128)(2,1)S(1)} reshape(bf16[8,2,672]{2,1,0:T(2,128)(2,1)} %all-to-all-done.2) | data formatting | bytes 43008
  31.9 0.6 gather_fusion.5
  32.5 0.1 copy_select_fusion
  32.7 5.2 %all-to-all-done.1 = bf16[56,3,128]{2,1,0:T(4,128)(2,1)S(1)} async-done(((bf16[56,3,128]{2,1,0:T(4,128)(2,1)}), bf16[56,3,128]{2,1,0:T(4,128)(2,1)S(1)}, u32[]{:S(2)}, u32[]{:S(2)}) %all-to-all-start.1) | async-done | bytes 43040 | tf_op jit(solution)/shard_map/all_to_all | solution.py:112
  37.9 3.6 %all-to-all-start = ((bf16[56,128,64]{1,2,0:T(8,128)(2,1)}), bf16[56,128,64]{1,2,0:T(8,128)(2,1)S(1)}, u32[]{:S(2)}, u32[]{:S(2)}) async-start(bf16[56,128,64]{1,2,0:T(8,128)(2,1)} %broadcast_select_fusion), calls=%async_computation | async-start | bytes 1835008 | tf_op jit(solution)/shard_map/all_to_all | solution.py:126
  41.5 0.1 copy.42
  41.6 1.9 %all_gather.7 = bf16[2,56,128]{1,0,2:T(2,128)(2,1)S(1)} all-gather(bf16[2,56,64]{1,0,2:T(2,128)(2,1)S(1)} %copy.42), channel_id=1, replica_groups=mesh['grp'=2,'dp'=8,'head'=2] {'head'}, dimensions={2}, use_global_device_ids=true | all-gather | bytes 43008 | tf_op jit(solution)/shard_map/all_gather | solution.py:50
  43.5 0.1 slice_convert_fusion.2
  43.6 0.1 copy.44
  43.7 0.1 copy.46
  43.7 0.1 copy.45
  43.8 0.1 copy.43
  43.9 0.7 fusion.13
  44.6 0.6 gather_fusion.3
  45.2 0.1 copy_select_fusion.1
  45.4 0.7 fusion.15
  46.1 0.1 convert_multiply_fusion.2
  46.2 17.5 %all-to-all-done = bf16[56,128,64]{1,2,0:T(8,128)(2,1)S(1)} async-done(((bf16[56,128,64]{1,2,0:T(8,128)(2,1)}), bf16[56,128,64]{1,2,0:T(8,128)(2,1)S(1)}, u32[]{:S(2)}, u32[]{:S(2)}) %all-to-all-start) | async-done | bytes 917536 | tf_op jit(solution)/shard_map/all_to_all | solution.py:126
  63.7 1.6 %gather_fusion.1 = bf16[56,128,64]{1,2,0:T(8,128)(2,1)} fusion(bf16[56,128,64]{1,2,0:T(8,128)(2,1)S(1)} %all-to-all-done, s32[1024]{0:T(1024)S(1)} %pad_clamp_fusion), kind=kCustom, calls=%fused_computation.1 | custom fusion | bytes 1835232 | tf_op jit(solution)/shard_map/gather | solution.py:70
  65.3 3.1 %multiply_reduce_fusion.1 = (f32[56,128]{1,0:T(8,128)S(1)}, bf16[56,128,64]{1,2,0:T(8,128)(2,1)S(1)}) fusion(f32[56,64]{1,0:T(8,128)S(1)} %copy.44, f32[56,64]{1,0:T(8,128)S(1)} %copy.43, f32[56,128]{1,0:T(8,128)S(1)} %get-tuple-element.23, f32[56]{0:T(128)S(1)} %get-tuple-element.26, bf16[56,128,64]{1,2,0:T(8,128)(2,1)} %gather_fusion.1, ...), kind=kLoop, calls=%fused_computation.9 | loop fusion | flops 3662848 | bytes 2838808 | tf_op jit(solution)/shard_map/reduce_sum | solution.py:35
  68.3 2.0 %fusion.5 = bf16[56,128,64]{1,2,0:T(8,128)(2,1)} fusion(bf16[56,128,64]{1,2,0:T(8,128)(2,1)S(1)} %get-tuple-element.11, f32[56,64]{1,0:T(8,128)S(1)} %copy.45, f32[56,128]{1,0:T(8,128)S(1)} %get-tuple-element.22, f32[56]{0:T(128)S(1)} %get-tuple-element.27, pred[56]{0:T(512)(128)(4,1)S(1)} %iota_compare_fusion), kind=kLoop, calls=%fused_computation.19 | loop fusion | flops 2752512 | bytes 1878296 | tf_op jit(solution)/shard_map/jit(_where)/select_n | solution.py:144
  70.3 1.4 %multiply_reduce_fusion = f32[56,128]{1,0:T(8,128)S(1)} fusion(bf16[56,128,64]{1,2,0:T(8,128)(2,1)S(1)} %get-tuple-element.11, f32[56,64]{1,0:T(8,128)S(1)} %copy.46, f32[56,64]{1,0:T(8,128)S(1)} %copy.45, f32[56,128]{1,0:T(8,128)S(1)} %get-tuple-element.22, f32[56]{0:T(128)S(1)} %get-tuple-element.27), kind=kLoop, calls=%fused_computation.6 | loop fusion | flops 2745344 | bytes 1003744 | tf_op jit(solution)/shard_map/reduce_sum | solution.py:35
  71.8 0.1 fusion.29
  71.8 0.7 maximum_select_fusion
  (36 shorter events, 0.2 us)
Async XLA Ops:
  0.6 21.3 %copy-start = (bf16[4096,128]{1,0:T(8,128)(2,1)S(1)}, bf16[4096,128]{1,0:T(8,128)(2,1)}, u32[]{:S(2)}) copy-start(bf16[4096,128]{1,0:T(8,128)(2,1)} %param.20) | copy-start | bytes 3145732
  0.6 14.5 %copy-start.3 = (bf16[56,3,128]{2,0,1:T(8,128)(2,1)S(1)}, bf16[56,3,128]{2,0,1:T(8,128)(2,1)}, u32[]{:S(2)}) copy-start(bf16[56,3,128]{2,0,1:T(8,128)(2,1)} %param.30) | copy-start | bytes 129028
  0.7 15.3 %copy-start.1 = (bf16[56,128,64]{1,2,0:T(8,128)(2,1)S(1)}, bf16[56,128,64]{1,2,0:T(8,128)(2,1)}, u32[]{:S(2)}) copy-start(bf16[56,128,64]{1,2,0:T(8,128)(2,1)} %param.32) | copy-start | bytes 2752516
  4.5 20.5 %all-to-all-start.2 = ((bf16[8,2,672]{2,1,0:T(2,128)(2,1)}), bf16[8,2,672]{2,1,0:T(2,128)(2,1)}, u32[]{:S(2)}, u32[]{:S(2)}) async-start(bf16[8,2,672]{2,1,0:T(2,128)(2,1)} %reshape.469), calls=%async_computation.2 | async-start | bytes 49152 | tf_op jit(solution)/shard_map/all_to_all | solution.py:119
  16.7 1.1 %copy-start.6 = (bf16[2,56,2048]{2,1,0:T(8,128)(2,1)S(1)}, bf16[2,56,2048]{2,1,0:T(8,128)(2,1)}, u32[]{:S(2)}) copy-start(bf16[2,56,2048]{2,1,0:T(8,128)(2,1)} %param.18) | copy-start | bytes 1376260
  17.8 2.6 %copy-start.8 = (bf16[4096,1]{0,1:T(2,128)(2,1)S(1)}, bf16[4096,1]{0,1:T(2,128)(2,1)}, u32[]{:S(2)}) copy-start(bf16[4096,1]{0,1:T(2,128)(2,1)} %param.22) | copy-start | bytes 24580
  17.8 3.0 %copy-start.5 = (bf16[4096,64]{0,1:T(8,128)(2,1)S(1)}, bf16[4096,64]{0,1:T(8,128)(2,1)}, u32[]{:S(2)}) copy-start(bf16[4096,64]{0,1:T(8,128)(2,1)} %param.21) | copy-start | bytes 1572868
  21.9 1.2 %copy-start.4 = (bf16[4096,128]{1,0:T(8,128)(2,1)S(1)}, bf16[4096,128]{1,0:T(8,128)(2,1)}, u32[]{:S(2)}) copy-start(bf16[4096,128]{1,0:T(8,128)(2,1)} %param.19) | copy-start | bytes 3145732
  23.1 1.8 %copy-start.7 = (bf16[112,64]{0,1:T(8,128)(2,1)S(1)}, bf16[112,64]{0,1:T(8,128)(2,1)}, u32[]{:S(2)}) copy-start(bf16[112,64]{0,1:T(8,128)(2,1)} %convolution_convert_fusion.2) | copy-start | bytes 43012
  23.1 9.4 %copy-start.2 = (bf16[56,3,64]{2,0,1:T(8,128)(2,1)S(1)}, bf16[56,3,64]{2,0,1:T(8,128)(2,1)}, u32[]{:S(2)}) copy-start(bf16[56,3,64]{2,0,1:T(8,128)(2,1)} %param.31) | copy-start | bytes 64516
  23.1 9.5 %copy-start.9 = (f32[4,64]{1,0:T(4,128)S(1)}, f32[4,64]{1,0:T(4,128)}, u32[]{:S(2)}) copy-start(f32[4,64]{1,0:T(4,128)} %param.25) | copy-start | bytes 3076
  25.0 12.9 %all-to-all-start.1 = ((bf16[56,3,128]{2,1,0:T(4,128)(2,1)}), bf16[56,3,128]{2,1,0:T(4,128)(2,1)S(1)}, u32[]{:S(2)}, u32[]{:S(2)}) async-start(bf16[56,3,128]{2,1,0:T(4,128)(2,1)} %copy.37), calls=%async_computation.1 | async-start | bytes 114688 | tf_op jit(solution)/shard_map/all_to_all | solution.py:112
  32.6 8.8 %copy-start.12 = (f32[64]{0:T(128)S(1)}, f32[64]{0:T(128)}, u32[]{:S(2)}) copy-start(f32[64]{0:T(128)} %param.26) | copy-start | bytes 772
  37.9 25.8 %all-to-all-start = ((bf16[56,128,64]{1,2,0:T(8,128)(2,1)}), bf16[56,128,64]{1,2,0:T(8,128)(2,1)S(1)}, u32[]{:S(2)}, u32[]{:S(2)}) async-start(bf16[56,128,64]{1,2,0:T(8,128)(2,1)} %broadcast_select_fusion), calls=%async_computation | async-start | bytes 1835008 | tf_op jit(solution)/shard_map/all_to_all | solution.py:126
  41.4 3.9 %copy-start.10 = (f32[4,128]{1,0:T(4,128)S(1)}, f32[4,128]{1,0:T(4,128)}, u32[]{:S(2)}) copy-start(f32[4,128]{1,0:T(4,128)} %param.23) | copy-start | bytes 6148
  41.4 4.6 %copy-start.11 = (f32[128]{0:T(128)S(1)}, f32[128]{0:T(128)}, u32[]{:S(2)}) copy-start(f32[128]{0:T(128)} %param.24) | copy-start | bytes 1540
where the time goes:
time: 73.2 us; the launch traced here: 72.5 us
  waiting for transfers between devices  22.7 us (31%)
  starting transfers between devices  16.8 us (23%)
  other arithmetic  13.1 us (18%)
  local copies, waits for them, and re-layouts  9.68 us (13%)
  blocking collectives  4.43 us (6%)
  between operations  3.55 us (5%)
  matrix products  2.24 us (3%)
    all_to_all x1, waiting for transfers between devices, per_device(): lax.all_to_all(pick_rows(scan_state, send_index, occupied), 'dp', split_a...  17.5 us
    all_to_all x1, starting transfers between devices, per_device(): lax.all_to_all(pick_rows(group_window, send_index, occupied), 'dp', split...  7.25 us
    all_to_all x1, starting transfers between devices, per_device(): lax.all_to_all(pick_rows(inner_window, send_index, occupied), 'dp', split...  6.01 us
    all_to_all x1, waiting for transfers between devices, per_device(): lax.all_to_all(pick_rows(inner_window, send_index, occupied), 'dp', split...  5.19 us
    reduce_sum x2, other arithmetic, recurrence(): jnp.sum(hidden * output_map[:, None, :], axis=2)  4.51 us
    all_to_all x1, starting transfers between devices, per_device(): lax.all_to_all(pick_rows(scan_state, send_index, occupied), 'dp', split_a...  3.55 us
    gather x3, local copies, waits for them, and re-layouts, pick_rows(): member[clipped]  3.08 us
    gather x3, local copies, waits for them, and re-layouts, settle(): return jnp.where(moved.reshape(expand), arrived[clipped], own)  2.89 us
  transfers between devices with their start and end apart: 3, of which 2 were waited for; matrix products, arithmetic and copies ran while one was open for 16% of the time, Pallas kernels for 0%

commit v1 on v0

v1 whole, which is shorter than its diff:
```python
import functools

import jax
import jax.numpy as jnp
from jax import lax
from jax.experimental import pallas as pl
from jax.experimental.pallas import tpu as pltpu
from jax.sharding import PartitionSpec as P

F32 = jnp.float32
BF16 = jnp.bfloat16
VMEM_LIMIT = 32 * 1024 * 1024
MAX_SHIFTS = 16
LANES = 128


def round_up(value, step):
    return -(-value // step) * step


def silu(value):
    return value * jax.nn.sigmoid(value)


def block_rows_of(replicas):
    return 1 if replicas <= MAX_SHIFTS else replicas


def pack_kernel(replicas, cap, cap_rows, send, scan, inner, group, *refs):
    per_block = block_rows_of(replicas)
    count = replicas - 1 if per_block == 1 else 1
    state_out, window_out = refs[:count], refs[count : 2 * count]
    table, picked, sem = refs[2 * count :]
    me = lax.axis_index("dp")
    plan = []
    for block in range(count):
        for inside in range(per_block):
            target = lax.rem(me + block + 1, replicas) if per_block == 1 else inside
            for c in range(cap):
                plan.append((block, inside * cap + c, inside * cap_rows + c, target * cap + c))

    def copy(position, block, row, index):
        return pltpu.make_async_copy(scan.at[index], state_out[block].at[row], sem.at[position])

    indices = []
    for position, (block, row, _, place) in enumerate(plan):
        index = send[0, place]
        indices.append(index)

        @pl.when(index >= 0)
        def _():
            copy(position, block, row, index).start()

    taps = inner.shape[0]
    width = group.shape[2]
    for tap in range(taps):
        table[:, tap * LANES : (tap + 1) * LANES] = inner[tap].astype(F32)
        table[:, (taps + tap) * LANES : (taps + tap) * LANES + width] = group[tap].astype(F32)
        table[:, (taps + tap) * LANES + width : (taps + tap + 1) * LANES] = jnp.zeros(
            (table.shape[0], LANES - width), F32
        )
    picked[...] = jnp.zeros_like(picked)
    rows = per_block * cap_rows
    for (block, _, row, _), index in zip(plan, indices):
        picked[pl.ds(block * rows + row, 1), :] = table[pl.ds(jnp.maximum(index, 0), 1), :]
    for block in range(count):
        window_out[block][...] = picked[block * rows : (block + 1) * rows, :].astype(BF16)
    for (position, (block, row, _, _)), index in zip(enumerate(plan), indices):

        @pl.when(index >= 0)
        def _():
            copy(position, block, row, index).wait()


def pack(replicas, cap, send_list, scan, inner, group):
    per_block = block_rows_of(replicas)
    count = replicas - 1 if per_block == 1 else 1
    cap_rows = round_up(cap, 8)
    taps, slots, _ = inner.shape
    lanes = 2 * taps * LANES
    rows = per_block * cap_rows
    state_shape = jax.ShapeDtypeStruct((per_block * cap,) + scan.shape[1:], BF16)
    window_shape = jax.ShapeDtypeStruct((rows, lanes), BF16)
    vmem = pl.BlockSpec(memory_space=pltpu.VMEM)
    smem = pl.BlockSpec(memory_space=pltpu.SMEM)
    hbm = pl.BlockSpec(memory_space=pl.ANY)
    outs = pl.pallas_call(
        functools.partial(pack_kernel, replicas, cap, cap_rows),
        out_shape=[state_shape] * count + [window_shape] * count,
        in_specs=[smem, hbm, vmem, vmem],
        out_specs=[hbm] * count + [vmem] * count,
        scratch_shapes=[
            pltpu.VMEM((slots, lanes), F32),
            pltpu.VMEM((count * rows, lanes), F32),
            pltpu.SemaphoreType.DMA((replicas * cap,)),
        ],
        compiler_params=pltpu.CompilerParams(vmem_limit_bytes=VMEM_LIMIT),
        cost_estimate=pl.CostEstimate(flops=0, bytes_accessed=2_000_000, transcendentals=0),
        name="pack_leaving",
    )(send_list, scan, inner, group)
    return outs[:count], outs[count:]


def arrival_row(replicas, cap, cap_rows, me, entry):
    source = entry // cap
    inside = entry - source * cap
    if block_rows_of(replicas) == 1:
        source = lax.rem(me - source + replicas, replicas) - 1
    return source * cap_rows + inside


def split_order(receive, slots, order):
    def step(slot, counts):
        kept, moved = counts
        stays = receive[0, slot] < 0
        order[jnp.where(stays, kept, slots // 2 + moved)] = slot
        return (kept + jnp.where(stays, 1, 0), moved + jnp.where(stays, 0, 1))

    lax.fori_loop(0, slots, step, (jnp.int32(0), jnp.int32(0)))


def project_kernel(
    replicas,
    cap,
    cap_rows,
    receive,
    live,
    decay_log,
    delta_bias,
    skip_gain,
    own,
    other,
    inner_weight,
    gate_weight,
    group_weight,
    delta_weight,
    inner_taps,
    inner_offset,
    group_taps,
    group_offset,
    inner,
    group,
    *refs,
):
    arrived = refs[:-12]
    (
        inner_next,
        group_next,
        driven,
        decay,
        skipped,
        gate,
        maps,
        table,
        landed,
        small,
        ordered,
        order,
    ) = refs[-12:]
    me = lax.axis_index("dp")
    head = lax.axis_index("head")
    taps, slots, _ = inner.shape
    half = own.shape[1]
    width = group.shape[2]
    steps = own.shape[0] // slots

    split_order(receive, slots, order)
    for tap in range(taps):
        table[:, tap * LANES : (tap + 1) * LANES] = inner[tap].astype(F32)
        table[:, (taps + tap) * LANES : (taps + tap) * LANES + width] = group[tap].astype(F32)
    rows = arrived[0].shape[0]
    for block, ref in enumerate(arrived):
        landed[block * rows : (block + 1) * rows, :] = ref[...].astype(F32)
    for position in range(slots // 2):
        slot = order[slots // 2 + position]
        row = arrival_row(replicas, cap, cap_rows, me, receive[0, slot])
        table[pl.ds(slot, 1), :] = landed[pl.ds(row, 1), :]

    mine = pl.ds(pl.multiple_of(head * half, half), half)
    theirs = pl.ds(pl.multiple_of((1 - head) * half, half), half)

    def columns(weight):
        return jnp.dot(own[...], weight[mine, :], preferred_element_type=F32) + jnp.dot(
            other[...], weight[theirs, :], preferred_element_type=F32
        )

    def rows_of(weight, count):
        def one(tokens, part):
            piece = weight[:, part]
            if count > 1:
                piece = jnp.broadcast_to(piece, (count, half))
            return lax.dot_general(
                tokens, piece, (((1,), (1,)), ((), ())), preferred_element_type=F32
            )

        return one(own[...], mine) + one(other[...], theirs)

    def rounded(value):
        return value.astype(BF16).astype(F32)

    inner_raw = rounded(columns(inner_weight))
    gate_raw = rounded(columns(gate_weight))
    group_raw = rounded(rows_of(group_weight, 1))
    delta_raw = rounded(rows_of(delta_weight, LANES))

    living = lax.broadcasted_iota(jnp.int32, (slots, LANES), 0) < live[0]
    gate[...] = silu(gate_raw)
    shifted = delta_raw + delta_bias[0]
    delta = jnp.maximum(shifted, 0.0) + jnp.log1p(jnp.exp(-jnp.abs(shifted)))
    slope = jnp.exp(jnp.full((1, LANES), decay_log[0], F32))
    decay[...] = jnp.exp(-delta * slope)

    def convolve(carried, raw, weights, offset):
        joined = carried + [raw[step * slots : (step + 1) * slots] for step in range(steps)]
        results = []
        for step in range(steps):
            summed = offset[...]
            for tap in range(taps + 1):
                summed = summed + joined[step + tap] * weights[tap : tap + 1, :]
            results.append(rounded(silu(summed)))
        return results, joined[steps:]

    inner_conv, inner_carry = convolve(
        [table[:, tap * LANES : (tap + 1) * LANES] for tap in range(taps)],
        inner_raw,
        inner_taps,
        inner_offset,
    )
    group_conv, group_carry = convolve(
        [
            table[:, (taps + tap) * LANES : (taps + tap) * LANES + width]
            for tap in range(taps)
        ],
        group_raw,
        group_taps,
        group_offset,
    )
    for tap in range(taps):
        inner_next[tap] = jnp.where(living, inner_carry[tap], 0.0).astype(BF16)
        group_next[tap] = jnp.where(living[:, :width], group_carry[tap], 0.0).astype(BF16)
    for step in range(steps):
        part = slice(step * slots, (step + 1) * slots)
        driven[part, :] = delta[part] * inner_conv[step]
        skipped[part, :] = inner_conv[step] * skip_gain[0]
        small[part, :width] = group_conv[step]
        small[part, width:] = jnp.zeros((slots, LANES - width), F32)
    stride = LANES // steps
    ordered[...] = jnp.zeros_like(ordered)
    for position in range(slots):
        slot = order[position]
        for step in range(steps):
            ordered[pl.ds(step * stride + position, 1), :] = small[
                pl.ds(step * slots + slot, 1), :
            ]
    maps[...] = ordered[...].T[:width].astype(BF16)


def project(replicas, cap, scalars, operands, arrived):
    cap_rows = round_up(cap, 8)
    own, inner, group = operands[0], operands[-2], operands[-1]
    taps, slots, _ = inner.shape
    width = group.shape[2]
    rows = own.shape[0]
    lanes = 2 * taps * LANES
    vmem = pl.BlockSpec(memory_space=pltpu.VMEM)
    smem = pl.BlockSpec(memory_space=pltpu.SMEM)
    full = jax.ShapeDtypeStruct((rows, LANES), F32)
    return pl.pallas_call(
        functools.partial(project_kernel, replicas, cap, cap_rows),
        out_shape=[
            jax.ShapeDtypeStruct(inner.shape, BF16),
            jax.ShapeDtypeStruct(group.shape, BF16),
            full,
            full,
            full,
            full,
            jax.ShapeDtypeStruct((width, LANES), BF16),
        ],
        in_specs=[smem] * len(scalars) + [vmem] * (len(operands) + len(arrived)),
        out_specs=[vmem] * 7,
        scratch_shapes=[
            pltpu.VMEM((slots, lanes), F32),
            pltpu.VMEM((sum(block.shape[0] for block in arrived), lanes), F32),
            pltpu.VMEM((rows, LANES), F32),
            pltpu.VMEM((LANES, LANES), F32),
            pltpu.SMEM((slots,), jnp.int32),
        ],
        compiler_params=pltpu.CompilerParams(vmem_limit_bytes=VMEM_LIMIT),
        cost_estimate=pl.CostEstimate(
            flops=300_000_000, bytes_accessed=5_000_000, transcendentals=100_000
        ),
        name="project_convolve",
    )(*scalars, *operands, *arrived)


def advance_slot(state, driven, decay, sums, maps, position, slot, slots, steps):
    input_map, output_map = maps
    stride = LANES // steps
    hidden = state.astype(F32)
    for step in range(steps):
        lane = step * stride + position
        row = pl.ds(step * slots + slot, 1)
        hidden = decay[row, :] * hidden + driven[row, :] * input_map[:, lane : lane + 1]
        sums[row, :] = jnp.sum(hidden * output_map[:, lane : lane + 1], axis=0, keepdims=True)
        result = hidden.astype(BF16)
        hidden = result.astype(F32)
    return result


def pair_maps(own_maps, other_maps):
    first = lax.axis_index("head") == 0
    mine, theirs = own_maps[...].astype(F32), other_maps[...].astype(F32)
    return jnp.where(first, mine, theirs), jnp.where(first, theirs, mine)


def stay_kernel(
    steps, receive, live, driven, decay, own_maps, other_maps, scan, sums, scan_next, done, order, sem
):
    slots = scan.shape[0]
    split_order(receive, slots, order)
    maps = pair_maps(own_maps, other_maps)
    copies = []
    for position in range(slots // 2):
        slot = order[position]
        result = advance_slot(
            scan[slot], driven, decay, sums, maps, position, slot, slots, steps
        )
        done[position] = jnp.where(slot < live[0], result, jnp.zeros_like(result))
        copies.append(
            pltpu.make_async_copy(done.at[position], scan_next.at[slot], sem.at[position])
        )
        copies[-1].start()
    for copy in copies:
        copy.wait()


def arrive_kernel(
    replicas,
    cap,
    steps,
    receive,
    live,
    driven,
    decay,
    skipped,
    gate,
    own_maps,
    other_maps,
    sums_in,
    scan_in,
    *refs,
):
    del scan_in
    arrived = refs[:-7]
    gated, scan_next, sums, held, done, order, sem = refs[-7:]
    slots = scan_next.shape[0]
    rows = arrived[0].shape[0]
    loads = []
    for block, ref in enumerate(arrived):
        loads.append(
            pltpu.make_async_copy(
                ref, held.at[pl.ds(block * rows, rows)], sem.at[slots // 2 + block]
            )
        )
        loads[-1].start()
    me = lax.axis_index("dp")
    split_order(receive, slots, order)
    maps = pair_maps(own_maps, other_maps)
    sums[...] = sums_in[...]
    for load in loads:
        load.wait()
    copies = []
    for position in range(slots // 2):
        slot = order[slots // 2 + position]
        row = arrival_row(replicas, cap, cap, me, receive[0, slot])
        result = advance_slot(
            held[row], driven, decay, sums, maps, slots // 2 + position, slot, slots, steps
        )
        done[position] = jnp.where(slot < live[0], result, jnp.zeros_like(result))
        copies.append(
            pltpu.make_async_copy(done.at[position], scan_next.at[slot], sem.at[position])
        )
        copies[-1].start()
    living = lax.broadcasted_iota(jnp.int32, (slots, LANES), 0) < live[0]
    for step in range(steps):
        part = slice(step * slots, (step + 1) * slots)
        value = (sums[part, :] + skipped[part, :]) * gate[part, :]
        gated[step] = jnp.where(living, value, 0.0).astype(BF16)
    for copy in copies:
        copy.wait()


def stay(steps, receive, live, driven, decay, own_maps, other_maps, scan):
    slots = scan.shape[0]
    vmem = pl.BlockSpec(memory_space=pltpu.VMEM)
    smem = pl.BlockSpec(memory_space=pltpu.SMEM)
    hbm = pl.BlockSpec(memory_space=pl.ANY)
    return pl.pallas_call(
        functools.partial(stay_kernel, steps),
        out_shape=[
            jax.ShapeDtypeStruct(driven.shape, F32),
            jax.ShapeDtypeStruct(scan.shape, BF16),
        ],
        in_specs=[smem] * 2 + [vmem] * 5,
        out_specs=[vmem, hbm],
        scratch_shapes=[
            pltpu.VMEM((slots // 2,) + scan.shape[1:], BF16),
            pltpu.SMEM((slots,), jnp.int32),
            pltpu.SemaphoreType.DMA((slots // 2,)),
        ],
        compiler_params=pltpu.CompilerParams(vmem_limit_bytes=VMEM_LIMIT),
        cost_estimate=pl.CostEstimate(
            flops=10_000_000, bytes_accessed=2_000_000, transcendentals=0
        ),
        name="advance_staying",
    )(receive, live, driven, decay, own_maps, other_maps, scan)


def arrive(replicas, cap, steps, receive, live, operands, sums, scan_next, arrived):
    slots = scan_next.shape[0]
    vmem = pl.BlockSpec(memory_space=pltpu.VMEM)
    smem = pl.BlockSpec(memory_space=pltpu.SMEM)
    hbm = pl.BlockSpec(memory_space=pl.ANY)
    held = sum(block.shape[0] for block in arrived)
    return pl.pallas_call(
        functools.partial(arrive_kernel, replicas, cap, steps),
        out_shape=[
            jax.ShapeDtypeStruct((steps, slots, LANES), BF16),
            jax.ShapeDtypeStruct(scan_next.shape, BF16),
        ],
        in_specs=[smem] * 2 + [vmem] * (len(operands) + 1) + [hbm] * (1 + len(arrived)),
        out_specs=[vmem, hbm],
        scratch_shapes=[
            pltpu.VMEM(sums.shape, F32),
            pltpu.VMEM((held,) + scan_next.shape[1:], BF16),
            pltpu.VMEM((slots // 2,) + scan_next.shape[1:], BF16),
            pltpu.SMEM((slots,), jnp.int32),
            pltpu.SemaphoreType.DMA((slots // 2 + len(arrived),)),
        ],
        input_output_aliases={3 + len(operands): 1},
        compiler_params=pltpu.CompilerParams(vmem_limit_bytes=VMEM_LIMIT),
        cost_estimate=pl.CostEstimate(
            flops=10_000_000, bytes_accessed=2_000_000, transcendentals=0
        ),
        name="advance_arrived",
    )(receive, live, *operands, sums, scan_next, *arrived)


def swap_heads(value):
    return lax.ppermute(value, "head", [(0, 1), (1, 0)])


def move(replicas, blocks):
    if block_rows_of(replicas) > 1:
        return [lax.all_to_all(block, "dp", 0, 0, tiled=True) for block in blocks]
    return [
        lax.ppermute(
            block, "dp", [(source, (source + shift) % replicas) for source in range(replicas)]
        )
        for shift, block in enumerate(blocks, 1)
    ]


def per_device(
    replicas,
    tokens,
    inner_weight,
    gate_weight,
    group_weight,
    delta_weight,
    inner_taps,
    inner_offset,
    group_taps,
    group_offset,
    decay_log,
    delta_bias,
    skip_gain,
    inner_window,
    group_window,
    scan_state,
    send_list,
    receive_list,
    live_count,
):
    steps, slots, half = tokens.shape
    cap = send_list.shape[1] // replicas
    scan = jnp.transpose(scan_state, (0, 2, 1))
    inner = jnp.transpose(inner_window, (1, 0, 2))
    group = jnp.transpose(group_window, (1, 0, 2))
    own = tokens.reshape(steps * slots, half)

    states, windows = pack(replicas, cap, send_list, scan, inner, group)
    windows = move(replicas, windows)
    states = move(replicas, states)
    other = swap_heads(own)
    scalars = (receive_list, live_count, decay_log, delta_bias, skip_gain)
    operands = (
        own,
        other,
        inner_weight,
        gate_weight,
        group_weight.T,
        delta_weight.T,
        inner_taps,
        inner_offset[None],
        group_taps,
        group_offset[None],
        inner,
        group,
    )
    inner_next, group_next, driven, decay, skipped, gate, maps = project(
        replicas, cap, scalars, operands, windows
    )
    other_maps = swap_heads(maps)
    sums, scan_next = stay(
        steps, receive_list, live_count, driven, decay, maps, other_maps, scan
    )
    gated, scan_next = arrive(
        replicas,
        cap,
        steps,
        receive_list,
        live_count,
        (driven, decay, skipped, gate, maps, other_maps),
        sums,
        scan_next,
        states,
    )
    return (
        gated,
        jnp.transpose(inner_next, (1, 0, 2)),
        jnp.transpose(group_next, (1, 0, 2)),
        jnp.transpose(scan_next, (0, 2, 1)),
    )


def solution(mesh):
    in_specs = (
        P(None, ("grp", "dp"), "head"),
        P(None, "head"),
        P(None, "head"),
        P(None, "head"),
        P(None, "head"),
        P(None, "head"),
        P("head"),
        P(None, "head"),
        P("head"),
        P("head"),
        P("head"),
        P("head"),
        P(("grp", "dp"), None, "head"),
        P(("grp", "dp"), None, "head"),
        P(("grp", "dp"), "head", None),
        P(("grp", "dp"), None),
        P(("grp", "dp"), None),
        P(("grp", "dp")),
    )
    out_specs = (
        P(None, ("grp", "dp"), "head"),
        P(("grp", "dp"), None, "head"),
        P(("grp", "dp"), None, "head"),
        P(("grp", "dp"), "head", None),
    )
    return jax.shard_map(
        functools.partial(per_device, mesh.shape["dp"]),
        mesh=mesh,
        in_specs=in_specs,
        out_specs=out_specs,
        check_vma=False,
    )
```

time: 73.2 us -> 64.8 us (0.89)
  the two profiles are of different devices: /device:TPU:0 before, /device:TPU:11 now
where the time goes in v1:
time: 64.8 us; the launch traced here: 64.4 us
  starting transfers between devices  24.6 us (38%)
  waiting for transfers between devices  17 us (26%)
  Pallas kernels  13 us (20%)
  local copies, waits for them, and re-layouts  6.53 us (10%)
  between operations  3.33 us (5%)
    ppermute x14, starting transfers between devices, move(): lax.ppermute(block, 'dp', [(source, (source + shift) % replicas) for sour...  19.5 us
    ppermute x14, waiting for transfers between devices, move(): lax.ppermute(block, 'dp', [(source, (source + shift) % replicas) for sour...  17 us
    unnamed x30, local copies, waits for them, and re-layouts  6.53 us
    ppermute x2, starting transfers between devices, swap_heads(): return lax.ppermute(value, 'head', [(0, 1), (1, 0)])  5.13 us
    pallas_call x1, Pallas kernels, arrive(): pl.pallas_call(functools.partial(arrive_kernel, replicas, cap, steps), ou...  4.49 us
    pallas_call x1, Pallas kernels, project(): pl.pallas_call(functools.partial(project_kernel, replicas, cap, cap_rows)...  3.29 us
    pallas_call x1, Pallas kernels, stay(): pl.pallas_call(functools.partial(stay_kernel, steps), out_shape=[jax.Shap...  2.77 us
    pallas_call x1, Pallas kernels, pack(): pl.pallas_call(functools.partial(pack_kernel, replicas, cap, cap_rows), o...  2.4 us
  transfers between devices with their start and end apart: 16, of which 7 were waited for; matrix products, arithmetic and copies ran while one was open for 0% of the time, Pallas kernels for 13%

profile of v1, /device:TPU:11, one launch (start us, length us, event | category | flops | bytes accessed | tf_op | source)
XLA Modules:
  0.0 64.4 jit_solution(10703726961444126375)
XLA Ops:
  0.6 0.7 %collective-permute-start = (bf16[112,2048]{1,0:T(8,128)(2,1)}, bf16[112,2048]{1,0:T(8,128)(2,1)S(1)}, u32[]{:S(2)}, u32[]{:S(2)}) collective-permute-start(bf16[112,2048]{1,0:T(8,128)(2,1)} %bitcast.14), channel_id=1, source_target_pairs={{0,1},{1,0},{2,3},{3,2},{4,5},{5,4},{6,7},{7,6},{8,9},{9,8},{10,11... | collective-permute-start | bytes 1376264 | tf_op jit(solution)/shard_map/ppermute | solution.py:450
  1.4 0.7 %copy-done.12 = s32[1,56]{1,0:T(1,128)S(1)} copy-done((s32[1,56]{1,0:T(1,128)S(1)}, s32[1,56]{1,0:T(1,128)}, u32[]{:S(2)}) %copy-start.12) | copy-done | bytes 248
  2.0 1.2 %copy-done = bf16[56,128,64]{1,2,0:T(8,128)(2,1)S(1)} copy-done((bf16[56,128,64]{1,2,0:T(8,128)(2,1)S(1)}, bf16[56,128,64]{1,2,0:T(8,128)(2,1)}, u32[]{:S(2)}) %copy-start) | copy-done | bytes 917528
  3.2 0.8 %copy-done.6 = bf16[56,3,128]{2,0,1:T(8,128)(2,1)S(1)} copy-done((bf16[56,3,128]{2,0,1:T(8,128)(2,1)S(1)}, bf16[56,3,128]{2,0,1:T(8,128)(2,1)}, u32[]{:S(2)}) %copy-start.6) | copy-done | bytes 43032
  4.0 0.8 %copy-done.7 = bf16[56,3,64]{2,0,1:T(8,128)(2,1)S(1)} copy-done((bf16[56,3,64]{2,0,1:T(8,128)(2,1)S(1)}, bf16[56,3,64]{2,0,1:T(8,128)(2,1)}, u32[]{:S(2)}) %copy-start.7) | copy-done | bytes 21528
  4.8 2.4 %pack_leaving.1 = (bf16[7,64,128]{2,1,0:T(8,128)(2,1)S(1)}, bf16[7,64,128]{2,1,0:T(8,128)(2,1)S(1)}, bf16[7,64,128]{2,1,0:T(8,128)(2,1)S(1)}, bf16[7,64,128]{2,1...) custom-call(s32[1,56]{1,0:T(1,128)S(1)} %copy-done.12, ...), custom_call_target="tpu_custom_call" | custom-call | bytes 2000000 | tf_op jit(solution)/shard_map/pack_leaving/pallas_call | solution.py:87
  7.2 0.0 copy-start.8
  7.2 1.3 %collective-permute-start.9 = (bf16[7,64,128]{2,1,0:T(8,128)(2,1)S(1)}, bf16[7,64,128]{2,1,0:T(8,128)(2,1)S(1)}, u32[]{:S(2)}, u32[]{:S(2)}) collective-permute-start(bf16[7,64,128]{2,1,0:T(8,128)(2,1)S(1)} %get-tuple-element.43), channel_id=1, source_target_pairs={{0,2},{2,4},{4,6},{6,8},{8,10},{10,12},{12,14},{14,0},{1,3},{3,5},... | collective-permute-start | bytes 344072 | tf_op jit(solution)/shard_map/ppermute | solution.py:457
  8.5 1.3 %collective-permute-start.10 = (bf16[7,64,128]{2,1,0:T(8,128)(2,1)S(1)}, bf16[7,64,128]{2,1,0:T(8,128)(2,1)S(1)}, u32[]{:S(2)}, u32[]{:S(2)}) collective-permute-start(bf16[7,64,128]{2,1,0:T(8,128)(2,1)S(1)} %get-tuple-element.44), channel_id=1, source_target_pairs={{0,4},{2,6},{4,8},{6,10},{8,12},{10,14},{12,0},{14,2},{1,5},{3,7},... | collective-permute-start | bytes 344072 | tf_op jit(solution)/shard_map/ppermute | solution.py:457
  9.8 1.2 %collective-permute-start.1 = (bf16[8,768]{1,0:T(8,128)(2,1)S(1)}, bf16[8,768]{1,0:T(8,128)(2,1)S(1)}, u32[]{:S(2)}, u32[]{:S(2)}) collective-permute-start(bf16[8,768]{1,0:T(8,128)(2,1)S(1)} %get-tuple-element.29), channel_id=1, source_target_pairs={{0,2},{2,4},{4,6},{6,8},{8,10},{10,12},{12,14},{14,0},{1,3},{3,5},... | collective-permute-start | bytes 36872 | tf_op jit(solution)/shard_map/ppermute | solution.py:457
  11.0 0.0 collective-permute-start.2
  11.0 2.8 %collective-permute-done.1.refs_0_ = bf16[8,768]{1,0:T(8,128)(2,1)S(1)} collective-permute-done((bf16[8,768]{1,0:T(8,128)(2,1)S(1)}, bf16[8,768]{1,0:T(8,128)(2,1)S(1)}, u32[]{:S(2)}, u32[]{:S(2)}) %collective-permute-start.1) | collective-permute-done | bytes 12320 | tf_op jit(solution)/shard_map/ppermute | solution.py:457
  13.8 3.8 %collective-permute-start.3 = (bf16[8,768]{1,0:T(8,128)(2,1)S(1)}, bf16[8,768]{1,0:T(8,128)(2,1)S(1)}, u32[]{:S(2)}, u32[]{:S(2)}) collective-permute-start(bf16[8,768]{1,0:T(8,128)(2,1)S(1)} %get-tuple-element.31), channel_id=1, source_target_pairs={{0,6},{2,8},{4,10},{6,12},{8,14},{10,0},{12,2},{14,4},{1,7},{3,9},... | collective-permute-start | bytes 36872 | tf_op jit(solution)/shard_map/ppermute | solution.py:457
  17.6 0.0 collective-permute-done.2.refs_1_
  17.6 0.1 collective-permute-start.4
  17.7 1.0 %collective-permute-done.3.refs_2_ = bf16[8,768]{1,0:T(8,128)(2,1)S(1)} collective-permute-done((bf16[8,768]{1,0:T(8,128)(2,1)S(1)}, bf16[8,768]{1,0:T(8,128)(2,1)S(1)}, u32[]{:S(2)}, u32[]{:S(2)}) %collective-permute-start.3) | collective-permute-done | bytes 12320 | tf_op jit(solution)/shard_map/ppermute | solution.py:457
  18.7 3.3 %collective-permute-start.5 = (bf16[8,768]{1,0:T(8,128)(2,1)S(1)}, bf16[8,768]{1,0:T(8,128)(2,1)S(1)}, u32[]{:S(2)}, u32[]{:S(2)}) collective-permute-start(bf16[8,768]{1,0:T(8,128)(2,1)S(1)} %get-tuple-element.33), channel_id=1, source_target_pairs={{0,10},{2,12},{4,14},{6,0},{8,2},{10,4},{12,6},{14,8},{1,11},{3,13... | collective-permute-start | bytes 36872 | tf_op jit(solution)/shard_map/ppermute | solution.py:457
  21.9 0.0 collective-permute-done.4.refs_3_
  21.9 1.2 %collective-permute-start.6 = (bf16[8,768]{1,0:T(8,128)(2,1)S(1)}, bf16[8,768]{1,0:T(8,128)(2,1)S(1)}, u32[]{:S(2)}, u32[]{:S(2)}) collective-permute-start(bf16[8,768]{1,0:T(8,128)(2,1)S(1)} %get-tuple-element.34), channel_id=1, source_target_pairs={{0,12},{2,14},{4,0},{6,2},{8,4},{10,6},{12,8},{14,10},{1,13},{3,15... | collective-permute-start | bytes 36872 | tf_op jit(solution)/shard_map/ppermute | solution.py:457
  23.2 0.0 collective-permute-done.5.refs_4_
  23.2 0.2 collective-permute-start.7
  26.0 0.0 collective-permute-done.6.refs_5_
  26.0 0.6 collective-permute-done.7.refs_6_
  26.6 0.0 collective-permute-done.other
  26.6 0.0 copy-start.13
  26.7 0.0 copy-start.14
  26.7 0.6 copy-done.11
  27.3 0.0 copy-done.10
  27.3 0.0 copy-done.14
  27.4 1.2 %copy-done.2 = bf16[4096,128]{1,0:T(8,128)(2,1)S(1)} copy-done((bf16[4096,128]{1,0:T(8,128)(2,1)S(1)}, bf16[4096,128]{1,0:T(8,128)(2,1)}, u32[]{:S(2)}) %copy-start.2) | copy-done | bytes 1048600
  28.6 1.2 %copy-done.3 = bf16[4096,128]{1,0:T(8,128)(2,1)S(1)} copy-done((bf16[4096,128]{1,0:T(8,128)(2,1)S(1)}, bf16[4096,128]{1,0:T(8,128)(2,1)}, u32[]{:S(2)}) %copy-start.3) | copy-done | bytes 1048600
  29.8 3.3 %project_convolve.1 = (bf16[3,56,128]{2,1,0:T(8,128)(2,1)}, bf16[3,56,64]{2,1,0:T(8,128)(2,1)}, f32[112,128]{1,0:T(8,128)S(1)}, f32[112,128]{1,0:T(8,128)S(1)}, ...) custom-call(s32[1,56]{1,0:T(1,128)S(1)} %copy-done.9, s32[1]{0:T(128)S(6)} %copy.27.live, ...), custom_call_target="tpu_custom_call" | custom-call | flops 300000000 | bytes 5000000 | tf_op jit(solution)/shard_map/project_convolve/pallas_call | solution.py:268
  33.1 4.4 %collective-permute-start.8 = (bf16[64,128]{1,0:T(8,128)(2,1)S(1)}, bf16[64,128]{1,0:T(8,128)(2,1)S(1)}, u32[]{:S(2)}, u32[]{:S(2)}) collective-permute-start(bf16[64,128]{1,0:T(8,128)(2,1)S(1)} %get-tuple-element.40.own_maps), channel_id=1, source_target_pairs={{0,1},{1,0},{2,3},{3,2},{4,5},{5,4},{6,7},{7,6},{8,9},{9,8},{10,11... | collective-permute-start | bytes 49160 | tf_op jit(solution)/shard_map/ppermute | solution.py:450
  37.5 3.4 %collective-permute-start.11 = (bf16[7,64,128]{2,1,0:T(8,128)(2,1)S(1)}, bf16[7,64,128]{2,1,0:T(8,128)(2,1)S(1)}, u32[]{:S(2)}, u32[]{:S(2)}) collective-permute-start(bf16[7,64,128]{2,1,0:T(8,128)(2,1)S(1)} %get-tuple-element.45), channel_id=1, source_target_pairs={{0,6},{2,8},{4,10},{6,12},{8,14},{10,0},{12,2},{14,4},{1,7},{3,9},... | collective-permute-start | bytes 344072 | tf_op jit(solution)/shard_map/ppermute | solution.py:457
  40.9 0.0 collective-permute-start.12
  40.9 0.0 collective-permute-done.9.refs_0_
  40.9 1.9 %collective-permute-start.13 = (bf16[7,64,128]{2,1,0:T(8,128)(2,1)S(1)}, bf16[7,64,128]{2,1,0:T(8,128)(2,1)S(1)}, u32[]{:S(2)}, u32[]{:S(2)}) collective-permute-start(bf16[7,64,128]{2,1,0:T(8,128)(2,1)S(1)} %get-tuple-element.47), channel_id=1, source_target_pairs={{0,10},{2,12},{4,14},{6,0},{8,2},{10,4},{12,6},{14,8},{1,11},{3,13... | collective-permute-start | bytes 344072 | tf_op jit(solution)/shard_map/ppermute | solution.py:457
  42.8 0.0 collective-permute-done.10.refs_1_
  42.8 1.1 %collective-permute-start.14 = (bf16[7,64,128]{2,1,0:T(8,128)(2,1)S(1)}, bf16[7,64,128]{2,1,0:T(8,128)(2,1)S(1)}, u32[]{:S(2)}, u32[]{:S(2)}) collective-permute-start(bf16[7,64,128]{2,1,0:T(8,128)(2,1)S(1)} %get-tuple-element.48), channel_id=1, source_target_pairs={{0,12},{2,14},{4,0},{6,2},{8,4},{10,6},{12,8},{14,10},{1,13},{3,15... | collective-permute-start | bytes 344072 | tf_op jit(solution)/shard_map/ppermute | solution.py:457
  43.9 0.0 collective-permute-done.8.other_maps
  43.9 0.6 collective-permute-start.15
  44.5 2.8 %advance_staying.1 = (f32[112,128]{1,0:T(8,128)S(1)}, bf16[56,64,128]{2,1,0:T(8,128)(2,1)}) custom-call(s32[1,56]{1,0:T(1,128)S(1)} %copy-done.9, s32[1]{0:T(128)S(6)} %copy.27.live, f32[112,128]{1,0:T(8,128)S(1)} %get-tuple-element.36.driven, f32[112,128]{1,0:T(8,128)S(1)} %get-tuple-element.37.decay, bf16[64,128]{1,0:T(8,128)(2,1)S(1)} %get-tuple-element.40.own_maps, ...), custom_call_target="tpu_custom_call" | custom-call | flops 10000000 | bytes 2000000 | tf_op jit(solution)/shard_map/advance_staying/pallas_call | solution.py:398
  47.3 4.5 %collective-permute-done.11.refs_2_ = bf16[7,64,128]{2,1,0:T(8,128)(2,1)S(1)} collective-permute-done((bf16[7,64,128]{2,1,0:T(8,128)(2,1)S(1)}, bf16[7,64,128]{2,1,0:T(8,128)(2,1)S(1)}, u32[]{:S(2)}, u32[]{:S(2)}) %collective-permute-start.11) | collective-permute-done | bytes 114720 | tf_op jit(solution)/shard_map/ppermute | solution.py:457
  51.8 2.5 %collective-permute-done.12.refs_3_ = bf16[7,64,128]{2,1,0:T(8,128)(2,1)S(1)} collective-permute-done((bf16[7,64,128]{2,1,0:T(8,128)(2,1)S(1)}, bf16[7,64,128]{2,1,0:T(8,128)(2,1)S(1)}, u32[]{:S(2)}, u32[]{:S(2)}) %collective-permute-start.12) | collective-permute-done | bytes 114720 | tf_op jit(solution)/shard_map/ppermute | solution.py:457
  54.3 0.0 collective-permute-done.13.refs_4_
  54.3 1.5 %collective-permute-done.14.refs_5_ = bf16[7,64,128]{2,1,0:T(8,128)(2,1)S(1)} collective-permute-done((bf16[7,64,128]{2,1,0:T(8,128)(2,1)S(1)}, bf16[7,64,128]{2,1,0:T(8,128)(2,1)S(1)}, u32[]{:S(2)}, u32[]{:S(2)}) %collective-permute-start.14) | collective-permute-done | bytes 114720 | tf_op jit(solution)/shard_map/ppermute | solution.py:457
  55.8 4.2 %collective-permute-done.15.refs_6_ = bf16[7,64,128]{2,1,0:T(8,128)(2,1)S(1)} collective-permute-done((bf16[7,64,128]{2,1,0:T(8,128)(2,1)S(1)}, bf16[7,64,128]{2,1,0:T(8,128)(2,1)S(1)}, u32[]{:S(2)}, u32[]{:S(2)}) %collective-permute-start.15) | collective-permute-done | bytes 114720 | tf_op jit(solution)/shard_map/ppermute | solution.py:457
  59.9 4.5 %advance_arrived.1 = (bf16[2,56,128]{2,1,0:T(8,128)(2,1)}, bf16[56,64,128]{2,1,0:T(8,128)(2,1)}) custom-call(s32[1,56]{1,0:T(1,128)S(1)} %copy-done.9, s32[1]{0:T(128)S(6)} %copy.27.live, f32[112,128]{1,0:T(8,128)S(1)} %get-tuple-element.36.driven, f32[112,128]{1,0:T(8,128)S(1)} %get-tuple-element.37.decay, ...), custom_call_target="tpu_custom_call", output_to_operand_aliasing={{1}: (9, {})} | custom-call | flops 10000000 | bytes 2000000 | tf_op jit(solution)/shard_map/advance_arrived/pallas_call | solution.py:425
  (18 shorter events, 0.0 us)
Async XLA Ops:
  0.6 26.0 %collective-permute-start = (bf16[112,2048]{1,0:T(8,128)(2,1)}, bf16[112,2048]{1,0:T(8,128)(2,1)S(1)}, u32[]{:S(2)}, u32[]{:S(2)}) collective-permute-start(bf16[112,2048]{1,0:T(8,128)(2,1)} %bitcast.14), channel_id=1, source_target_pairs={{0,1},{1,0},{2,3},{3,2},{4,5},{5,4},{6,7},{7,6},{8,9},{9,8},{10,11... | collective-permute-start | bytes 1376264 | tf_op jit(solution)/shard_map/ppermute | solution.py:450
  1.4 0.7 %copy-start.12 = (s32[1,56]{1,0:T(1,128)S(1)}, s32[1,56]{1,0:T(1,128)}, u32[]{:S(2)}) copy-start(s32[1,56]{1,0:T(1,128)} %send.1) | copy-start | bytes 676
  2.0 1.2 %copy-start = (bf16[56,128,64]{1,2,0:T(8,128)(2,1)S(1)}, bf16[56,128,64]{1,2,0:T(8,128)(2,1)}, u32[]{:S(2)}) copy-start(bf16[56,128,64]{1,2,0:T(8,128)(2,1)} %param.32) | copy-start | bytes 2752516
  3.2 0.8 %copy-start.6 = (bf16[56,3,128]{2,0,1:T(8,128)(2,1)S(1)}, bf16[56,3,128]{2,0,1:T(8,128)(2,1)}, u32[]{:S(2)}) copy-start(bf16[56,3,128]{2,0,1:T(8,128)(2,1)} %param.30) | copy-start | bytes 129028
  4.0 0.8 %copy-start.7 = (bf16[56,3,64]{2,0,1:T(8,128)(2,1)S(1)}, bf16[56,3,64]{2,0,1:T(8,128)(2,1)}, u32[]{:S(2)}) copy-start(bf16[56,3,64]{2,0,1:T(8,128)(2,1)} %param.31) | copy-start | bytes 64516
  4.8 21.9 %copy-start.4 = (bf16[4096,64]{0,1:T(8,128)(2,1)S(1)}, bf16[4096,64]{0,1:T(8,128)(2,1)}, u32[]{:S(2)}) copy-start(bf16[4096,64]{0,1:T(8,128)(2,1)} %param.21) | copy-start | bytes 1572868
  4.8 21.9 %copy-start.5 = (bf16[2,56,2048]{2,1,0:T(8,128)(2,1)S(1)}, bf16[2,56,2048]{2,1,0:T(8,128)(2,1)}, u32[]{:S(2)}) copy-start(bf16[2,56,2048]{2,1,0:T(8,128)(2,1)} %param.18) | copy-start | bytes 1376260
  7.2 19.5 %copy-start.8 = (bf16[4096,1]{0,1:T(2,128)(2,1)S(1)}, bf16[4096,1]{0,1:T(2,128)(2,1)}, u32[]{:S(2)}) copy-start(bf16[4096,1]{0,1:T(2,128)(2,1)} %param.22) | copy-start | bytes 24580
  7.2 33.7 %collective-permute-start.9 = (bf16[7,64,128]{2,1,0:T(8,128)(2,1)S(1)}, bf16[7,64,128]{2,1,0:T(8,128)(2,1)S(1)}, u32[]{:S(2)}, u32[]{:S(2)}) collective-permute-start(bf16[7,64,128]{2,1,0:T(8,128)(2,1)S(1)} %get-tuple-element.43), channel_id=1, source_target_pairs={{0,2},{2,4},{4,6},{6,8},{8,10},{10,12},{12,14},{14,0},{1,3},{3,5},... | collective-permute-start | bytes 344072 | tf_op jit(solution)/shard_map/ppermute | solution.py:457
  8.5 34.3 %collective-permute-start.10 = (bf16[7,64,128]{2,1,0:T(8,128)(2,1)S(1)}, bf16[7,64,128]{2,1,0:T(8,128)(2,1)S(1)}, u32[]{:S(2)}, u32[]{:S(2)}) collective-permute-start(bf16[7,64,128]{2,1,0:T(8,128)(2,1)S(1)} %get-tuple-element.44), channel_id=1, source_target_pairs={{0,4},{2,6},{4,8},{6,10},{8,12},{10,14},{12,0},{14,2},{1,5},{3,7},... | collective-permute-start | bytes 344072 | tf_op jit(solution)/shard_map/ppermute | solution.py:457
  9.8 4.0 %collective-permute-start.1 = (bf16[8,768]{1,0:T(8,128)(2,1)S(1)}, bf16[8,768]{1,0:T(8,128)(2,1)S(1)}, u32[]{:S(2)}, u32[]{:S(2)}) collective-permute-start(bf16[8,768]{1,0:T(8,128)(2,1)S(1)} %get-tuple-element.29), channel_id=1, source_target_pairs={{0,2},{2,4},{4,6},{6,8},{8,10},{10,12},{12,14},{14,0},{1,3},{3,5},... | collective-permute-start | bytes 36872 | tf_op jit(solution)/shard_map/ppermute | solution.py:457
  11.0 6.6 %collective-permute-start.2 = (bf16[8,768]{1,0:T(8,128)(2,1)S(1)}, bf16[8,768]{1,0:T(8,128)(2,1)S(1)}, u32[]{:S(2)}, u32[]{:S(2)}) collective-permute-start(bf16[8,768]{1,0:T(8,128)(2,1)S(1)} %get-tuple-element.30), channel_id=1, source_target_pairs={{0,4},{2,6},{4,8},{6,10},{8,12},{10,14},{12,0},{14,2},{1,5},{3,7},... | collective-permute-start | bytes 36872 | tf_op jit(solution)/shard_map/ppermute | solution.py:457
  13.8 4.9 %collective-permute-start.3 = (bf16[8,768]{1,0:T(8,128)(2,1)S(1)}, bf16[8,768]{1,0:T(8,128)(2,1)S(1)}, u32[]{:S(2)}, u32[]{:S(2)}) collective-permute-start(bf16[8,768]{1,0:T(8,128)(2,1)S(1)} %get-tuple-element.31), channel_id=1, source_target_pairs={{0,6},{2,8},{4,10},{6,12},{8,14},{10,0},{12,2},{14,4},{1,7},{3,9},... | collective-permute-start | bytes 36872 | tf_op jit(solution)/shard_map/ppermute | solution.py:457
  17.6 4.3 %collective-permute-start.4 = (bf16[8,768]{1,0:T(8,128)(2,1)S(1)}, bf16[8,768]{1,0:T(8,128)(2,1)S(1)}, u32[]{:S(2)}, u32[]{:S(2)}) collective-permute-start(bf16[8,768]{1,0:T(8,128)(2,1)S(1)} %get-tuple-element.32), channel_id=1, source_target_pairs={{0,8},{2,10},{4,12},{6,14},{8,0},{10,2},{12,4},{14,6},{1,9},{3,11}... | collective-permute-start | bytes 36872 | tf_op jit(solution)/shard_map/ppermute | solution.py:457
  18.7 4.5 %collective-permute-start.5 = (bf16[8,768]{1,0:T(8,128)(2,1)S(1)}, bf16[8,768]{1,0:T(8,128)(2,1)S(1)}, u32[]{:S(2)}, u32[]{:S(2)}) collective-permute-start(bf16[8,768]{1,0:T(8,128)(2,1)S(1)} %get-tuple-element.33), channel_id=1, source_target_pairs={{0,10},{2,12},{4,14},{6,0},{8,2},{10,4},{12,6},{14,8},{1,11},{3,13... | collective-permute-start | bytes 36872 | tf_op jit(solution)/shard_map/ppermute | solution.py:457
  21.9 4.1 %collective-permute-start.6 = (bf16[8,768]{1,0:T(8,128)(2,1)S(1)}, bf16[8,768]{1,0:T(8,128)(2,1)S(1)}, u32[]{:S(2)}, u32[]{:S(2)}) collective-permute-start(bf16[8,768]{1,0:T(8,128)(2,1)S(1)} %get-tuple-element.34), channel_id=1, source_target_pairs={{0,12},{2,14},{4,0},{6,2},{8,4},{10,6},{12,8},{14,10},{1,13},{3,15... | collective-permute-start | bytes 36872 | tf_op jit(solution)/shard_map/ppermute | solution.py:457
  23.2 3.4 %collective-permute-start.7 = (bf16[8,768]{1,0:T(8,128)(2,1)S(1)}, bf16[8,768]{1,0:T(8,128)(2,1)S(1)}, u32[]{:S(2)}, u32[]{:S(2)}) collective-permute-start(bf16[8,768]{1,0:T(8,128)(2,1)S(1)} %get-tuple-element.35), channel_id=1, source_target_pairs={{0,14},{2,0},{4,2},{6,4},{8,6},{10,8},{12,10},{14,12},{1,15},{3,1}... | collective-permute-start | bytes 36872 | tf_op jit(solution)/shard_map/ppermute | solution.py:457
  26.6 0.7 %copy-start.11 = (f32[4,64]{1,0:T(4,128)S(1)}, f32[4,64]{1,0:T(4,128)}, u32[]{:S(2)}) copy-start(f32[4,64]{1,0:T(4,128)} %group_taps.1) | copy-start | bytes 3076
  26.6 0.7 %copy-start.10 = (f32[4,128]{1,0:T(4,128)S(1)}, f32[4,128]{1,0:T(4,128)}, u32[]{:S(2)}) copy-start(f32[4,128]{1,0:T(4,128)} %inner_taps.1) | copy-start | bytes 6148
  26.6 0.7 %copy-start.9 = (s32[1,56]{1,0:T(1,128)S(1)}, s32[1,56]{1,0:T(1,128)}, u32[]{:S(2)}) copy-start(s32[1,56]{1,0:T(1,128)} %receive.5) | copy-start | bytes 676
  26.6 0.7 %copy-start.13 = (f32[128]{0:T(128)S(1)}, f32[128]{0:T(128)}, u32[]{:S(2)}) copy-start(f32[128]{0:T(128)} %param.24) | copy-start | bytes 1540
  26.7 0.7 %copy-start.14 = (f32[64]{0:T(128)S(1)}, f32[64]{0:T(128)}, u32[]{:S(2)}) copy-start(f32[64]{0:T(128)} %param.26) | copy-start | bytes 772
  27.3 1.2 %copy-start.2 = (bf16[4096,128]{1,0:T(8,128)(2,1)S(1)}, bf16[4096,128]{1,0:T(8,128)(2,1)}, u32[]{:S(2)}) copy-start(bf16[4096,128]{1,0:T(8,128)(2,1)} %inner_weight.1) | copy-start | bytes 3145732
  28.6 1.2 %copy-start.3 = (bf16[4096,128]{1,0:T(8,128)(2,1)S(1)}, bf16[4096,128]{1,0:T(8,128)(2,1)}, u32[]{:S(2)}) copy-start(bf16[4096,128]{1,0:T(8,128)(2,1)} %gate_weight.1) | copy-start | bytes 3145732
  29.8 14.7 %copy-start.1 = (bf16[56,128,64]{1,2,0:T(8,128)(2,1)S(1)}, bf16[56,128,64]{1,2,0:T(8,128)(2,1)}, u32[]{:S(2)}) copy-start(bf16[56,128,64]{1,2,0:T(8,128)(2,1)} %param.32) | copy-start | bytes 2752516
  33.1 10.8 %collective-permute-start.8 = (bf16[64,128]{1,0:T(8,128)(2,1)S(1)}, bf16[64,128]{1,0:T(8,128)(2,1)S(1)}, u32[]{:S(2)}, u32[]{:S(2)}) collective-permute-start(bf16[64,128]{1,0:T(8,128)(2,1)S(1)} %get-tuple-element.40.own_maps), channel_id=1, source_target_pairs={{0,1},{1,0},{2,3},{3,2},{4,5},{5,4},{6,7},{7,6},{8,9},{9,8},{10,11... | collective-permute-start | bytes 49160 | tf_op jit(solution)/shard_map/ppermute | solution.py:450
  37.5 14.3 %collective-permute-start.11 = (bf16[7,64,128]{2,1,0:T(8,128)(2,1)S(1)}, bf16[7,64,128]{2,1,0:T(8,128)(2,1)S(1)}, u32[]{:S(2)}, u32[]{:S(2)}) collective-permute-start(bf16[7,64,128]{2,1,0:T(8,128)(2,1)S(1)} %get-tuple-element.45), channel_id=1, source_target_pairs={{0,6},{2,8},{4,10},{6,12},{8,14},{10,0},{12,2},{14,4},{1,7},{3,9},... | collective-permute-start | bytes 344072 | tf_op jit(solution)/shard_map/ppermute | solution.py:457
  40.9 13.3 %collective-permute-start.12 = (bf16[7,64,128]{2,1,0:T(8,128)(2,1)S(1)}, bf16[7,64,128]{2,1,0:T(8,128)(2,1)S(1)}, u32[]{:S(2)}, u32[]{:S(2)}) collective-permute-start(bf16[7,64,128]{2,1,0:T(8,128)(2,1)S(1)} %get-tuple-element.46), channel_id=1, source_target_pairs={{0,8},{2,10},{4,12},{6,14},{8,0},{10,2},{12,4},{14,6},{1,9},{3,11}... | collective-permute-start | bytes 344072 | tf_op jit(solution)/shard_map/ppermute | solution.py:457
  40.9 13.3 %collective-permute-start.13 = (bf16[7,64,128]{2,1,0:T(8,128)(2,1)S(1)}, bf16[7,64,128]{2,1,0:T(8,128)(2,1)S(1)}, u32[]{:S(2)}, u32[]{:S(2)}) collective-permute-start(bf16[7,64,128]{2,1,0:T(8,128)(2,1)S(1)} %get-tuple-element.47), channel_id=1, source_target_pairs={{0,10},{2,12},{4,14},{6,0},{8,2},{10,4},{12,6},{14,8},{1,11},{3,13... | collective-permute-start | bytes 344072 | tf_op jit(solution)/shard_map/ppermute | solution.py:457
  42.8 13.0 %collective-permute-start.14 = (bf16[7,64,128]{2,1,0:T(8,128)(2,1)S(1)}, bf16[7,64,128]{2,1,0:T(8,128)(2,1)S(1)}, u32[]{:S(2)}, u32[]{:S(2)}) collective-permute-start(bf16[7,64,128]{2,1,0:T(8,128)(2,1)S(1)} %get-tuple-element.48), channel_id=1, source_target_pairs={{0,12},{2,14},{4,0},{6,2},{8,4},{10,6},{12,8},{14,10},{1,13},{3,15... | collective-permute-start | bytes 344072 | tf_op jit(solution)/shard_map/ppermute | solution.py:457
  43.9 16.0 %collective-permute-start.15 = (bf16[7,64,128]{2,1,0:T(8,128)(2,1)S(1)}, bf16[7,64,128]{2,1,0:T(8,128)(2,1)S(1)}, u32[]{:S(2)}, u32[]{:S(2)}) collective-permute-start(bf16[7,64,128]{2,1,0:T(8,128)(2,1)S(1)} %get-tuple-element.49), channel_id=1, source_target_pairs={{0,14},{2,0},{4,2},{6,4},{8,6},{10,8},{12,10},{14,12},{1,15},{3,1}... | collective-permute-start | bytes 344072 | tf_op jit(solution)/shard_map/ppermute | solution.py:457

commit v2 on v1

v2 whole, which is shorter than its diff:
```python
import functools

import jax
import jax.numpy as jnp
from jax import lax
from jax.experimental import pallas as pl
from jax.experimental.pallas import tpu as pltpu
from jax.sharding import PartitionSpec as P

F32 = jnp.float32
BF16 = jnp.bfloat16
VMEM_LIMIT = 32 * 1024 * 1024
SMALL_LIMIT = 8 * 1024 * 1024
LARGE_LIMIT = 60 * 1024 * 1024
PLAN = 128
LANES = 128


def round_up(value, step):
    return -(-value // step) * step


def silu(value):
    return value * jax.nn.sigmoid(value)


def pack_kernel(scan, send, out, table, sem, list_sem):
    load = pltpu.make_async_copy(send, table, list_sem)
    load.start()
    load.wait()

    def each(act):
        for place in range(out.shape[0]):
            index = table[0, place]

            @pl.when(index >= 0)
            def _():
                act(pltpu.make_async_copy(scan.at[index], out.at[place], sem.at[place]))

    each(lambda copy: copy.start())
    each(lambda copy: copy.wait())


def pack(send_list, scan):
    places = send_list.shape[1]
    hbm = pl.BlockSpec(memory_space=pl.ANY)
    return pl.pallas_call(
        pack_kernel,
        out_shape=jax.ShapeDtypeStruct((places,) + scan.shape[1:], BF16),
        in_specs=[hbm, hbm],
        out_specs=hbm,
        scratch_shapes=[
            pltpu.SMEM(send_list.shape, jnp.int32),
            pltpu.SemaphoreType.DMA((places,)),
            pltpu.SemaphoreType.DMA,
        ],
        compiler_params=pltpu.CompilerParams(vmem_limit_bytes=LARGE_LIMIT),
        cost_estimate=pl.CostEstimate(flops=0, bytes_accessed=1_000_000, transcendentals=0),
        name="pack_states",
    )(scan, send_list)


def lane_table(inner, group, table, key):
    taps, _, channels = inner.shape
    width = group.shape[2]
    for tap in range(taps):
        table[:, tap * channels : (tap + 1) * channels] = inner[tap].astype(F32)
    first = taps * channels
    for tap in range(taps):
        table[:, first + tap * width : first + (tap + 1) * width] = group[tap].astype(F32)
    first += taps * width
    table[:, first:] = jnp.full((table.shape[0], table.shape[1] - first), key, F32)


def window_lanes(inner, group):
    taps = inner.shape[0]
    return round_up(taps * (inner.shape[2] + group.shape[2]) + 1, LANES)


def windows_kernel(send, inner, group, out, table, picked):
    lane_table(inner, group, table, -1.0)
    picked[...] = jnp.full(picked.shape, -1.0, F32)
    key_lane = inner.shape[0] * (inner.shape[2] + group.shape[2])
    is_key = lax.broadcasted_iota(jnp.int32, (1, table.shape[1]), 1) >= key_lane
    count = 0
    for place in range(send.shape[1]):
        index = send[0, place]
        key = jnp.where(index >= 0, place, -1).astype(F32)
        row = table[pl.ds(jnp.maximum(index, 0), 1), :]
        picked[pl.ds(count, 1), :] = jnp.where(is_key, key, row)
        count = count + jnp.where(index >= 0, 1, 0)
    out[...] = picked[: out.shape[0]].astype(BF16)


def pack_windows(send_list, inner, group):
    _, slots, _ = inner.shape
    lanes = window_lanes(inner, group)
    rows = round_up(slots // 2, 16)
    vmem = pl.BlockSpec(memory_space=pltpu.VMEM)
    smem = pl.BlockSpec(memory_space=pltpu.SMEM)
    return pl.pallas_call(
        windows_kernel,
        out_shape=jax.ShapeDtypeStruct((rows, lanes), BF16),
        in_specs=[smem, vmem, vmem],
        out_specs=vmem,
        scratch_shapes=[
            pltpu.VMEM((slots, lanes), F32),
            pltpu.VMEM((round_up(send_list.shape[1] + 1, 8), lanes), F32),
        ],
        compiler_params=pltpu.CompilerParams(vmem_limit_bytes=SMALL_LIMIT),
        cost_estimate=pl.CostEstimate(flops=0, bytes_accessed=200_000, transcendentals=0),
        name="pack_windows",
    )(send_list, inner, group)


def split_order(receive, slots, plan):
    def step(slot, counts):
        kept, moved = counts
        entry = receive[0, slot]
        stays = entry < 0
        plan[0, jnp.where(stays, kept, slots // 2 + moved)] = slot
        plan[0, jnp.where(stays, PLAN - 1, slots + moved)] = entry
        return (kept + jnp.where(stays, 1, 0), moved + jnp.where(stays, 0, 1))

    lax.fori_loop(0, slots, step, (jnp.int32(0), jnp.int32(0)))


def project_kernel(
    replicas,
    cap,
    receive,
    live,
    decay_log,
    delta_bias,
    skip_gain,
    own,
    other,
    inner_weight,
    gate_weight,
    group_weight,
    delta_weight,
    inner_taps,
    inner_offset,
    group_taps,
    group_offset,
    inner,
    group,
    receive_lanes,
    arrived,
    inner_next,
    group_next,
    driven,
    decay,
    skipped,
    gate,
    maps,
    plan,
    table,
    small,
    ordered,
):
    me = lax.axis_index("dp")
    head = lax.axis_index("head")
    taps, slots, channels = inner.shape
    half = own.shape[1]
    width = group.shape[2]
    steps = own.shape[0] // slots

    split_order(receive, slots, plan)
    lane_table(inner, group, table, 0.0)
    rows = arrived.shape[0] // replicas
    places = replicas * cap
    entry = receive_lanes[...].astype(F32)
    source = jnp.floor((entry + 0.5) * (1.0 / cap))
    wanted = entry + source * float(places - cap) + (me * cap).astype(F32)
    wanted = jnp.where(entry >= 0.0, wanted, -2.0)
    key_lane = taps * (channels + width)
    key = arrived[:, key_lane : key_lane + 1].astype(F32)
    owner = (lax.broadcasted_iota(jnp.int32, (arrived.shape[0], 1), 0) // rows).astype(F32)
    key = jnp.where(key >= 0.0, key + owner * float(places), -1.0)
    hits = (key == wanted).astype(F32).astype(BF16)

    def pick(value):
        return lax.dot_general(
            hits, value, (((0,), (0,)), ((), ())), preferred_element_type=F32
        )

    taken = pick(jnp.ones((arrived.shape[0], LANES), BF16)) > 0.5
    for first in range(0, table.shape[1], LANES):
        lanes = slice(first, first + LANES)
        table[:, lanes] = jnp.where(taken, pick(arrived[:, lanes]), table[:, lanes])

    mine = pl.ds(pl.multiple_of(head * half, half), half)
    theirs = pl.ds(pl.multiple_of((1 - head) * half, half), half)

    def columns(weight):
        return jnp.dot(own[...], weight[mine, :], preferred_element_type=F32) + jnp.dot(
            other[...], weight[theirs, :], preferred_element_type=F32
        )

    def rows_of(weight, count):
        def one(tokens, part):
            piece = weight[:, part]
            if count > 1:
                piece = jnp.broadcast_to(piece, (count, half))
            return lax.dot_general(
                tokens, piece, (((1,), (1,)), ((), ())), preferred_element_type=F32
            )

        return one(own[...], mine) + one(other[...], theirs)

    def rounded(value):
        return value.astype(BF16).astype(F32)

    inner_raw = rounded(columns(inner_weight))
    gate_raw = rounded(columns(gate_weight))
    group_raw = rounded(rows_of(group_weight, 1))
    delta_raw = rounded(rows_of(delta_weight, LANES))

    living = lax.broadcasted_iota(jnp.int32, (slots, LANES), 0) < live[0]
    gate[...] = silu(gate_raw)
    shifted = delta_raw + delta_bias[0]
    delta = jnp.maximum(shifted, 0.0) + jnp.log1p(jnp.exp(-jnp.abs(shifted)))
    slope = jnp.exp(jnp.full((1, LANES), decay_log[0], F32))
    decay[...] = jnp.exp(-delta * slope)

    def convolve(carried, raw, weights, offset):
        joined = carried + [raw[step * slots : (step + 1) * slots] for step in range(steps)]
        results = []
        for step in range(steps):
            summed = offset[...]
            for tap in range(taps + 1):
                summed = summed + joined[step + tap] * weights[tap : tap + 1, :]
            results.append(rounded(silu(summed)))
        return results, joined[steps:]

    inner_conv, inner_carry = convolve(
        [table[:, tap * channels : (tap + 1) * channels] for tap in range(taps)],
        inner_raw,
        inner_taps,
        inner_offset,
    )
    first = taps * channels
    group_conv, group_carry = convolve(
        [table[:, first + tap * width : first + (tap + 1) * width] for tap in range(taps)],
        group_raw,
        group_taps,
        group_offset,
    )
    for tap in range(taps):
        inner_next[tap] = jnp.where(living, inner_carry[tap], 0.0).astype(BF16)
        group_next[tap] = jnp.where(living[:, :width], group_carry[tap], 0.0).astype(BF16)
    for step in range(steps):
        part = slice(step * slots, (step + 1) * slots)
        driven[part, :] = delta[part] * inner_conv[step]
        skipped[part, :] = inner_conv[step] * skip_gain[0]
        small[part, :width] = group_conv[step]
        small[part, width:] = jnp.zeros((slots, LANES - width), F32)
    stride = LANES // steps
    ordered[...] = jnp.zeros_like(ordered)
    for position in range(slots):
        slot = plan[0, position]
        for step in range(steps):
            ordered[pl.ds(step * stride + position, 1), :] = small[
                pl.ds(step * slots + slot, 1), :
            ]
    maps[...] = ordered[...].T[:width].astype(BF16)


def project(replicas, cap, scalars, operands):
    own, inner, group = operands[0], operands[-4], operands[-3]
    _, slots, _ = inner.shape
    width = group.shape[2]
    rows = own.shape[0]
    vmem = pl.BlockSpec(memory_space=pltpu.VMEM)
    smem = pl.BlockSpec(memory_space=pltpu.SMEM)
    full = jax.ShapeDtypeStruct((rows, LANES), F32)
    return pl.pallas_call(
        functools.partial(project_kernel, replicas, cap),
        out_shape=[
            jax.ShapeDtypeStruct(inner.shape, BF16),
            jax.ShapeDtypeStruct(group.shape, BF16),
            full,
            full,
            full,
            full,
            jax.ShapeDtypeStruct((width, LANES), BF16),
            jax.ShapeDtypeStruct((1, PLAN), jnp.int32),
        ],
        in_specs=[smem] * len(scalars) + [vmem] * len(operands),
        out_specs=[vmem] * 7 + [smem],
        scratch_shapes=[
            pltpu.VMEM((slots, window_lanes(inner, group)), F32),
            pltpu.VMEM((rows, LANES), F32),
            pltpu.VMEM((LANES, LANES), F32),
        ],
        compiler_params=pltpu.CompilerParams(vmem_limit_bytes=VMEM_LIMIT),
        cost_estimate=pl.CostEstimate(
            flops=300_000_000, bytes_accessed=5_000_000, transcendentals=100_000
        ),
        name="project_convolve",
    )(*scalars, *operands)


def advance_slot(state, driven, decay, sums, maps, position, slot, slots, steps):
    input_map, output_map = maps
    stride = LANES // steps
    hidden = state.astype(F32)
    for step in range(steps):
        lane = step * stride + position
        row = pl.ds(step * slots + slot, 1)
        hidden = decay[row, :] * hidden + driven[row, :] * input_map[:, lane : lane + 1]
        sums[row, :] = jnp.sum(hidden * output_map[:, lane : lane + 1], axis=0, keepdims=True)
        result = hidden.astype(BF16)
        hidden = result.astype(F32)
    return result


def pair_maps(own_maps, other_maps):
    first = lax.axis_index("head") == 0
    mine, theirs = own_maps[...].astype(F32), other_maps[...].astype(F32)
    return jnp.where(first, mine, theirs), jnp.where(first, theirs, mine)


def stay_kernel(
    steps, plan, live, driven, decay, own_maps, other_maps, scan, sums, scan_next, done, sem
):
    slots = scan.shape[0]
    maps = pair_maps(own_maps, other_maps)
    copies = []
    for position in range(slots // 2):
        slot = plan[0, position]
        result = advance_slot(
            scan[slot], driven, decay, sums, maps, position, slot, slots, steps
        )
        done[position] = jnp.where(slot < live[0], result, jnp.zeros_like(result))
        copies.append(
            pltpu.make_async_copy(done.at[position], scan_next.at[slot], sem.at[position])
        )
        copies[-1].start()
    for copy in copies:
        copy.wait()


def arrive_kernel(
    steps,
    plan,
    live,
    driven,
    decay,
    skipped,
    gate,
    own_maps,
    other_maps,
    sums_in,
    scan_in,
    arrived,
    gated_out,
    scan_next,
    sums,
    done,
    gated,
    sem,
):
    del scan_in
    slots = scan_next.shape[0]
    moving = slots // 2
    maps = pair_maps(own_maps, other_maps)
    sums[...] = sums_in[...]
    copies = []
    for position in range(moving, slots):
        slot = plan[0, position]
        result = advance_slot(
            arrived[plan[0, moving + position]],
            driven,
            decay,
            sums,
            maps,
            position,
            slot,
            slots,
            steps,
        )
        place = position - moving
        done[place] = jnp.where(slot < live[0], result, jnp.zeros_like(result))
        copies.append(pltpu.make_async_copy(done.at[place], scan_next.at[slot], sem.at[place]))
        copies[-1].start()
    living = lax.broadcasted_iota(jnp.int32, (slots, LANES), 0) < live[0]
    for step in range(steps):
        part = slice(step * slots, (step + 1) * slots)
        value = (sums[part, :] + skipped[part, :]) * gate[part, :]
        gated[step] = jnp.where(living, value, 0.0).astype(BF16)
    copies.append(pltpu.make_async_copy(gated, gated_out, sem.at[moving]))
    copies[-1].start()
    for copy in copies:
        copy.wait()


def stay(steps, plan, live, driven, decay, own_maps, other_maps, scan):
    slots = scan.shape[0]
    vmem = pl.BlockSpec(memory_space=pltpu.VMEM)
    smem = pl.BlockSpec(memory_space=pltpu.SMEM)
    hbm = pl.BlockSpec(memory_space=pl.ANY)
    return pl.pallas_call(
        functools.partial(stay_kernel, steps),
        out_shape=[
            jax.ShapeDtypeStruct(driven.shape, F32),
            jax.ShapeDtypeStruct(scan.shape, BF16),
        ],
        in_specs=[smem] * 2 + [vmem] * 5,
        out_specs=[vmem, hbm],
        scratch_shapes=[
            pltpu.VMEM((slots // 2,) + scan.shape[1:], BF16),
            pltpu.SemaphoreType.DMA((slots // 2,)),
        ],
        compiler_params=pltpu.CompilerParams(vmem_limit_bytes=SMALL_LIMIT),
        cost_estimate=pl.CostEstimate(
            flops=10_000_000, bytes_accessed=2_000_000, transcendentals=0
        ),
        name="advance_staying",
    )(plan, live, driven, decay, own_maps, other_maps, scan)


def arrive(steps, plan, live, operands, sums, scan_next, arrived):
    slots = scan_next.shape[0]
    vmem = pl.BlockSpec(memory_space=pltpu.VMEM)
    smem = pl.BlockSpec(memory_space=pltpu.SMEM)
    hbm = pl.BlockSpec(memory_space=pl.ANY)
    gated = jax.ShapeDtypeStruct((steps, slots, LANES), BF16)
    return pl.pallas_call(
        functools.partial(arrive_kernel, steps),
        out_shape=[gated, jax.ShapeDtypeStruct(scan_next.shape, BF16)],
        in_specs=[smem] * 2 + [vmem] * (len(operands) + 1) + [hbm, vmem],
        out_specs=[hbm, hbm],
        scratch_shapes=[
            pltpu.VMEM(sums.shape, F32),
            pltpu.VMEM((slots // 2,) + scan_next.shape[1:], BF16),
            pltpu.VMEM(gated.shape, BF16),
            pltpu.SemaphoreType.DMA((slots // 2 + 1,)),
        ],
        input_output_aliases={3 + len(operands): 1},
        compiler_params=pltpu.CompilerParams(vmem_limit_bytes=SMALL_LIMIT),
        cost_estimate=pl.CostEstimate(
            flops=10_000_000, bytes_accessed=2_000_000, transcendentals=0
        ),
        name="advance_arrived",
    )(plan, live, *operands, sums, scan_next, arrived)


def swap_heads(value):
    return lax.ppermute(value, "head", [(0, 1), (1, 0)])


def per_device(
    replicas,
    tokens,
    inner_weight,
    gate_weight,
    group_weight,
    delta_weight,
    inner_taps,
    inner_offset,
    group_taps,
    group_offset,
    decay_log,
    delta_bias,
    skip_gain,
    inner_window,
    group_window,
    scan_state,
    send_list,
    receive_list,
    live_count,
):
    steps, slots, half = tokens.shape
    cap = send_list.shape[1] // replicas
    scan = jnp.transpose(scan_state, (0, 2, 1))
    inner = jnp.transpose(inner_window, (1, 0, 2))
    group = jnp.transpose(group_window, (1, 0, 2))
    own = tokens.reshape(steps * slots, half)

    states = lax.all_to_all(pack(send_list, scan), "dp", 0, 0, tiled=True)
    windows = lax.all_gather(pack_windows(send_list, inner, group), "dp", axis=0, tiled=True)
    scalars = (receive_list, live_count, decay_log, delta_bias, skip_gain)
    operands = (
        own,
        swap_heads(own),
        inner_weight,
        gate_weight,
        group_weight.T,
        delta_weight.T,
        inner_taps,
        inner_offset[None],
        group_taps,
        group_offset[None],
        inner,
        group,
        receive_list,
        windows,
    )
    inner_next, group_next, driven, decay, skipped, gate, maps, plan = project(
        replicas, cap, scalars, operands
    )
    other_maps = swap_heads(maps)
    sums, scan_next = stay(steps, plan, live_count, driven, decay, maps, other_maps, scan)
    gated, scan_next = arrive(
        steps,
        plan,
        live_count,
        (driven, decay, skipped, gate, maps, other_maps),
        sums,
        scan_next,
        states,
    )
    return (
        gated,
        jnp.transpose(inner_next, (1, 0, 2)),
        jnp.transpose(group_next, (1, 0, 2)),
        jnp.transpose(scan_next, (0, 2, 1)),
    )


def solution(mesh):
    in_specs = (
        P(None, ("grp", "dp"), "head"),
        P(None, "head"),
        P(None, "head"),
        P(None, "head"),
        P(None, "head"),
        P(None, "head"),
        P("head"),
        P(None, "head"),
        P("head"),
        P("head"),
        P("head"),
        P("head"),
        P(("grp", "dp"), None, "head"),
        P(("grp", "dp"), None, "head"),
        P(("grp", "dp"), "head", None),
        P(("grp", "dp"), None),
        P(("grp", "dp"), None),
        P(("grp", "dp")),
    )
    out_specs = (
        P(None, ("grp", "dp"), "head"),
        P(("grp", "dp"), None, "head"),
        P(("grp", "dp"), None, "head"),
        P(("grp", "dp"), "head", None),
    )
    return jax.shard_map(
        functools.partial(per_device, mesh.shape["dp"]),
        mesh=mesh,
        in_specs=in_specs,
        out_specs=out_specs,
        check_vma=False,
    )
```

time: 64.8 us -> 84.4 us (1.30)
  the two profiles are of different devices: /device:TPU:11 before, /device:TPU:0 now
where the time goes in v2:
time: 84.4 us; the launch traced here: 83.8 us
  blocking collectives  39.1 us (46%)
  Pallas kernels  24.7 us (29%)
  local copies, waits for them, and re-layouts  8.01 us (9%)
  starting transfers between devices  7.37 us (9%)
  between operations  3.44 us (4%)
  waiting for transfers between devices  1.19 us (1%)
    all_gather x1, blocking collectives, per_device(): lax.all_gather(pack_windows(send_list, inner, group), 'dp', axis=0, tiled...  39.1 us
    pallas_call x1, Pallas kernels, pack(): pl.pallas_call(pack_kernel, out_shape=jax.ShapeDtypeStruct((places,) + sc...  16.3 us
    unnamed x52, local copies, waits for them, and re-layouts  8.01 us
    all_to_all x1, starting transfers between devices, per_device(): states = lax.all_to_all(pack(send_list, scan), 'dp', 0, 0, tiled=True)  7.36 us
    pallas_call x1, Pallas kernels, project(): pl.pallas_call(functools.partial(project_kernel, replicas, cap), out_shap...  3.25 us
    pallas_call x1, Pallas kernels, arrive(): pl.pallas_call(functools.partial(arrive_kernel, steps), out_shape=[gated,...  2.1 us
    pallas_call x1, Pallas kernels, stay(): pl.pallas_call(functools.partial(stay_kernel, steps), out_shape=[jax.Shap...  2.07 us
  transfers between devices with their start and end apart: 3, of which 1 were waited for; matrix products, arithmetic and copies ran while one was open for 0% of the time, Pallas kernels for 7%

profile of v2, /device:TPU:0, one launch (start us, length us, event | category | flops | bytes accessed | tf_op | source)
XLA Modules:
  0.0 83.8 jit_solution(4447959724414287294)
XLA Ops:
  0.6 0.0 copy-start.23
  0.6 0.0 copy-start.3
  0.7 16.3 %pack_states.1 = bf16[56,64,128]{2,1,0:T(8,128)(2,1)} custom-call(bf16[56,64,128]{2,1,0:T(8,128)(2,1)} %bitcast.11, s32[1,56]{1,0:T(1,128)} %send.3), custom_call_target="tpu_custom_call" | custom-call | bytes 1000000 | tf_op jit(solution)/shard_map/pack_states/pallas_call | solution.py:47
  17.0 0.0 copy-start.1
  17.0 0.0 copy-start.2
  17.0 7.4 %all-to-all-start = ((bf16[56,64,128]{2,1,0:T(8,128)(2,1)}), bf16[56,64,128]{2,1,0:T(8,128)(2,1)S(1)}, u32[]{:S(2)}, u32[]{:S(2)}) async-start(bf16[56,64,128]{2,1,0:T(8,128)(2,1)} %pack_states.1), calls=%async_computation | async-start | bytes 1835008 | tf_op jit(solution)/shard_map/all_to_all | solution.py:482
  24.4 0.0 collective-permute-start
  27.0 0.0 copy-done.23
  27.0 0.0 copy-start.9
  27.0 0.8 copy-done.9
  27.8 0.8 copy-done.11
  28.6 1.0 %pack_windows.1 = bf16[32,640]{1,0:T(8,128)(2,1)S(1)} custom-call(s32[1,56]{1,0:T(1,128)S(1)} %copy-done.23, bf16[3,56,128]{2,1,0:T(8,128)(2,1)S(1)} %bitcast.16, bf16[3,56,64]{2,1,0:T(8,128)(2,1)S(1)} %bitcast.18), custom_call_target="tpu_custom_call" | custom-call | bytes 200000 | tf_op jit(solution)/shard_map/pack_windows/pallas_call | solution.py:101
  29.5 0.0 copy-start.10
  29.5 0.0 copy-start.12
  29.5 0.0 copy-start.17
  29.6 39.1 %all_gather.3.arrived = bf16[256,640]{1,0:T(8,128)(2,1)S(1)} all-gather(bf16[32,640]{1,0:T(8,128)(2,1)S(1)} %pack_windows.1), channel_id=1, replica_groups=mesh['grp'=2,'dp'=8,'head'=2] {'dp'}, dimensions={0}, use_global_device_ids=true | all-gather | bytes 368640 | tf_op jit(solution)/shard_map/all_gather | solution.py:483
  68.6 0.0 collective-permute-done.other
  68.6 0.0 copy-start.20
  68.6 0.0 copy-start.24
  68.7 0.0 copy-start.25
  68.7 0.0 copy-done.3
  68.7 0.0 copy-done.1
  68.7 0.0 copy-done.2
  68.7 0.0 copy-done.10
  68.7 0.0 copy-done.12
  68.7 0.0 copy-done.17
  68.7 0.6 copy-done.19
  69.3 0.0 copy-done.18
  69.3 0.0 copy-done.20
  69.3 0.0 copy-done.24
  69.3 0.0 copy-done.25
  69.3 1.0 %copy-done.4 = bf16[2,56,2048]{2,1,0:T(8,128)(2,1)S(1)} copy-done((bf16[2,56,2048]{2,1,0:T(8,128)(2,1)S(1)}, bf16[2,56,2048]{2,1,0:T(8,128)(2,1)}, u32[]{:S(2)}) %copy-start.4) | copy-done | bytes 458776
  70.4 3.3 %project_convolve.1 = (bf16[3,56,128]{2,1,0:T(8,128)(2,1)}, bf16[3,56,64]{2,1,0:T(8,128)(2,1)}, f32[112,128]{1,0:T(8,128)S(1)}, f32[112,128]{1,0:T(8,128)S(1)}, ...) custom-call(s32[1,56]{1,0:T(1,128)S(1)} %copy-done.20, ...), custom_call_target="tpu_custom_call" | custom-call | flops 300000000 | bytes 5000000 | tf_op jit(solution)/shard_map/project_convolve/pallas_call | solution.py:278
  73.6 0.0 copy-start.13
  73.6 0.6 copy-done.13
  74.3 0.6 copy-done.15
  74.9 0.0 collective-permute-start.1
  74.9 1.2 %collective-permute-done.1.other_maps = bf16[64,128]{1,0:T(8,128)(2,1)S(1)} collective-permute-done((bf16[64,128]{1,0:T(8,128)(2,1)S(1)}, bf16[64,128]{1,0:T(8,128)(2,1)S(1)}, u32[]{:S(2)}, u32[]{:S(2)}) %collective-permute-start.1) | collective-permute-done | bytes 16416 | tf_op jit(solution)/shard_map/ppermute | solution.py:451
  76.1 0.0 copy-done.21
  76.1 0.0 copy-done
  76.1 2.1 %advance_staying.1 = (f32[112,128]{1,0:T(8,128)S(1)}, bf16[56,64,128]{2,1,0:T(8,128)(2,1)}) custom-call(s32[1,128]{1,0:T(1,128)S(1)} %get-tuple-element.16.plan, s32[1]{0:T(128)S(6)} %copy.27.live, f32[112,128]{1,0:T(8,128)S(1)} %get-tuple-element.17.driven, f32[112,128]{1,0:T(8,128)S(1)} %get-tuple-element.18.decay, ...), custom_call_target="tpu_custom_call" | custom-call | flops 10000000 | bytes 2000000 | tf_op jit(solution)/shard_map/advance_staying/pallas_call | solution.py:404
  78.2 0.6 copy-done.5
  78.8 0.6 copy-done.7
  79.4 0.0 all-to-all-done.arrived
  79.4 0.6 copy-done.22
  80.0 0.8 copy-done.6
  80.9 0.8 copy-done.8
  81.7 2.1 %advance_arrived.1 = (bf16[2,56,128]{2,1,0:T(8,128)(2,1)}, bf16[56,64,128]{2,1,0:T(8,128)(2,1)}) custom-call(s32[1,128]{1,0:T(1,128)S(1)} %copy-done.22, s32[1]{0:T(128)S(6)} %copy.27.live, f32[112,128]{1,0:T(8,128)S(1)} %copy-done.6, f32[112,128]{1,0:T(8,128)S(1)} %copy-done.8, f32[112,128]{1,0:T(8,128)S(1)} %copy-done.14, ...), custom_call_target="tpu_custom_call", output_to_operand_aliasing={{1}: (9, {})} | custom-call | flops 10000000 | bytes 2000000 | tf_op jit(solution)/shard_map/advance_arrived/pallas_call | solution.py:430
  (16 shorter events, 0.0 us)
Async XLA Ops:
  0.6 26.4 %copy-start.23 = (s32[1,56]{1,0:T(1,128)S(1)}, s32[1,56]{1,0:T(1,128)}, u32[]{:S(2)}) copy-start(s32[1,56]{1,0:T(1,128)} %send.3) | copy-start | bytes 676
  0.6 68.0 %copy-start.3 = (bf16[4096,64]{0,1:T(8,128)(2,1)S(1)}, bf16[4096,64]{0,1:T(8,128)(2,1)}, u32[]{:S(2)}) copy-start(bf16[4096,64]{0,1:T(8,128)(2,1)} %param.21) | copy-start | bytes 1572868
  17.0 51.7 %copy-start.1 = (bf16[4096,128]{1,0:T(8,128)(2,1)S(1)}, bf16[4096,128]{1,0:T(8,128)(2,1)}, u32[]{:S(2)}) copy-start(bf16[4096,128]{1,0:T(8,128)(2,1)} %inner_weight.1) | copy-start | bytes 3145732
  17.0 51.7 %copy-start.2 = (bf16[4096,128]{1,0:T(8,128)(2,1)S(1)}, bf16[4096,128]{1,0:T(8,128)(2,1)}, u32[]{:S(2)}) copy-start(bf16[4096,128]{1,0:T(8,128)(2,1)} %gate_weight.1) | copy-start | bytes 3145732
  17.0 62.4 %all-to-all-start = ((bf16[56,64,128]{2,1,0:T(8,128)(2,1)}), bf16[56,64,128]{2,1,0:T(8,128)(2,1)S(1)}, u32[]{:S(2)}, u32[]{:S(2)}) async-start(bf16[56,64,128]{2,1,0:T(8,128)(2,1)} %pack_states.1), calls=%async_computation | async-start | bytes 1835008 | tf_op jit(solution)/shard_map/all_to_all | solution.py:482
  24.4 44.2 %collective-permute-start = (bf16[112,2048]{1,0:T(8,128)(2,1)}, bf16[112,2048]{1,0:T(8,128)(2,1)S(1)}, u32[]{:S(2)}, u32[]{:S(2)}) collective-permute-start(bf16[112,2048]{1,0:T(8,128)(2,1)} %bitcast.14), channel_id=1, source_target_pairs={{0,1},{1,0},{2,3},{3,2},{4,5},{5,4},{6,7},{7,6},{8,9},{9,8},{10,11... | collective-permute-start | bytes 1376264 | tf_op jit(solution)/shard_map/ppermute | solution.py:451
  27.0 0.8 copy-start.9
  27.8 0.8 copy-start.11
  29.5 39.2 %copy-start.10 = (bf16[56,3,128]{2,0,1:T(8,128)(2,1)S(1)}, bf16[56,3,128]{2,0,1:T(8,128)(2,1)}, u32[]{:S(2)}) copy-start(bf16[56,3,128]{2,0,1:T(8,128)(2,1)} %param.30) | copy-start | bytes 129028
  29.5 39.2 %copy-start.12 = (bf16[56,3,64]{2,0,1:T(8,128)(2,1)S(1)}, bf16[56,3,64]{2,0,1:T(8,128)(2,1)}, u32[]{:S(2)}) copy-start(bf16[56,3,64]{2,0,1:T(8,128)(2,1)} %param.31) | copy-start | bytes 64516
  29.5 39.2 %copy-start.17 = (bf16[4096,1]{0,1:T(2,128)(2,1)S(1)}, bf16[4096,1]{0,1:T(2,128)(2,1)}, u32[]{:S(2)}) copy-start(bf16[4096,1]{0,1:T(2,128)(2,1)} %param.22) | copy-start | bytes 24580
  68.6 0.7 copy-start.19
  68.6 0.7 copy-start.18
  68.6 0.7 copy-start.20
  68.6 0.7 copy-start.24
  68.7 0.7 copy-start.25
  69.3 1.0 %copy-start.4 = (bf16[2,56,2048]{2,1,0:T(8,128)(2,1)S(1)}, bf16[2,56,2048]{2,1,0:T(8,128)(2,1)}, u32[]{:S(2)}) copy-start(bf16[2,56,2048]{2,1,0:T(8,128)(2,1)} %param.18) | copy-start | bytes 1376260
  70.4 5.7 %copy-start = (bf16[56,128,64]{1,2,0:T(8,128)(2,1)S(1)}, bf16[56,128,64]{1,2,0:T(8,128)(2,1)}, u32[]{:S(2)}) copy-start(bf16[56,128,64]{1,2,0:T(8,128)(2,1)} %param.32) | copy-start | bytes 2752516
  73.6 0.6 copy-start.13
  74.2 0.6 copy-start.15
  74.9 1.2 %copy-start.21 = (s32[1,128]{1,0:T(1,128)}, s32[1,128]{1,0:T(1,128)S(1)}, u32[]{:S(2)}) copy-start(s32[1,128]{1,0:T(1,128)S(1)} %get-tuple-element.16.plan) | copy-start | bytes 1540
  74.9 1.2 %collective-permute-start.1 = (bf16[64,128]{1,0:T(8,128)(2,1)S(1)}, bf16[64,128]{1,0:T(8,128)(2,1)S(1)}, u32[]{:S(2)}, u32[]{:S(2)}) collective-permute-start(bf16[64,128]{1,0:T(8,128)(2,1)S(1)} %get-tuple-element.21.own_maps), channel_id=1, source_target_pairs={{0,1},{1,0},{2,3},{3,2},{4,5},{5,4},{6,7},{7,6},{8,9},{9,8},{10,11... | collective-permute-start | bytes 49160 | tf_op jit(solution)/shard_map/ppermute | solution.py:451
  76.1 3.3 %copy-start.14 = (f32[112,128]{1,0:T(8,128)S(1)}, f32[112,128]{1,0:T(8,128)}, u32[]{:S(2)}) copy-start(f32[112,128]{1,0:T(8,128)} %copy-done.13) | copy-start | bytes 172036
  76.1 3.3 %copy-start.16 = (f32[112,128]{1,0:T(8,128)S(1)}, f32[112,128]{1,0:T(8,128)}, u32[]{:S(2)}) copy-start(f32[112,128]{1,0:T(8,128)} %copy-done.15) | copy-start | bytes 172036
  78.1 0.6 copy-start.5
  78.8 0.6 copy-start.7
  79.4 0.7 copy-start.22
  80.0 0.8 copy-start.6
  80.9 0.8 copy-start.8

commit v3 on v0

v3 whole, which is shorter than its diff:
```python
import functools

import jax
import jax.numpy as jnp
from jax import lax
from jax.experimental import pallas as pl
from jax.experimental.pallas import tpu as pltpu
from jax.sharding import PartitionSpec as P

F32 = jnp.float32
BF16 = jnp.bfloat16
SMALL_LIMIT = 8 * 1024 * 1024
MEDIUM_LIMIT = 32 * 1024 * 1024
LARGE_LIMIT = 60 * 1024 * 1024
MAX_SHIFTS = 16
LANES = 128
ROWS = 8

VMEM = pl.BlockSpec(memory_space=pltpu.VMEM)
SMEM = pl.BlockSpec(memory_space=pltpu.SMEM)
HBM = pl.BlockSpec(memory_space=pl.ANY)


def round_up(value, step):
    return -(-value // step) * step


def silu(value):
    return value * jax.nn.sigmoid(value)


def rounded(value):
    return value.astype(BF16).astype(F32)


def shifts_of(replicas):
    if replicas > MAX_SHIFTS:
        return []
    return sorted(range(1, replicas), key=lambda shift: abs(2 * shift - replicas))


def both_halves(mine, theirs):
    first = lax.axis_index("head") == 0
    return jnp.concatenate(
        [jnp.where(first, mine, theirs), jnp.where(first, theirs, mine)], axis=-1
    )


def pack_kernel(replicas, cap, scan, send, inner, group, group_other, *refs):
    shifts = shifts_of(replicas)
    count = max(1, len(shifts))
    outs = refs[:count]
    (indices, inner_in, mine_in, theirs_in, held, table, picked, cast) = refs[count : count + 8]
    load_sem, in_sem, out_sem, window_sem = refs[count + 8 :]
    loads = [
        pltpu.make_async_copy(source, target, load_sem.at[place])
        for place, (source, target) in enumerate(
            [(send, indices), (inner, inner_in), (group, mine_in), (group_other, theirs_in)]
        )
    ]
    for load in loads:
        load.start()
    me = lax.axis_index("dp")
    taps, _, channels = inner_in.shape
    state_rows = scan.shape[1]
    blocks = []
    if shifts:
        for ref, shift in zip(outs, shifts):
            blocks.append((ref.at[0], lax.rem(me + shift, replicas)))
    else:
        blocks = [(outs[0].at[target], target) for target in range(replicas)]
    loads[0].wait()

    plan = []
    for block, (ref, target) in enumerate(blocks):
        for c in range(cap):
            plan.append((block, ref, c, indices[0, target * cap + c]))

    def fetch(place, index):
        return pltpu.make_async_copy(scan.at[index], held.at[place], in_sem.at[place])

    def store(place, ref, c):
        return pltpu.make_async_copy(
            held.at[place], ref.at[pl.ds(c * state_rows, state_rows)], out_sem.at[place]
        )

    for place, (_, _, _, index) in enumerate(plan):

        @pl.when(index >= 0)
        def _():
            fetch(place, index).start()

    for load in loads[1:]:
        load.wait()
    for tap in range(taps):
        table[:, tap * LANES : (tap + 1) * LANES] = inner_in[tap].astype(F32)
        table[:, (taps + tap) * LANES : (taps + tap + 1) * LANES] = both_halves(
            mine_in[tap].astype(F32), theirs_in[tap].astype(F32)
        )
    picked[...] = jnp.zeros_like(picked)
    for place, (block, _, c, index) in enumerate(plan):
        row = table[pl.ds(jnp.maximum(index, 0), 1), :]
        for kind in range(2 * taps):
            picked[block, kind * ROWS + c : kind * ROWS + c + 1, :] = row[
                :, kind * LANES : (kind + 1) * LANES
            ]
    windows = []
    for block, (ref, _) in enumerate(blocks):
        cast[block] = picked[block].astype(BF16)
        windows.append(
            pltpu.make_async_copy(
                cast.at[block],
                ref.at[pl.ds(cap * state_rows, cast.shape[1])],
                window_sem.at[block],
            )
        )
        windows[-1].start()

    for place, (_, ref, c, index) in enumerate(plan):

        @pl.when(index >= 0)
        def _():
            fetch(place, index).wait()
            store(place, ref, c).start()

    for place, (_, ref, c, index) in enumerate(plan):

        @pl.when(index >= 0)
        def _():
            store(place, ref, c).wait()

    for window in windows:
        window.wait()


def pack(replicas, cap, send_list, scan, inner, group, group_other):
    shifts = shifts_of(replicas)
    count = max(1, len(shifts))
    per_block = 1 if shifts else replicas
    taps, slots, _ = inner.shape
    window_rows = 2 * taps * ROWS
    rows = cap * scan.shape[1] + window_rows
    blocks = count * per_block
    places = blocks * cap
    return pl.pallas_call(
        functools.partial(pack_kernel, replicas, cap),
        out_shape=[jax.ShapeDtypeStruct((per_block, rows, LANES), BF16)] * count,
        in_specs=[HBM] * 5,
        out_specs=[HBM] * count,
        scratch_shapes=[
            pltpu.SMEM(send_list.shape, jnp.int32),
            pltpu.VMEM(inner.shape, BF16),
            pltpu.VMEM(group.shape, BF16),
            pltpu.VMEM(group.shape, BF16),
            pltpu.VMEM((places,) + scan.shape[1:], BF16),
            pltpu.VMEM((slots, 2 * taps * LANES), F32),
            pltpu.VMEM((blocks, window_rows, LANES), F32),
            pltpu.VMEM((blocks, window_rows, LANES), BF16),
            pltpu.SemaphoreType.DMA((4,)),
            pltpu.SemaphoreType.DMA((places,)),
            pltpu.SemaphoreType.DMA((places,)),
            pltpu.SemaphoreType.DMA((blocks,)),
        ],
        compiler_params=pltpu.CompilerParams(vmem_limit_bytes=LARGE_LIMIT),
        cost_estimate=pl.CostEstimate(flops=0, bytes_accessed=2_000_000, transcendentals=0),
        name="pack_leaving",
    )(scan, send_list, inner, group, group_other)


def make_plan(replicas, cap, receive, slots, plan, inverse):
    moving = slots // 2
    for entry in range(replicas * cap):
        inverse[entry] = -1

    def kept_step(slot, kept):
        entry = receive[0, slot]
        stays = entry < 0
        plan[0, jnp.where(stays, kept, slots - 1)] = slot
        inverse[jnp.where(stays, replicas * cap, entry)] = slot
        return kept + jnp.where(stays, 1, 0)

    lax.fori_loop(0, slots, kept_step, 0)

    def source_step(source, units):
        present = inverse[source * cap] >= 0
        unit = jnp.minimum(units, moving // cap - 1)

        @pl.when(present)
        def _():
            for c in range(cap):
                plan[0, moving + unit * cap + c] = inverse[source * cap + c]

        plan[0, slots + source] = jnp.where(present, unit, -1)
        return units + jnp.where(present, 1, 0)

    lax.fori_loop(0, replicas, source_step, 0)


def project_kernel(
    replicas,
    cap,
    receive,
    decay_log,
    delta_bias,
    own,
    other,
    inner_weight,
    gate_weight,
    group_weight,
    delta_weight,
    group_taps,
    group_offset,
    inner_raw,
    gate,
    delta_out,
    decay,
    shared,
    plan,
    inverse,
):
    head = lax.axis_index("head")
    half = own.shape[1]
    rows = own.shape[0]
    taps = group_taps.shape[0]
    slots = receive.shape[1]
    make_plan(replicas, cap, receive, slots, plan, inverse)
    mine = pl.ds(pl.multiple_of(head * half, half), half)
    theirs = pl.ds(pl.multiple_of((1 - head) * half, half), half)

    def columns(weight):
        return jnp.dot(own[...], weight[mine, :], preferred_element_type=F32) + jnp.dot(
            other[...], weight[theirs, :], preferred_element_type=F32
        )

    def rows_of(weight, count):
        def one(tokens, part):
            piece = weight[:, part]
            if count > 1:
                piece = jnp.broadcast_to(piece, (count, half))
            return lax.dot_general(
                tokens, piece, (((1,), (1,)), ((), ())), preferred_element_type=F32
            )

        return one(own[...], mine) + one(other[...], theirs)

    shared[:rows, :] = rounded(rows_of(group_weight, 1))
    shared[rows : rows + taps, :] = group_taps[...]
    shared[rows + taps : rows + taps + 1, :] = group_offset[...]
    shared[rows + taps + 1 :, :] = jnp.zeros_like(shared[rows + taps + 1 :, :])
    inner_raw[...] = rounded(columns(inner_weight))
    gate[...] = silu(rounded(columns(gate_weight)))
    shifted = rounded(rows_of(delta_weight, LANES)) + delta_bias[0]
    delta = jnp.maximum(shifted, 0.0) + jnp.log1p(jnp.exp(-jnp.abs(shifted)))
    slope = jnp.exp(jnp.full((1, LANES), decay_log[0], F32))
    delta_out[...] = delta
    decay[...] = jnp.exp(-delta * slope)


def project(replicas, cap, scalars, operands):
    receive = scalars[0]
    own, group_taps = operands[0], operands[-2]
    rows = own.shape[0]
    slots = receive.shape[1]
    full = jax.ShapeDtypeStruct((rows, LANES), F32)
    shared_rows = round_up(rows + group_taps.shape[0] + 1, ROWS)
    return pl.pallas_call(
        functools.partial(project_kernel, replicas, cap),
        out_shape=[full] * 4
        + [
            jax.ShapeDtypeStruct((shared_rows, group_taps.shape[1]), F32),
            jax.ShapeDtypeStruct((1, round_up(slots + replicas, LANES)), jnp.int32),
        ],
        in_specs=[SMEM] * len(scalars) + [VMEM] * len(operands),
        out_specs=[VMEM] * 5 + [SMEM],
        scratch_shapes=[pltpu.SMEM((replicas * cap + 1,), jnp.int32)],
        compiler_params=pltpu.CompilerParams(vmem_limit_bytes=MEDIUM_LIMIT),
        cost_estimate=pl.CostEstimate(
            flops=300_000_000, bytes_accessed=5_000_000, transcendentals=100_000
        ),
        name="project_tokens",
    )(*scalars, *operands)


def convolve(carried, raw, weights, offset):
    joined = carried + raw
    results = []
    for step in range(len(raw)):
        summed = offset
        for tap in range(len(carried) + 1):
            summed = summed + joined[step + tap] * weights[tap : tap + 1, :]
        results.append(rounded(silu(summed)))
    return results


def transposed(rows, scratch, stride):
    scratch[...] = jnp.zeros_like(scratch)
    for step, value in enumerate(rows):
        scratch[step * stride : step * stride + value.shape[0], :] = value
    return [scratch[first : first + LANES].T for first in range(0, scratch.shape[0], LANES)]


def advance_slot(state, rows, driven, decay, sums, maps, lanes):
    hidden = state.astype(F32)
    width = state.shape[0]
    for row, lane in zip(rows, lanes):
        piece = maps[lane // LANES]
        column = piece[:, lane % LANES : lane % LANES + 1]
        hidden = decay[row, :] * hidden + driven[row, :] * column[:width]
        sums[row, :] = jnp.sum(hidden * column[width:], axis=0, keepdims=True)
        result = hidden.astype(BF16)
        hidden = result.astype(F32)
    return result


def stay_kernel(
    replicas,
    cap,
    plan,
    live,
    skip_gain,
    inner_raw,
    gate,
    delta,
    decay,
    shared,
    shared_other,
    inner_taps,
    inner_offset,
    inner,
    group,
    group_other,
    scan,
    gated,
    group_weights,
    inner_moved,
    group_moved,
    gate_moved,
    delta_moved,
    decay_moved,
    scan_next,
    both,
    driven,
    skipped,
    sums,
    maps_in,
    ordered,
    done,
    sem,
):
    taps, slots, _ = inner.shape
    rows = inner_raw.shape[0]
    steps = rows // slots
    moving = slots // 2
    moved_rows = inner_moved.shape[0] // steps
    both[...] = both_halves(shared[...], shared_other[...])
    group_weights[...] = both[rows : rows + group_weights.shape[0], :]

    def parts(ref):
        return [ref[step * slots : (step + 1) * slots, :] for step in range(steps)]

    inner_conv = convolve(
        [inner[tap].astype(F32) for tap in range(taps)],
        parts(inner_raw),
        inner_taps[...],
        inner_offset[...],
    )
    group_conv = convolve(
        [both_halves(group[tap].astype(F32), group_other[tap].astype(F32)) for tap in range(taps)],
        parts(both),
        group_weights[: taps + 1, :],
        group_weights[taps + 1 : taps + 2, :],
    )
    for step in range(steps):
        part = slice(step * slots, (step + 1) * slots)
        driven[part, :] = delta[part, :] * inner_conv[step]
        skipped[part, :] = inner_conv[step] * skip_gain[0]
        maps_in[part, :] = group_conv[step]
    sums[...] = jnp.zeros_like(sums)
    stride = ordered.shape[0] // steps
    ordered[...] = jnp.zeros_like(ordered)
    for position in range(moving):
        slot = plan[0, position]
        for step in range(steps):
            ordered[step * stride + position : step * stride + position + 1, :] = maps_in[
                pl.ds(step * slots + slot, 1), :
            ]
    maps = [ordered[first : first + LANES].T for first in range(0, ordered.shape[0], LANES)]
    copies = []
    for position in range(moving):
        slot = plan[0, position]
        result = advance_slot(
            scan[slot],
            [pl.ds(step * slots + slot, 1) for step in range(steps)],
            driven,
            decay,
            sums,
            maps,
            [step * stride + position for step in range(steps)],
        )
        done[position] = jnp.where(slot < live[0], result, jnp.zeros_like(result))
        copies.append(
            pltpu.make_async_copy(done.at[position], scan_next.at[slot], sem.at[position])
        )
        copies[-1].start()
    gated[...] = (sums[...] + skipped[...]) * gate[...]
    pairs = (
        (inner_raw, inner_moved),
        (both, group_moved),
        (gate, gate_moved),
        (delta, delta_moved),
        (decay, decay_moved),
    )
    for _, target in pairs:
        target[...] = jnp.zeros_like(target)
    for position in range(moving):
        slot = plan[0, moving + position]
        place = position // cap * ROWS + position % cap
        for step in range(steps):
            row = step * moved_rows + place
            for source, target in pairs:
                target[row : row + 1, :] = source[pl.ds(step * slots + slot, 1), :]
    for copy in copies:
        copy.wait()


def stay(replicas, cap, scalars, operands):
    inner_raw, inner, scan = operands[0], operands[-4], operands[-1]
    _, slots, _ = inner.shape
    rows = inner_raw.shape[0]
    steps = rows // slots
    taps = operands[6].shape[0]
    moving = slots // 2
    moved_rows = moving // cap * ROWS
    full = jax.ShapeDtypeStruct((rows, LANES), F32)
    moved = jax.ShapeDtypeStruct((steps * moved_rows, LANES), F32)
    return pl.pallas_call(
        functools.partial(stay_kernel, replicas, cap),
        out_shape=[full, jax.ShapeDtypeStruct((round_up(taps + 1, ROWS), LANES), F32)]
        + [moved] * 5
        + [jax.ShapeDtypeStruct(scan.shape, BF16)],
        in_specs=[SMEM] * len(scalars) + [VMEM] * len(operands),
        out_specs=[VMEM] * 7 + [HBM],
        scratch_shapes=[
            pltpu.VMEM(operands[4].shape[:1] + (LANES,), F32),
            pltpu.VMEM((rows, LANES), F32),
            pltpu.VMEM((rows, LANES), F32),
            pltpu.VMEM((rows, LANES), F32),
            pltpu.VMEM((rows, LANES), F32),
            pltpu.VMEM((round_up(rows, LANES), LANES), F32),
            pltpu.VMEM((moving,) + scan.shape[1:], BF16),
            pltpu.SemaphoreType.DMA((moving,)),
        ],
        compiler_params=pltpu.CompilerParams(vmem_limit_bytes=SMALL_LIMIT),
        cost_estimate=pl.CostEstimate(
            flops=10_000_000, bytes_accessed=2_000_000, transcendentals=0
        ),
        name="advance_staying",
    )(*scalars, *operands)


def arrive_kernel(
    replicas,
    cap,
    plan,
    live,
    skip_gain,
    gated_in,
    group_weights,
    inner_moved,
    group_moved,
    gate_moved,
    delta_moved,
    decay_moved,
    inner_raw,
    shared,
    inner_taps,
    inner_offset,
    inner,
    group,
    scan_in,
    *refs,
):
    del scan_in
    arrived = refs[:-16]
    gated_out, inner_next, group_next, scan_next = refs[-16:-12]
    (held, driven, sums, ordered, table, gated, inner_out, group_out) = refs[-12:-4]
    done, load_sem, sem, out_sem = refs[-4:]
    shifts = shifts_of(replicas)
    taps, slots, _ = inner.shape
    moving = slots // 2
    units = moving // cap
    state_rows = scan_next.shape[1]
    moved_rows = units * ROWS
    steps = inner_raw.shape[0] // slots
    width = group.shape[2]
    me = lax.axis_index("dp")
    head = lax.axis_index("head")

    if shifts:
        sources = [
            (ref.at[0], lax.rem(me - shift + replicas, replicas))
            for ref, shift in zip(arrived, shifts)
        ]
    else:
        sources = [(arrived[0].at[source], source) for source in range(replicas)]

    def each(act):
        for ref, source in sources:
            unit = plan[0, slots + source]

            @pl.when(unit >= 0)
            def _():
                act(pltpu.make_async_copy(ref, held.at[unit], load_sem.at[unit]))

    each(lambda copy: copy.start())

    living = lax.broadcasted_iota(jnp.int32, (slots, LANES), 0) < live[0]
    for step in range(steps):
        part = slice(step * slots, (step + 1) * slots)
        tap = taps - steps + step
        inner_out[tap] = jnp.where(living, inner_raw[part, :], 0.0).astype(BF16)
        group_out[tap] = jnp.where(living[:, :width], shared[part, :], 0.0).astype(BF16)
    table[:, :LANES] = inner[steps].astype(F32)
    group_own = group[steps].astype(F32)
    table[:, LANES:] = jnp.concatenate([group_own, group_own], axis=1)
    gated[...] = gated_in[...]
    each(lambda copy: copy.wait())

    kinds = [[] for _ in range(2 * taps)]
    for unit in range(units):
        block = held[unit, cap * state_rows :, :].astype(F32)
        for kind in range(2 * taps):
            kinds[kind].append(block[kind * ROWS : (kind + 1) * ROWS])
    windows = [jnp.concatenate(kind, axis=0) for kind in kinds]

    def parts(ref):
        return [ref[step * moved_rows : (step + 1) * moved_rows, :] for step in range(steps)]

    inner_conv = convolve(
        windows[:taps], parts(inner_moved), inner_taps[...], inner_offset[...]
    )
    group_conv = convolve(
        windows[taps:],
        parts(group_moved),
        group_weights[: taps + 1, :],
        group_weights[taps + 1 : taps + 2, :],
    )
    for step, delta in enumerate(parts(delta_moved)):
        driven[step * moved_rows : (step + 1) * moved_rows, :] = delta * inner_conv[step]
    stride = ordered.shape[0] // steps
    maps = transposed(group_conv, ordered, stride)
    sums[...] = jnp.zeros_like(sums)
    copies = []
    for position in range(moving):
        unit, c = position // cap, position % cap
        place = unit * ROWS + c
        slot = plan[0, moving + position]
        result = advance_slot(
            held[unit, c * state_rows : (c + 1) * state_rows, :],
            [slice(step * moved_rows + place, step * moved_rows + place + 1) for step in range(steps)],
            driven,
            decay_moved,
            sums,
            maps,
            [step * stride + place for step in range(steps)],
        )
        done[position] = jnp.where(slot < live[0], result, jnp.zeros_like(result))
        copies.append(
            pltpu.make_async_copy(done.at[position], scan_next.at[slot], sem.at[position])
        )
        copies[-1].start()

    for step in range(steps):
        part = slice(step * moved_rows, (step + 1) * moved_rows)
        skipped = inner_conv[step] * skip_gain[0]
        sums[part, :] = (sums[part, :] + skipped) * gate_moved[part, :]
    driven[:moved_rows, :] = windows[steps]
    driven[moved_rows : 2 * moved_rows, :] = windows[taps + steps]
    for position in range(moving):
        place = position // cap * ROWS + position % cap
        slot = plan[0, moving + position]
        for step in range(steps):
            row = step * moved_rows + place
            gated[pl.ds(step * slots + slot, 1), :] = sums[row : row + 1, :]
        table[pl.ds(slot, 1), :] = jnp.concatenate(
            [driven[place : place + 1, :], driven[moved_rows + place : moved_rows + place + 1, :]],
            axis=1,
        )
    for step in range(steps):
        part = slice(step * slots, (step + 1) * slots)
        done_gated = jnp.where(living, gated[part, :], 0.0).astype(BF16)
        inner_out[taps + step] = done_gated
    inner_out[0] = jnp.where(living, table[:, :LANES], 0.0).astype(BF16)
    carried = jnp.where(head == 0, table[:, LANES : LANES + width], table[:, LANES + width :])
    group_out[0] = jnp.where(living[:, :width], carried, 0.0).astype(BF16)
    for place, (source, target) in enumerate(
        [
            (inner_out.at[pl.ds(0, taps)], inner_next),
            (inner_out.at[pl.ds(taps, steps)], gated_out),
            (group_out, group_next),
        ]
    ):
        copies.append(pltpu.make_async_copy(source, target, out_sem.at[place]))
        copies[-1].start()
    for copy in copies:
        copy.wait()


def arrive(replicas, cap, scalars, operands, scan_next, arrived):
    inner_moved, inner_raw, inner, group = operands[2], operands[7], operands[-2], operands[-1]
    taps, slots, _ = inner.shape
    rows = inner_raw.shape[0]
    steps = rows // slots
    moving = slots // 2
    units = moving // cap
    gated = jax.ShapeDtypeStruct((steps, slots, LANES), BF16)
    return pl.pallas_call(
        functools.partial(arrive_kernel, replicas, cap),
        out_shape=[
            gated,
            jax.ShapeDtypeStruct(inner.shape, BF16),
            jax.ShapeDtypeStruct(group.shape, BF16),
            jax.ShapeDtypeStruct(scan_next.shape, BF16),
        ],
        in_specs=[SMEM] * len(scalars) + [VMEM] * len(operands) + [HBM] * (1 + len(arrived)),
        out_specs=[HBM] * 4,
        scratch_shapes=[
            pltpu.VMEM((units,) + arrived[0].shape[1:], BF16),
            pltpu.VMEM(inner_moved.shape, F32),
            pltpu.VMEM(inner_moved.shape, F32),
            pltpu.VMEM((round_up(inner_moved.shape[0], LANES), LANES), F32),
            pltpu.VMEM((slots, 2 * LANES), F32),
            pltpu.VMEM((rows, LANES), F32),
            pltpu.VMEM((taps + steps, slots, LANES), BF16),
            pltpu.VMEM(group.shape, BF16),
            pltpu.VMEM((moving,) + scan_next.shape[1:], BF16),
            pltpu.SemaphoreType.DMA((units,)),
            pltpu.SemaphoreType.DMA((moving,)),
            pltpu.SemaphoreType.DMA((3,)),
        ],
        input_output_aliases={len(scalars) + len(operands): 3},
        compiler_params=pltpu.CompilerParams(vmem_limit_bytes=SMALL_LIMIT),
        cost_estimate=pl.CostEstimate(
            flops=10_000_000, bytes_accessed=2_000_000, transcendentals=0
        ),
        name="advance_arrived",
    )(*scalars, *operands, scan_next, *arrived)


def swap_heads(value):
    return lax.ppermute(value, "head", [(0, 1), (1, 0)])


def move(replicas, blocks):
    shifts = shifts_of(replicas)
    if not shifts:
        return [lax.all_to_all(blocks[0], "dp", 0, 0, tiled=True)]
    return [
        lax.ppermute(
            block, "dp", [(source, (source + shift) % replicas) for source in range(replicas)]
        )
        for shift, block in zip(shifts, blocks)
    ]


def per_device(
    replicas,
    tokens,
    inner_weight,
    gate_weight,
    group_weight,
    delta_weight,
    inner_taps,
    inner_offset,
    group_taps,
    group_offset,
    decay_log,
    delta_bias,
    skip_gain,
    inner_window,
    group_window,
    scan_state,
    send_list,
    receive_list,
    live_count,
):
    steps, slots, half = tokens.shape
    cap = send_list.shape[1] // replicas
    scan = jnp.transpose(scan_state, (0, 2, 1))
    inner = jnp.transpose(inner_window, (1, 0, 2))
    group = jnp.transpose(group_window, (1, 0, 2))
    own = tokens.reshape(steps * slots, half)

    group_other = swap_heads(group)
    arrived = move(replicas, pack(replicas, cap, send_list, scan, inner, group, group_other))
    inner_raw, gate, delta, decay, shared, plan = project(
        replicas,
        cap,
        (receive_list, decay_log, delta_bias),
        (
            own,
            swap_heads(own),
            inner_weight,
            gate_weight,
            group_weight.T,
            delta_weight.T,
            group_taps,
            group_offset[None],
        ),
    )
    scalars = (plan, live_count, skip_gain)
    *prepared, scan_next = stay(
        replicas,
        cap,
        scalars,
        (
            inner_raw,
            gate,
            delta,
            decay,
            shared,
            swap_heads(shared),
            inner_taps,
            inner_offset[None],
            inner,
            group,
            group_other,
            scan,
        ),
    )
    gated, inner_next, group_next, scan_next = arrive(
        replicas,
        cap,
        scalars,
        (*prepared, inner_raw, shared, inner_taps, inner_offset[None], inner, group),
        scan_next,
        arrived,
    )
    return (
        gated,
        jnp.transpose(inner_next, (1, 0, 2)),
        jnp.transpose(group_next, (1, 0, 2)),
        jnp.transpose(scan_next, (0, 2, 1)),
    )


def solution(mesh):
    in_specs = (
        P(None, ("grp", "dp"), "head"),
        P(None, "head"),
        P(None, "head"),
        P(None, "head"),
        P(None, "head"),
        P(None, "head"),
        P("head"),
        P(None, "head"),
        P("head"),
        P("head"),
        P("head"),
        P("head"),
        P(("grp", "dp"), None, "head"),
        P(("grp", "dp"), None, "head"),
        P(("grp", "dp"), "head", None),
        P(("grp", "dp"), None),
        P(("grp", "dp"), None),
        P(("grp", "dp")),
    )
    out_specs = (
        P(None, ("grp", "dp"), "head"),
        P(("grp", "dp"), None, "head"),
        P(("grp", "dp"), None, "head"),
        P(("grp", "dp"), "head", None),
    )
    return jax.shard_map(
        functools.partial(per_device, mesh.shape["dp"]),
        mesh=mesh,
        in_specs=in_specs,
        out_specs=out_specs,
        check_vma=False,
    )
```

time: 73.2 us -> 41.4 us (0.57)
  waiting for transfers between devices: 22.7 us -> 2.81 us
  other arithmetic: 13.1 us -> 0 us
  Pallas kernels: 0 us -> 12.3 us
  local copies, waits for them, and re-layouts: 9.68 us -> 5.23 us
  blocking collectives: 4.43 us -> 0 us
  matrix products: 2.24 us -> 0 us
    all_to_all x3 -> x0, waiting for transfers between devices: 22.7 us -> none  [the longest x1 17.5 us: per_device(): lax.all_to_all(pick_rows(scan_state, send_index, occupied), 'dp', split_a...]
    ppermute x0 -> x10, starting transfers between devices: none -> 17.1 us  [the longest x7 16.4 us: move(): lax.ppermute(block, 'dp', [(source, (source + shift) % replicas) for sour...]
    all_to_all x3 -> x0, starting transfers between devices: 16.8 us -> none  [the longest x1 7.25 us: per_device(): lax.all_to_all(pick_rows(group_window, send_index, occupied), 'dp', split...]
    pallas_call x0 -> x4, Pallas kernels: none -> 12.3 us  [the longest x1 3.37 us: pack(): pl.pallas_call(functools.partial(pack_kernel, replicas, cap), out_shape=[...]
    select_n x11 -> x0, other arithmetic: 6.77 us -> none  [the longest x1 1.97 us: per_device(): scan_next = jnp.where(living[:, None, None], scan_carry, zero)]
    gather x6 -> x0, local copies, waits for them, and re-layouts: 5.97 us -> none  [the longest x3 3.08 us: pick_rows(): member[clipped]]
    reduce_sum x4 -> x0, other arithmetic: 4.55 us -> none  [the longest x2 4.51 us: recurrence(): jnp.sum(hidden * output_map[:, None, :], axis=2)]
    all_gather x2 -> x0, blocking collectives: 4.43 us -> none  [the longest x1 2.58 us: per_device(): block_rows = lax.all_gather(token_rows, 'head', axis=1, tiled=True)]
  transfers between devices with their start and end apart: 3 -> 10, of which waited for: 2 -> 2; matrix products, arithmetic and copies ran while one was open for 16% -> 0% of each run, Pallas kernels for 0% -> 22%
where the time goes in v3:
time: 41.4 us; the launch traced here: 40.9 us
  starting transfers between devices  17.1 us (41%)
  Pallas kernels  12.3 us (30%)
  local copies, waits for them, and re-layouts  5.23 us (13%)
  between operations  3.46 us (8%)
  waiting for transfers between devices  2.81 us (7%)
    ppermute x7, starting transfers between devices, move(): lax.ppermute(block, 'dp', [(source, (source + shift) % replicas) for sour...  16.4 us
    unnamed x40, local copies, waits for them, and re-layouts  5.23 us
    pallas_call x1, Pallas kernels, pack(): pl.pallas_call(functools.partial(pack_kernel, replicas, cap), out_shape=[...  3.37 us
    pallas_call x1, Pallas kernels, arrive(): pl.pallas_call(functools.partial(arrive_kernel, replicas, cap), out_shape...  3.16 us
    pallas_call x1, Pallas kernels, project(): pl.pallas_call(functools.partial(project_kernel, replicas, cap), out_shap...  2.92 us
    pallas_call x1, Pallas kernels, stay(): pl.pallas_call(functools.partial(stay_kernel, replicas, cap), out_shape=[...  2.84 us
    ppermute x3, waiting for transfers between devices, swap_heads(): return lax.ppermute(value, 'head', [(0, 1), (1, 0)])  1.64 us
    ppermute x7, waiting for transfers between devices, move(): lax.ppermute(block, 'dp', [(source, (source + shift) % replicas) for sour...  1.17 us
  transfers between devices with their start and end apart: 10, of which 2 were waited for; matrix products, arithmetic and copies ran while one was open for 0% of the time, Pallas kernels for 22%

profile of v3, /device:TPU:0, one launch (start us, length us, event | category | flops | bytes accessed | tf_op | source)
XLA Modules:
  0.0 40.9 jit_solution(4461131281943897986)
XLA Ops:
  0.6 0.0 copy-start.1
  0.6 0.5 %collective-permute-start = (bf16[112,2048]{1,0:T(8,128)(2,1)}, bf16[112,2048]{1,0:T(8,128)(2,1)S(1)}, u32[]{:S(2)}, u32[]{:S(2)}) collective-permute-start(bf16[112,2048]{1,0:T(8,128)(2,1)} %bitcast.14), channel_id=1, source_target_pairs={{0,1},{1,0},{2,3},{3,2},{4,5},{5,4},{6,7},{7,6},{8,9},{9,8},{10,11... | collective-permute-start | bytes 1376264 | tf_op jit(solution)/shard_map/ppermute | solution.py:651
  1.2 0.1 collective-permute-start.2
  1.2 1.6 %collective-permute-done.2.group_other = bf16[3,56,64]{2,1,0:T(8,128)(2,1)S(1)} collective-permute-done((bf16[3,56,64]{2,1,0:T(8,128)(2,1)}, bf16[3,56,64]{2,1,0:T(8,128)(2,1)S(1)}, u32[]{:S(2)}, u32[]{:S(2)}) %collective-permute-start.2) | collective-permute-done | bytes 21536 | tf_op jit(solution)/shard_map/ppermute | solution.py:651
  2.9 0.6 %copy-done.7 = bf16[3,56,64]{2,1,0:T(8,128)(2,1)} copy-done((bf16[3,56,64]{2,1,0:T(8,128)(2,1)}, bf16[3,56,64]{2,1,0:T(8,128)(2,1)S(1)}, u32[]{:S(2)}) %copy-start.7) | copy-done | bytes 21528
  3.5 3.4 %pack_leaving.1 = (bf16[1,496,128]{2,1,0:T(8,128)(2,1)}, bf16[1,496,128]{2,1,0:T(8,128)(2,1)}, bf16[1,496,128]{2,1,0:T(8,128)(2,1)}, bf16[1,496,128]{2,1,0:T(8,1...) custom-call(bf16[56,64,128]{2,1,0:T(8,128)(2,1)} %bitcast.11, ...), custom_call_target="tpu_custom_call" | custom-call | bytes 2000000 | tf_op jit(solution)/shard_map/pack_leaving/pallas_call | solution.py:145
  6.9 4.0 %collective-permute-start.3 = (bf16[1,496,128]{2,1,0:T(8,128)(2,1)}, bf16[1,496,128]{2,1,0:T(8,128)(2,1)S(1)}, u32[]{:S(2)}, u32[]{:S(2)}) collective-permute-start(bf16[1,496,128]{2,1,0:T(8,128)(2,1)} %get-tuple-element.43), channel_id=1, source_target_pairs={{0,8},{2,10},{4,12},{6,14},{8,0},{10,2},{12,4},{14,6},{1,9},{3,11}... | collective-permute-start | bytes 380936 | tf_op jit(solution)/shard_map/ppermute | solution.py:659
  10.9 2.5 %collective-permute-start.4 = (bf16[1,496,128]{2,1,0:T(8,128)(2,1)}, bf16[1,496,128]{2,1,0:T(8,128)(2,1)S(1)}, u32[]{:S(2)}, u32[]{:S(2)}) collective-permute-start(bf16[1,496,128]{2,1,0:T(8,128)(2,1)} %get-tuple-element.44), channel_id=1, source_target_pairs={{0,6},{2,8},{4,10},{6,12},{8,14},{10,0},{12,2},{14,4},{1,7},{3,9},... | collective-permute-start | bytes 380936 | tf_op jit(solution)/shard_map/ppermute | solution.py:659
  14.7 0.0 collective-permute-done.other
  14.7 0.0 copy-start.11
  14.7 0.0 copy-start.13
  14.7 0.0 copy-start.14
  14.7 0.0 copy-done.1
  14.8 0.0 copy-done.9
  14.8 0.6 %copy-done.11 = f32[4,64]{1,0:T(4,128)S(1)} copy-done((f32[4,64]{1,0:T(4,128)S(1)}, f32[4,64]{1,0:T(4,128)}, u32[]{:S(2)}) %copy-start.11) | copy-done | bytes 1048
  15.4 0.0 copy-done.13
  15.4 0.0 copy-done.14
  15.4 1.2 %copy-done.2 = bf16[4096,128]{1,0:T(8,128)(2,1)S(1)} copy-done((bf16[4096,128]{1,0:T(8,128)(2,1)S(1)}, bf16[4096,128]{1,0:T(8,128)(2,1)}, u32[]{:S(2)}) %copy-start.2) | copy-done | bytes 1048600
  16.6 1.0 %copy-done.3 = bf16[4096,64]{0,1:T(8,128)(2,1)S(1)} copy-done((bf16[4096,64]{0,1:T(8,128)(2,1)S(1)}, bf16[4096,64]{0,1:T(8,128)(2,1)}, u32[]{:S(2)}) %copy-start.3) | copy-done | bytes 524312
  17.7 1.0 %copy-done.4 = bf16[2,56,2048]{2,1,0:T(8,128)(2,1)S(1)} copy-done((bf16[2,56,2048]{2,1,0:T(8,128)(2,1)S(1)}, bf16[2,56,2048]{2,1,0:T(8,128)(2,1)}, u32[]{:S(2)}) %copy-start.4) | copy-done | bytes 458776
  18.7 0.0 copy-start.15
  18.7 0.0 copy-start
  18.7 0.0 copy-start.5
  18.7 0.0 copy-start.6
  18.7 0.0 copy-start.8
  18.8 2.9 %project_tokens.1 = (f32[112,128]{1,0:T(8,128)S(1)}, f32[112,128]{1,0:T(8,128)S(1)}, f32[112,128]{1,0:T(8,128)S(1)}, f32[112,128]{1,0:T(8,128)S(1)}, f32[120,64]{1,0:T(8,128)S(1)}, /*index=5*/s32[1,128]{1,0:T(1,128)S(1)}) custom-call(s32[1,56]{1,0:T(1,128)S(1)} %copy-done.13, f32[1]{0:T(128)S(6)} %copy.24.decay_log, f32[1]{0:T(128)S(6)} %copy.25.delta_bias, ...), custom_call_target="tpu_custom_call" | custom-call | flops 300000000 | bytes 5000000 | tf_op jit(solution)/shard_map/project_tokens/pallas_call | solution.py:266
  21.7 0.1 collective-permute-start.1
  21.8 1.4 %collective-permute-start.5 = (bf16[1,496,128]{2,1,0:T(8,128)(2,1)S(1)}, bf16[1,496,128]{2,1,0:T(8,128)(2,1)S(1)}, u32[]{:S(2)}, u32[]{:S(2)}) collective-permute-start(bf16[1,496,128]{2,1,0:T(8,128)(2,1)S(1)} %copy-done.19), channel_id=1, source_target_pairs={{0,10},{2,12},{4,14},{6,0},{8,2},{10,4},{12,6},{14,8},{1,11},{3,13... | collective-permute-start | bytes 380936 | tf_op jit(solution)/shard_map/ppermute | solution.py:659
  23.1 1.6 %collective-permute-start.6 = (bf16[1,496,128]{2,1,0:T(8,128)(2,1)S(1)}, bf16[1,496,128]{2,1,0:T(8,128)(2,1)S(1)}, u32[]{:S(2)}, u32[]{:S(2)}) collective-permute-start(bf16[1,496,128]{2,1,0:T(8,128)(2,1)S(1)} %copy-done.18), channel_id=1, source_target_pairs={{0,4},{2,6},{4,8},{6,10},{8,12},{10,14},{12,0},{14,2},{1,5},{3,7},... | collective-permute-start | bytes 380936 | tf_op jit(solution)/shard_map/ppermute | solution.py:659
  24.7 0.0 collective-permute-done.3.refs_0_
  24.7 2.2 %collective-permute-start.7 = (bf16[1,496,128]{2,1,0:T(8,128)(2,1)S(1)}, bf16[1,496,128]{2,1,0:T(8,128)(2,1)S(1)}, u32[]{:S(2)}, u32[]{:S(2)}) collective-permute-start(bf16[1,496,128]{2,1,0:T(8,128)(2,1)S(1)} %copy-done.17), channel_id=1, source_target_pairs={{0,12},{2,14},{4,0},{6,2},{8,4},{10,6},{12,8},{14,10},{1,13},{3,15... | collective-permute-start | bytes 380936 | tf_op jit(solution)/shard_map/ppermute | solution.py:659
  27.0 0.0 collective-permute-done.4.refs_1_
  27.0 0.0 copy-done.16
  27.0 2.4 %collective-permute-start.8 = (bf16[1,496,128]{2,1,0:T(8,128)(2,1)S(1)}, bf16[1,496,128]{2,1,0:T(8,128)(2,1)S(1)}, u32[]{:S(2)}, u32[]{:S(2)}) collective-permute-start(bf16[1,496,128]{2,1,0:T(8,128)(2,1)S(1)} %copy-done.16), channel_id=1, source_target_pairs={{0,2},{2,4},{4,6},{6,8},{8,10},{10,12},{12,14},{14,0},{1,3},{3,5},... | collective-permute-start | bytes 380936 | tf_op jit(solution)/shard_map/ppermute | solution.py:659
  29.4 0.0 collective-permute-done.1.shared_other
  29.4 0.0 copy-done.15
  29.4 2.3 %collective-permute-start.9 = (bf16[1,496,128]{2,1,0:T(8,128)(2,1)S(1)}, bf16[1,496,128]{2,1,0:T(8,128)(2,1)S(1)}, u32[]{:S(2)}, u32[]{:S(2)}) collective-permute-start(bf16[1,496,128]{2,1,0:T(8,128)(2,1)S(1)} %copy-done.15), channel_id=1, source_target_pairs={{0,14},{2,0},{4,2},{6,4},{8,6},{10,8},{12,10},{14,12},{1,15},{3,1}... | collective-permute-start | bytes 380936 | tf_op jit(solution)/shard_map/ppermute | solution.py:659
  33.0 0.0 copy-start.10
  33.0 0.0 copy-start.12
  33.1 0.6 %copy-done.10 = f32[4,128]{1,0:T(4,128)S(1)} copy-done((f32[4,128]{1,0:T(4,128)S(1)}, f32[4,128]{1,0:T(4,128)}, u32[]{:S(2)}) %copy-start.10) | copy-done | bytes 2072
  33.7 0.0 copy-done.12
  33.7 2.8 %advance_staying.1 = (f32[112,128]{1,0:T(8,128)S(1)}, f32[8,128]{1,0:T(8,128)S(1)}, f32[64,128]{1,0:T(8,128)S(1)}, f32[64,128]{1,0:T(8,128)S(1)}, f32[64,128]{1,...) custom-call(s32[1,128]{1,0:T(1,128)S(1)} %get-tuple-element.29.plan, ...), custom_call_target="tpu_custom_call" | custom-call | flops 10000000 | bytes 2000000 | tf_op jit(solution)/shard_map/advance_staying/pallas_call | solution.py:436
  36.6 0.0 collective-permute-done.5.refs_2_
  36.6 0.0 collective-permute-done.6.refs_3_
  36.6 0.0 collective-permute-done.7.refs_4_
  36.6 1.1 %collective-permute-done.8.refs_5_ = bf16[1,496,128]{2,1,0:T(8,128)(2,1)S(1)} collective-permute-done((bf16[1,496,128]{2,1,0:T(8,128)(2,1)S(1)}, bf16[1,496,128]{2,1,0:T(8,128)(2,1)S(1)}, u32[]{:S(2)}, u32[]{:S(2)}) %collective-permute-start.8) | collective-permute-done | bytes 127008 | tf_op jit(solution)/shard_map/ppermute | solution.py:659
  37.7 0.0 collective-permute-done.9.refs_6_
  37.7 3.2 %advance_arrived.1 = (bf16[2,56,128]{2,1,0:T(8,128)(2,1)}, bf16[3,56,128]{2,1,0:T(8,128)(2,1)}, bf16[3,56,64]{2,1,0:T(8,128)(2,1)}, bf16[56,64,128]{2,1,0:T(8,128)(2,1)}) custom-call(s32[1,128]{1,0:T(1,128)S(1)} %get-tuple-element.29.plan, s32[1]{0:T(128)S(6)} %copy.27.live, f32[1]{0:T(128)S(6)} %copy.26.skip_gain, ...), custom_call_target="tpu_custom_call", output_to_operand_aliasing={{3}: (16, {})} | custom-call | flops 10000000 | bytes 2000000 | tf_op jit(solution)/shard_map/advance_arrived/pallas_call | solution.py:617
  (16 shorter events, 0.0 us)
Async XLA Ops:
  0.6 14.1 %copy-start.1 = (bf16[4096,128]{1,0:T(8,128)(2,1)S(1)}, bf16[4096,128]{1,0:T(8,128)(2,1)}, u32[]{:S(2)}) copy-start(bf16[4096,128]{1,0:T(8,128)(2,1)} %inner_weight.1) | copy-start | bytes 3145732
  0.6 14.1 %collective-permute-start = (bf16[112,2048]{1,0:T(8,128)(2,1)}, bf16[112,2048]{1,0:T(8,128)(2,1)S(1)}, u32[]{:S(2)}, u32[]{:S(2)}) collective-permute-start(bf16[112,2048]{1,0:T(8,128)(2,1)} %bitcast.14), channel_id=1, source_target_pairs={{0,1},{1,0},{2,3},{3,2},{4,5},{5,4},{6,7},{7,6},{8,9},{9,8},{10,11... | collective-permute-start | bytes 1376264 | tf_op jit(solution)/shard_map/ppermute | solution.py:651
  1.2 1.7 %collective-permute-start.2 = (bf16[3,56,64]{2,1,0:T(8,128)(2,1)}, bf16[3,56,64]{2,1,0:T(8,128)(2,1)S(1)}, u32[]{:S(2)}, u32[]{:S(2)}) collective-permute-start(bf16[3,56,64]{2,1,0:T(8,128)(2,1)} %bitcast.19), channel_id=1, source_target_pairs={{0,1},{1,0},{2,3},{3,2},{4,5},{5,4},{6,7},{7,6},{8,9},{9,8},{10,11... | collective-permute-start | bytes 64520 | tf_op jit(solution)/shard_map/ppermute | solution.py:651
  2.9 0.6 %copy-start.7 = (bf16[3,56,64]{2,1,0:T(8,128)(2,1)}, bf16[3,56,64]{2,1,0:T(8,128)(2,1)S(1)}, u32[]{:S(2)}) copy-start(bf16[3,56,64]{2,1,0:T(8,128)(2,1)S(1)} %collective-permute-done.2.group_other) | copy-start | bytes 64516
  3.5 11.3 %copy-start.9 = (bf16[4096,1]{0,1:T(2,128)(2,1)S(1)}, bf16[4096,1]{0,1:T(2,128)(2,1)}, u32[]{:S(2)}) copy-start(bf16[4096,1]{0,1:T(2,128)(2,1)} %param.22) | copy-start | bytes 24580
  6.9 17.9 %collective-permute-start.3 = (bf16[1,496,128]{2,1,0:T(8,128)(2,1)}, bf16[1,496,128]{2,1,0:T(8,128)(2,1)S(1)}, u32[]{:S(2)}, u32[]{:S(2)}) collective-permute-start(bf16[1,496,128]{2,1,0:T(8,128)(2,1)} %get-tuple-element.43), channel_id=1, source_target_pairs={{0,8},{2,10},{4,12},{6,14},{8,0},{10,2},{12,4},{14,6},{1,9},{3,11}... | collective-permute-start | bytes 380936 | tf_op jit(solution)/shard_map/ppermute | solution.py:659
  10.9 16.1 %collective-permute-start.4 = (bf16[1,496,128]{2,1,0:T(8,128)(2,1)}, bf16[1,496,128]{2,1,0:T(8,128)(2,1)S(1)}, u32[]{:S(2)}, u32[]{:S(2)}) collective-permute-start(bf16[1,496,128]{2,1,0:T(8,128)(2,1)} %get-tuple-element.44), channel_id=1, source_target_pairs={{0,6},{2,8},{4,10},{6,12},{8,14},{10,0},{12,2},{14,4},{1,7},{3,9},... | collective-permute-start | bytes 380936 | tf_op jit(solution)/shard_map/ppermute | solution.py:659
  14.7 0.7 %copy-start.11 = (f32[4,64]{1,0:T(4,128)S(1)}, f32[4,64]{1,0:T(4,128)}, u32[]{:S(2)}) copy-start(f32[4,64]{1,0:T(4,128)} %group_taps.1) | copy-start | bytes 3076
  14.7 0.7 %copy-start.13 = (s32[1,56]{1,0:T(1,128)S(1)}, s32[1,56]{1,0:T(1,128)}, u32[]{:S(2)}) copy-start(s32[1,56]{1,0:T(1,128)} %receive.1) | copy-start | bytes 676
  14.7 0.7 %copy-start.14 = (f32[64]{0:T(128)S(1)}, f32[64]{0:T(128)}, u32[]{:S(2)}) copy-start(f32[64]{0:T(128)} %param.26) | copy-start | bytes 772
  15.4 1.2 %copy-start.2 = (bf16[4096,128]{1,0:T(8,128)(2,1)S(1)}, bf16[4096,128]{1,0:T(8,128)(2,1)}, u32[]{:S(2)}) copy-start(bf16[4096,128]{1,0:T(8,128)(2,1)} %gate_weight.1) | copy-start | bytes 3145732
  16.6 1.0 %copy-start.3 = (bf16[4096,64]{0,1:T(8,128)(2,1)S(1)}, bf16[4096,64]{0,1:T(8,128)(2,1)}, u32[]{:S(2)}) copy-start(bf16[4096,64]{0,1:T(8,128)(2,1)} %param.21) | copy-start | bytes 1572868
  17.7 1.0 %copy-start.4 = (bf16[2,56,2048]{2,1,0:T(8,128)(2,1)S(1)}, bf16[2,56,2048]{2,1,0:T(8,128)(2,1)}, u32[]{:S(2)}) copy-start(bf16[2,56,2048]{2,1,0:T(8,128)(2,1)} %param.18) | copy-start | bytes 1376260
  18.7 3.1 %copy-start.19 = (bf16[1,496,128]{2,1,0:T(8,128)(2,1)S(1)}, bf16[1,496,128]{2,1,0:T(8,128)(2,1)}, u32[]{:S(2)}) copy-start(bf16[1,496,128]{2,1,0:T(8,128)(2,1)} %get-tuple-element.45) | copy-start | bytes 380932
  18.7 4.5 %copy-start.18 = (bf16[1,496,128]{2,1,0:T(8,128)(2,1)S(1)}, bf16[1,496,128]{2,1,0:T(8,128)(2,1)}, u32[]{:S(2)}) copy-start(bf16[1,496,128]{2,1,0:T(8,128)(2,1)} %get-tuple-element.46) | copy-start | bytes 380932
  18.7 6.0 %copy-start.17 = (bf16[1,496,128]{2,1,0:T(8,128)(2,1)S(1)}, bf16[1,496,128]{2,1,0:T(8,128)(2,1)}, u32[]{:S(2)}) copy-start(bf16[1,496,128]{2,1,0:T(8,128)(2,1)} %get-tuple-element.47) | copy-start | bytes 380932
  18.7 8.3 %copy-start.16 = (bf16[1,496,128]{2,1,0:T(8,128)(2,1)S(1)}, bf16[1,496,128]{2,1,0:T(8,128)(2,1)}, u32[]{:S(2)}) copy-start(bf16[1,496,128]{2,1,0:T(8,128)(2,1)} %get-tuple-element.48) | copy-start | bytes 380932
  18.7 10.7 %copy-start.15 = (bf16[1,496,128]{2,1,0:T(8,128)(2,1)S(1)}, bf16[1,496,128]{2,1,0:T(8,128)(2,1)}, u32[]{:S(2)}) copy-start(bf16[1,496,128]{2,1,0:T(8,128)(2,1)} %get-tuple-element.49) | copy-start | bytes 380932
  18.7 14.3 %copy-start = (bf16[56,128,64]{1,2,0:T(8,128)(2,1)S(1)}, bf16[56,128,64]{1,2,0:T(8,128)(2,1)}, u32[]{:S(2)}) copy-start(bf16[56,128,64]{1,2,0:T(8,128)(2,1)} %param.32) | copy-start | bytes 2752516
  18.7 14.3 %copy-start.5 = (bf16[56,3,128]{2,0,1:T(8,128)(2,1)S(1)}, bf16[56,3,128]{2,0,1:T(8,128)(2,1)}, u32[]{:S(2)}) copy-start(bf16[56,3,128]{2,0,1:T(8,128)(2,1)} %param.30) | copy-start | bytes 129028
  18.7 14.3 %copy-start.6 = (bf16[56,3,64]{2,0,1:T(8,128)(2,1)S(1)}, bf16[56,3,64]{2,0,1:T(8,128)(2,1)}, u32[]{:S(2)}) copy-start(bf16[56,3,64]{2,0,1:T(8,128)(2,1)} %param.31) | copy-start | bytes 64516
  18.7 14.3 %copy-start.8 = (bf16[3,56,64]{2,1,0:T(8,128)(2,1)S(1)}, bf16[3,56,64]{2,1,0:T(8,128)(2,1)}, u32[]{:S(2)}) copy-start(bf16[3,56,64]{2,1,0:T(8,128)(2,1)} %copy-done.7) | copy-start | bytes 64516
  21.7 7.7 %collective-permute-start.1 = (f32[120,64]{1,0:T(8,128)S(1)}, f32[120,64]{1,0:T(8,128)S(1)}, u32[]{:S(2)}, u32[]{:S(2)}) collective-permute-start(f32[120,64]{1,0:T(8,128)S(1)} %get-tuple-element.34.shared), channel_id=1, source_target_pairs={{0,1},{1,0},{2,3},{3,2},{4,5},{5,4},{6,7},{7,6},{8,9},{9,8},{10,11... | collective-permute-start | bytes 92168 | tf_op jit(solution)/shard_map/ppermute | solution.py:651
  21.8 14.8 %collective-permute-start.5 = (bf16[1,496,128]{2,1,0:T(8,128)(2,1)S(1)}, bf16[1,496,128]{2,1,0:T(8,128)(2,1)S(1)}, u32[]{:S(2)}, u32[]{:S(2)}) collective-permute-start(bf16[1,496,128]{2,1,0:T(8,128)(2,1)S(1)} %copy-done.19), channel_id=1, source_target_pairs={{0,10},{2,12},{4,14},{6,0},{8,2},{10,4},{12,6},{14,8},{1,11},{3,13... | collective-permute-start | bytes 380936 | tf_op jit(solution)/shard_map/ppermute | solution.py:659
  23.1 13.4 %collective-permute-start.6 = (bf16[1,496,128]{2,1,0:T(8,128)(2,1)S(1)}, bf16[1,496,128]{2,1,0:T(8,128)(2,1)S(1)}, u32[]{:S(2)}, u32[]{:S(2)}) collective-permute-start(bf16[1,496,128]{2,1,0:T(8,128)(2,1)S(1)} %copy-done.18), channel_id=1, source_target_pairs={{0,4},{2,6},{4,8},{6,10},{8,12},{10,14},{12,0},{14,2},{1,5},{3,7},... | collective-permute-start | bytes 380936 | tf_op jit(solution)/shard_map/ppermute | solution.py:659
  24.7 11.8 %collective-permute-start.7 = (bf16[1,496,128]{2,1,0:T(8,128)(2,1)S(1)}, bf16[1,496,128]{2,1,0:T(8,128)(2,1)S(1)}, u32[]{:S(2)}, u32[]{:S(2)}) collective-permute-start(bf16[1,496,128]{2,1,0:T(8,128)(2,1)S(1)} %copy-done.17), channel_id=1, source_target_pairs={{0,12},{2,14},{4,0},{6,2},{8,4},{10,6},{12,8},{14,10},{1,13},{3,15... | collective-permute-start | bytes 380936 | tf_op jit(solution)/shard_map/ppermute | solution.py:659
  27.0 10.8 %collective-permute-start.8 = (bf16[1,496,128]{2,1,0:T(8,128)(2,1)S(1)}, bf16[1,496,128]{2,1,0:T(8,128)(2,1)S(1)}, u32[]{:S(2)}, u32[]{:S(2)}) collective-permute-start(bf16[1,496,128]{2,1,0:T(8,128)(2,1)S(1)} %copy-done.16), channel_id=1, source_target_pairs={{0,2},{2,4},{4,6},{6,8},{8,10},{10,12},{12,14},{14,0},{1,3},{3,5},... | collective-permute-start | bytes 380936 | tf_op jit(solution)/shard_map/ppermute | solution.py:659
  29.4 8.4 %collective-permute-start.9 = (bf16[1,496,128]{2,1,0:T(8,128)(2,1)S(1)}, bf16[1,496,128]{2,1,0:T(8,128)(2,1)S(1)}, u32[]{:S(2)}, u32[]{:S(2)}) collective-permute-start(bf16[1,496,128]{2,1,0:T(8,128)(2,1)S(1)} %copy-done.15), channel_id=1, source_target_pairs={{0,14},{2,0},{4,2},{6,4},{8,6},{10,8},{12,10},{14,12},{1,15},{3,1}... | collective-permute-start | bytes 380936 | tf_op jit(solution)/shard_map/ppermute | solution.py:659
  33.0 0.7 %copy-start.10 = (f32[4,128]{1,0:T(4,128)S(1)}, f32[4,128]{1,0:T(4,128)}, u32[]{:S(2)}) copy-start(f32[4,128]{1,0:T(4,128)} %inner_taps.3) | copy-start | bytes 6148
  33.0 0.7 %copy-start.12 = (f32[128]{0:T(128)S(1)}, f32[128]{0:T(128)}, u32[]{:S(2)}) copy-start(f32[128]{0:T(128)} %param.24) | copy-start | bytes 1540

commit v4 on v3

--- a/solution.py
+++ b/solution.py
@@ -13,8 +13,10 @@
 MEDIUM_LIMIT = 32 * 1024 * 1024
 LARGE_LIMIT = 60 * 1024 * 1024
 MAX_SHIFTS = 16
+WINDOWS_LIMIT = 8 * 1024 * 1024
 LANES = 128
 ROWS = 8
+EARLIER = 2
 
 VMEM = pl.BlockSpec(memory_space=pltpu.VMEM)
 SMEM = pl.BlockSpec(memory_space=pltpu.SMEM)
@@ -46,12 +48,63 @@
     )
 
 
-def pack_kernel(replicas, cap, scan, send, inner, group, group_other, *refs):
+def destinations(replicas, outs):
     shifts = shifts_of(replicas)
-    count = max(1, len(shifts))
+    me = lax.axis_index("dp")
+    if shifts:
+        return [
+            (ref.at[0], lax.rem(me + shift, replicas)) for ref, shift in zip(outs, shifts)
+        ]
+    return [(outs[0].at[target], target) for target in range(replicas)]
+
+
+def states_kernel(replicas, cap, scan, send, *refs):
+    count = max(1, len(shifts_of(replicas)))
     outs = refs[:count]
-    (indices, inner_in, mine_in, theirs_in, held, table, picked, cast) = refs[count : count + 8]
-    load_sem, in_sem, out_sem, window_sem = refs[count + 8 :]
+    indices, held, load_sem, in_sem, out_sem = refs[count:]
+    load = pltpu.make_async_copy(send, indices, load_sem)
+    load.start()
+    blocks = destinations(replicas, outs)
+    state_rows = scan.shape[1]
+    load.wait()
+    plan = []
+    for ref, target in blocks:
+        for c in range(cap):
+            plan.append((ref, c, indices[0, target * cap + c]))
+
+    def fetch(place, index):
+        return pltpu.make_async_copy(scan.at[index], held.at[place], in_sem.at[place])
+
+    def store(place, ref, c):
+        return pltpu.make_async_copy(
+            held.at[place], ref.at[pl.ds(c * state_rows, state_rows)], out_sem.at[place]
+        )
+
+    for place, (_, _, index) in enumerate(plan):
+
+        @pl.when(index >= 0)
+        def _():
+            fetch(place, index).start()
+
+    for place, (ref, c, index) in enumerate(plan):
+
+        @pl.when(index >= 0)
+        def _():
+            fetch(place, index).wait()
+            store(place, ref, c).start()
+
+    for place, (ref, c, index) in enumerate(plan):
+
+        @pl.when(index >= 0)
+        def _():
+            store(place, ref, c).wait()
+
+
+def windows_kernel(replicas, cap, state_rows, send, inner, group, group_other, *refs):
+    count = max(1, len(shifts_of(replicas)))
+    outs = refs[-9 - count : -9]
+    indices, inner_in, mine_in, theirs_in, table, picked, cast = refs[-9:-2]
+    load_sem, window_sem = refs[-2:]
     loads = [
         pltpu.make_async_copy(source, target, load_sem.at[place])
         for place, (source, target) in enumerate(
@@ -60,52 +113,24 @@
     ]
     for load in loads:
         load.start()
-    me = lax.axis_index("dp")
-    taps, _, channels = inner_in.shape
-    state_rows = scan.shape[1]
-    blocks = []
-    if shifts:
-        for ref, shift in zip(outs, shifts):
-            blocks.append((ref.at[0], lax.rem(me + shift, replicas)))
-    else:
-        blocks = [(outs[0].at[target], target) for target in range(replicas)]
-    loads[0].wait()
-
-    plan = []
-    for block, (ref, target) in enumerate(blocks):
-        for c in range(cap):
-            plan.append((block, ref, c, indices[0, target * cap + c]))
-
-    def fetch(place, index):
-        return pltpu.make_async_copy(scan.at[index], held.at[place], in_sem.at[place])
-
-    def store(place, ref, c):
-        return pltpu.make_async_copy(
-            held.at[place], ref.at[pl.ds(c * state_rows, state_rows)], out_sem.at[place]
-        )
-
-    for place, (_, _, _, index) in enumerate(plan):
-
-        @pl.when(index >= 0)
-        def _():
-            fetch(place, index).start()
-
-    for load in loads[1:]:
+    for load in loads:
         load.wait()
+    taps = inner_in.shape[0]
     for tap in range(taps):
         table[:, tap * LANES : (tap + 1) * LANES] = inner_in[tap].astype(F32)
         table[:, (taps + tap) * LANES : (taps + tap + 1) * LANES] = both_halves(
             mine_in[tap].astype(F32), theirs_in[tap].astype(F32)
         )
-    picked[...] = jnp.zeros_like(picked)
-    for place, (block, _, c, index) in enumerate(plan):
-        row = table[pl.ds(jnp.maximum(index, 0), 1), :]
-        for kind in range(2 * taps):
-            picked[block, kind * ROWS + c : kind * ROWS + c + 1, :] = row[
-                :, kind * LANES : (kind + 1) * LANES
-            ]
     windows = []
-    for block, (ref, _) in enumerate(blocks):
+    for block, (ref, target) in enumerate(destinations(replicas, outs)):
+        picked[block] = jnp.zeros(picked.shape[1:], F32)
+        for c in range(cap):
+            index = indices[0, target * cap + c]
+            row = table[pl.ds(jnp.maximum(index, 0), 1), :]
+            for kind in range(2 * taps):
+                picked[block, kind * ROWS + c : kind * ROWS + c + 1, :] = row[
+                    :, kind * LANES : (kind + 1) * LANES
+                ]
         cast[block] = picked[block].astype(BF16)
         windows.append(
             pltpu.make_async_copy(
@@ -115,25 +140,11 @@
             )
         )
         windows[-1].start()
-
-    for place, (_, ref, c, index) in enumerate(plan):
-
-        @pl.when(index >= 0)
-        def _():
-            fetch(place, index).wait()
-            store(place, ref, c).start()
-
-    for place, (_, ref, c, index) in enumerate(plan):
-
-        @pl.when(index >= 0)
-        def _():
-            store(place, ref, c).wait()
-
     for window in windows:
         window.wait()
 
 
-def pack(replicas, cap, send_list, scan, inner, group, group_other):
+def pack(replicas, cap, send_list, scan, inner, group, group_other, swapped):
     shifts = shifts_of(replicas)
     count = max(1, len(shifts))
     per_block = 1 if shifts else replicas
@@ -142,29 +153,44 @@
     rows = cap * scan.shape[1] + window_rows
     blocks = count * per_block
     places = blocks * cap
+    shapes = [jax.ShapeDtypeStruct((per_block, rows, LANES), BF16)] * count
+    states = pl.pallas_call(
+        functools.partial(states_kernel, replicas, cap),
+        out_shape=shapes,
+        in_specs=[HBM] * 2,
+        out_specs=[HBM] * count,
+        scratch_shapes=[
+            pltpu.SMEM(send_list.shape, jnp.int32),
+            pltpu.VMEM((places,) + scan.shape[1:], BF16),
+            pltpu.SemaphoreType.DMA,
+            pltpu.SemaphoreType.DMA((places,)),
+            pltpu.SemaphoreType.DMA((places,)),
+        ],
+        compiler_params=pltpu.CompilerParams(vmem_limit_bytes=LARGE_LIMIT),
+        cost_estimate=pl.CostEstimate(flops=0, bytes_accessed=2_000_000, transcendentals=0),
+        name="pack_states",
+    )(scan, send_list)
     return pl.pallas_call(
-        functools.partial(pack_kernel, replicas, cap),
-        out_shape=[jax.ShapeDtypeStruct((per_block, rows, LANES), BF16)] * count,
-        in_specs=[HBM] * 5,
+        functools.partial(windows_kernel, replicas, cap, scan.shape[1]),
+        out_shape=shapes,
+        in_specs=[HBM] * (4 + count + len(swapped)),
         out_specs=[HBM] * count,
         scratch_shapes=[
             pltpu.SMEM(send_list.shape, jnp.int32),
             pltpu.VMEM(inner.shape, BF16),
             pltpu.VMEM(group.shape, BF16),
             pltpu.VMEM(group.shape, BF16),
-            pltpu.VMEM((places,) + scan.shape[1:], BF16),
             pltpu.VMEM((slots, 2 * taps * LANES), F32),
             pltpu.VMEM((blocks, window_rows, LANES), F32),
             pltpu.VMEM((blocks, window_rows, LANES), BF16),
             pltpu.SemaphoreType.DMA((4,)),
-            pltpu.SemaphoreType.DMA((places,)),
-            pltpu.SemaphoreType.DMA((places,)),
             pltpu.SemaphoreType.DMA((blocks,)),
         ],
-        compiler_params=pltpu.CompilerParams(vmem_limit_bytes=LARGE_LIMIT),
-        cost_estimate=pl.CostEstimate(flops=0, bytes_accessed=2_000_000, transcendentals=0),
-        name="pack_leaving",
-    )(scan, send_list, inner, group, group_other)
+        input_output_aliases={4 + block: block for block in range(count)},
+        compiler_params=pltpu.CompilerParams(vmem_limit_bytes=WINDOWS_LIMIT),
+        cost_estimate=pl.CostEstimate(flops=0, bytes_accessed=500_000, transcendentals=0),
+        name="pack_windows",
+    )(send_list, inner, group, group_other, *states, *swapped)
 
 
 def make_plan(replicas, cap, receive, slots, plan, inverse):
@@ -194,91 +220,6 @@
         return units + jnp.where(present, 1, 0)
 
     lax.fori_loop(0, replicas, source_step, 0)
-
-
-def project_kernel(
-    replicas,
-    cap,
-    receive,
-    decay_log,
-    delta_bias,
-    own,
-    other,
-    inner_weight,
-    gate_weight,
-    group_weight,
-    delta_weight,
-    group_taps,
-    group_offset,
-    inner_raw,
-    gate,
-    delta_out,
-    decay,
-    shared,
-    plan,
-    inverse,
-):
-    head = lax.axis_index("head")
-    half = own.shape[1]
-    rows = own.shape[0]
-    taps = group_taps.shape[0]
-    slots = receive.shape[1]
-    make_plan(replicas, cap, receive, slots, plan, inverse)
-    mine = pl.ds(pl.multiple_of(head * half, half), half)
-    theirs = pl.ds(pl.multiple_of((1 - head) * half, half), half)
-
-    def columns(weight):
-        return jnp.dot(own[...], weight[mine, :], preferred_element_type=F32) + jnp.dot(
-            other[...], weight[theirs, :], preferred_element_type=F32
-        )
-
-    def rows_of(weight, count):
-        def one(tokens, part):
-            piece = weight[:, part]
-            if count > 1:
-                piece = jnp.broadcast_to(piece, (count, half))
-            return lax.dot_general(
-                tokens, piece, (((1,), (1,)), ((), ())), preferred_element_type=F32
-            )
-
-        return one(own[...], mine) + one(other[...], theirs)
-
-    shared[:rows, :] = rounded(rows_of(group_weight, 1))
-    shared[rows : rows + taps, :] = group_taps[...]
-    shared[rows + taps : rows + taps + 1, :] = group_offset[...]
-    shared[rows + taps + 1 :, :] = jnp.zeros_like(shared[rows + taps + 1 :, :])
-    inner_raw[...] = rounded(columns(inner_weight))
-    gate[...] = silu(rounded(columns(gate_weight)))
-    shifted = rounded(rows_of(delta_weight, LANES)) + delta_bias[0]
-    delta = jnp.maximum(shifted, 0.0) + jnp.log1p(jnp.exp(-jnp.abs(shifted)))
-    slope = jnp.exp(jnp.full((1, LANES), decay_log[0], F32))
-    delta_out[...] = delta
-    decay[...] = jnp.exp(-delta * slope)
-
-
-def project(replicas, cap, scalars, operands):
-    receive = scalars[0]
-    own, group_taps = operands[0], operands[-2]
-    rows = own.shape[0]
-    slots = receive.shape[1]
-    full = jax.ShapeDtypeStruct((rows, LANES), F32)
-    shared_rows = round_up(rows + group_taps.shape[0] + 1, ROWS)
-    return pl.pallas_call(
-        functools.partial(project_kernel, replicas, cap),
-        out_shape=[full] * 4
-        + [
-            jax.ShapeDtypeStruct((shared_rows, group_taps.shape[1]), F32),
-            jax.ShapeDtypeStruct((1, round_up(slots + replicas, LANES)), jnp.int32),
-        ],
-        in_specs=[SMEM] * len(scalars) + [VMEM] * len(operands),
-        out_specs=[VMEM] * 5 + [SMEM],
-        scratch_shapes=[pltpu.SMEM((replicas * cap + 1,), jnp.int32)],
-        compiler_params=pltpu.CompilerParams(vmem_limit_bytes=MEDIUM_LIMIT),
-        cost_estimate=pl.CostEstimate(
-            flops=300_000_000, bytes_accessed=5_000_000, transcendentals=100_000
-        ),
-        name="project_tokens",
-    )(*scalars, *operands)
 
 
 def convolve(carried, raw, weights, offset):
@@ -315,45 +256,86 @@
 def stay_kernel(
     replicas,
     cap,
-    plan,
+    receive,
     live,
+    decay_log,
+    delta_bias,
     skip_gain,
-    inner_raw,
-    gate,
-    delta,
-    decay,
-    shared,
-    shared_other,
+    own,
+    other,
+    inner_weight,
+    gate_weight,
+    group_weight,
+    group_weight_other,
+    delta_weight,
     inner_taps,
     inner_offset,
+    group_taps,
+    group_taps_other,
     inner,
     group,
     group_other,
     scan,
-    gated,
-    group_weights,
-    inner_moved,
-    group_moved,
-    gate_moved,
-    delta_moved,
-    decay_moved,
-    scan_next,
-    both,
-    driven,
-    skipped,
-    sums,
-    maps_in,
-    ordered,
-    done,
-    sem,
+    *refs,
 ):
+    (
+        plan,
+        gated,
+        group_weights,
+        inner_raw,
+        both,
+        inner_moved,
+        group_moved,
+        gate_moved,
+        delta_moved,
+        decay_moved,
+        scan_next,
+        inverse,
+        gate,
+        delta,
+        decay,
+        driven,
+        skipped,
+        sums,
+        maps_in,
+        ordered,
+        done,
+        sem,
+    ) = refs[-22:]
     taps, slots, _ = inner.shape
-    rows = inner_raw.shape[0]
+    rows, half = own.shape
     steps = rows // slots
     moving = slots // 2
     moved_rows = inner_moved.shape[0] // steps
-    both[...] = both_halves(shared[...], shared_other[...])
-    group_weights[...] = both[rows : rows + group_weights.shape[0], :]
+    head = lax.axis_index("head")
+    make_plan(replicas, cap, receive, slots, plan, inverse)
+    mine = pl.ds(pl.multiple_of(head * half, half), half)
+    theirs = pl.ds(pl.multiple_of((1 - head) * half, half), half)
+
+    def columns(weight):
+        return jnp.dot(own[...], weight[mine, :], preferred_element_type=F32) + jnp.dot(
+            other[...], weight[theirs, :], preferred_element_type=F32
+        )
+
+    def rows_of(weight, count):
+        def one(tokens, part):
+            piece = weight[:, part]
+            if count > 1:
+                piece = jnp.broadcast_to(piece, (count, half))
+            return lax.dot_general(
+                tokens, piece, (((1,), (1,)), ((), ())), preferred_element_type=F32
+            )
+
+        return one(own[...], mine) + one(other[...], theirs)
+
+    both[...] = rounded(both_halves(rows_of(group_weight, 1), rows_of(group_weight_other, 1)))
+    inner_raw[...] = rounded(columns(inner_weight))
+    gate[...] = silu(rounded(columns(gate_weight)))
+    shifted = rounded(rows_of(delta_weight, LANES)) + delta_bias[0]
+    rate = jnp.maximum(shifted, 0.0) + jnp.log1p(jnp.exp(-jnp.abs(shifted)))
+    delta[...] = rate
+    decay[...] = jnp.exp(-rate * jnp.exp(jnp.full((1, LANES), decay_log[0], F32)))
+    group_weights[: taps + 2, :] = both_halves(group_taps[...], group_taps_other[...])
 
     def parts(ref):
         return [ref[step * slots : (step + 1) * slots, :] for step in range(steps)]
@@ -423,39 +405,41 @@
         copy.wait()
 
 
-def stay(replicas, cap, scalars, operands):
-    inner_raw, inner, scan = operands[0], operands[-4], operands[-1]
-    _, slots, _ = inner.shape
-    rows = inner_raw.shape[0]
+def stay(replicas, cap, scalars, operands, earlier):
+    own, inner, scan = operands[0], operands[-4], operands[-1]
+    taps, slots, _ = inner.shape
+    rows = own.shape[0]
     steps = rows // slots
-    taps = operands[6].shape[0]
     moving = slots // 2
     moved_rows = moving // cap * ROWS
     full = jax.ShapeDtypeStruct((rows, LANES), F32)
     moved = jax.ShapeDtypeStruct((steps * moved_rows, LANES), F32)
     return pl.pallas_call(
         functools.partial(stay_kernel, replicas, cap),
-        out_shape=[full, jax.ShapeDtypeStruct((round_up(taps + 1, ROWS), LANES), F32)]
+        out_shape=[
+            jax.ShapeDtypeStruct((1, round_up(slots + replicas, LANES)), jnp.int32),
+            full,
+            jax.ShapeDtypeStruct((round_up(taps + 2, ROWS), LANES), F32),
+            full,
+            full,
+        ]
         + [moved] * 5
         + [jax.ShapeDtypeStruct(scan.shape, BF16)],
-        in_specs=[SMEM] * len(scalars) + [VMEM] * len(operands),
-        out_specs=[VMEM] * 7 + [HBM],
-        scratch_shapes=[
-            pltpu.VMEM(operands[4].shape[:1] + (LANES,), F32),
-            pltpu.VMEM((rows, LANES), F32),
-            pltpu.VMEM((rows, LANES), F32),
-            pltpu.VMEM((rows, LANES), F32),
-            pltpu.VMEM((rows, LANES), F32),
+        in_specs=[SMEM] * len(scalars) + [VMEM] * len(operands) + [HBM] * len(earlier),
+        out_specs=[SMEM] + [VMEM] * 9 + [HBM],
+        scratch_shapes=[pltpu.SMEM((replicas * cap + 1,), jnp.int32)]
+        + [pltpu.VMEM((rows, LANES), F32)] * 7
+        + [
             pltpu.VMEM((round_up(rows, LANES), LANES), F32),
             pltpu.VMEM((moving,) + scan.shape[1:], BF16),
             pltpu.SemaphoreType.DMA((moving,)),
         ],
-        compiler_params=pltpu.CompilerParams(vmem_limit_bytes=SMALL_LIMIT),
+        compiler_params=pltpu.CompilerParams(vmem_limit_bytes=MEDIUM_LIMIT),
         cost_estimate=pl.CostEstimate(
-            flops=10_000_000, bytes_accessed=2_000_000, transcendentals=0
+            flops=300_000_000, bytes_accessed=6_000_000, transcendentals=100_000
         ),
         name="advance_staying",
-    )(*scalars, *operands)
+    )(*scalars, *operands, *earlier)
 
 
 def arrive_kernel(
@@ -472,7 +456,7 @@
     delta_moved,
     decay_moved,
     inner_raw,
-    shared,
+    both,
     inner_taps,
     inner_offset,
     inner,
@@ -519,7 +503,8 @@
         part = slice(step * slots, (step + 1) * slots)
         tap = taps - steps + step
         inner_out[tap] = jnp.where(living, inner_raw[part, :], 0.0).astype(BF16)
-        group_out[tap] = jnp.where(living[:, :width], shared[part, :], 0.0).astype(BF16)
+        raw = jnp.where(head == 0, both[part, :width], both[part, width:])
+        group_out[tap] = jnp.where(living[:, :width], raw, 0.0).astype(BF16)
     table[:, :LANES] = inner[steps].astype(F32)
     group_own = group[steps].astype(F32)
     table[:, LANES:] = jnp.concatenate([group_own, group_own], axis=1)
@@ -691,48 +676,41 @@
     group = jnp.transpose(group_window, (1, 0, 2))
     own = tokens.reshape(steps * slots, half)
 
+    group_weight = group_weight.T
+    inner_offset = inner_offset[None]
+    group_taps = jnp.concatenate([group_taps, group_offset[None]], axis=0)
     group_other = swap_heads(group)
-    arrived = move(replicas, pack(replicas, cap, send_list, scan, inner, group, group_other))
-    inner_raw, gate, delta, decay, shared, plan = project(
+    swapped = [swap_heads(value) for value in (own, group_weight, group_taps)]
+    blocks = pack(replicas, cap, send_list, scan, inner, group, group_other, swapped)
+    arrived = move(replicas, blocks)
+    plan, gated, group_weights, inner_raw, both, *moved, scan_next = stay(
         replicas,
         cap,
-        (receive_list, decay_log, delta_bias),
+        (receive_list, live_count, decay_log, delta_bias, skip_gain),
         (
             own,
-            swap_heads(own),
+            swapped[0],
             inner_weight,
             gate_weight,
-            group_weight.T,
+            group_weight,
+            swapped[1],
             delta_weight.T,
+            inner_taps,
+            inner_offset,
             group_taps,
-            group_offset[None],
-        ),
-    )
-    scalars = (plan, live_count, skip_gain)
-    *prepared, scan_next = stay(
-        replicas,
-        cap,
-        scalars,
-        (
-            inner_raw,
-            gate,
-            delta,
-            decay,
-            shared,
-            swap_heads(shared),
-            inner_taps,
-            inner_offset[None],
+            swapped[2],
             inner,
             group,
             group_other,
             scan,
         ),
+        arrived[:EARLIER],
     )
     gated, inner_next, group_next, scan_next = arrive(
         replicas,
         cap,
-        scalars,
-        (*prepared, inner_raw, shared, inner_taps, inner_offset[None], inner, group),
+        (plan, live_count, skip_gain),
+        (gated, group_weights, *moved, inner_raw, both, inner_taps, inner_offset, inner, group),
         scan_next,
         arrived,
     )

time: 41.4 us -> 50.6 us (1.22)
  waiting for transfers between devices: 2.81 us -> 8.76 us
  local copies, waits for them, and re-layouts: 5.23 us -> 7.83 us
  Pallas kernels: 12.3 us -> 13.5 us
  starting transfers between devices: 17.1 us -> 16.5 us
    ppermute x7, waiting for transfers between devices: 1.17 us -> 8.75 us  [move(): lax.ppermute(block, 'dp', [(source, (source + shift) % replicas) for sour...]
    unnamed x40 -> x36, local copies, waits for them, and re-layouts: 5.23 us -> 7.83 us
    pallas_call x1, Pallas kernels: 2.84 us -> 5.43 us  [stay(): pl.pallas_call(functools.partial(stay_kernel, replicas, cap), out_shape=[...]
    ppermute x3 -> x4, waiting for transfers between devices: 1.64 us -> 0.01 us  [swap_heads(): return lax.ppermute(value, 'head', [(0, 1), (1, 0)])]
    pallas_call x2, Pallas kernels: 6.29 us -> 4.84 us  [the longest x1 3.29 us: pack(): pl.pallas_call(functools.partial(states_kernel, replicas, cap), out_shape...]
    ppermute x7, starting transfers between devices: 16.4 us -> 15 us  [move(): lax.ppermute(block, 'dp', [(source, (source + shift) % replicas) for sour...]
    ppermute x3 -> x4, starting transfers between devices: 0.67 us -> 1.45 us  [swap_heads(): return lax.ppermute(value, 'head', [(0, 1), (1, 0)])]
  transfers between devices with their start and end apart: 10 -> 11, of which waited for: 2 -> 2; matrix products, arithmetic and copies ran while one was open for 0% -> 0% of each run, Pallas kernels for 22% -> 17%
where the time goes in v4:
time: 50.6 us; the launch traced here: 50 us
  starting transfers between devices  16.5 us (33%)
  Pallas kernels  13.5 us (27%)
  waiting for transfers between devices  8.76 us (17%)
  local copies, waits for them, and re-layouts  7.83 us (15%)
  between operations  3.42 us (7%)
    ppermute x7, starting transfers between devices, move(): lax.ppermute(block, 'dp', [(source, (source + shift) % replicas) for sour...  15 us
    ppermute x7, waiting for transfers between devices, move(): lax.ppermute(block, 'dp', [(source, (source + shift) % replicas) for sour...  8.75 us
    unnamed x36, local copies, waits for them, and re-layouts  7.83 us
    pallas_call x1, Pallas kernels, stay(): pl.pallas_call(functools.partial(stay_kernel, replicas, cap), out_shape=[...  5.43 us
    pallas_call x1, Pallas kernels, pack(): pl.pallas_call(functools.partial(states_kernel, replicas, cap), out_shape...  3.29 us
    pallas_call x1, Pallas kernels, arrive(): pl.pallas_call(functools.partial(arrive_kernel, replicas, cap), out_shape...  3.21 us
    pallas_call x1, Pallas kernels, pack(): pl.pallas_call(functools.partial(windows_kernel, replicas, cap, scan.shap...  1.55 us
    ppermute x4, starting transfers between devices, swap_heads(): return lax.ppermute(value, 'head', [(0, 1), (1, 0)])  1.45 us
  transfers between devices with their start and end apart: 11, of which 2 were waited for; matrix products, arithmetic and copies ran while one was open for 0% of the time, Pallas kernels for 17%

profile of v4, /device:TPU:0, one launch (start us, length us, event | category | flops | bytes accessed | tf_op | source)
XLA Modules:
  0.0 50.0 jit_solution(12195040174332517106)
XLA Ops:
  0.6 0.5 %collective-permute-start.1 = (bf16[64,4096]{1,0:T(8,128)(2,1)}, bf16[64,4096]{1,0:T(8,128)(2,1)S(1)}, u32[]{:S(2)}, u32[]{:S(2)}) collective-permute-start(bf16[64,4096]{1,0:T(8,128)(2,1)} %bitcast.13), channel_id=1, source_target_pairs={{0,1},{1,0},{2,3},{3,2},{4,5},{5,4},{6,7},{7,6},{8,9},{9,8},{10,11... | collective-permute-start | bytes 1572872 | tf_op jit(solution)/shard_map/ppermute | solution.py:636
  1.2 0.1 collective-permute-start
  1.2 0.4 collective-permute-start.3
  1.7 0.2 copy-done.16
  1.8 0.1 copy-done.17
  1.9 0.4 collective-permute-start.2
  2.3 3.3 %pack_states.1 = (bf16[1,496,128]{2,1,0:T(8,128)(2,1)}, bf16[1,496,128]{2,1,0:T(8,128)(2,1)}, bf16[1,496,128]{2,1,0:T(8,128)(2,1)}, bf16[1,496,128]{2,1,0:T(8,12...) custom-call(bf16[56,64,128]{2,1,0:T(8,128)(2,1)} %bitcast.11, ...), custom_call_target="tpu_custom_call" | custom-call | bytes 2000000 | tf_op jit(solution)/shard_map/pack_states/pallas_call | solution.py:157
  5.6 0.0 copy-start.1
  5.6 0.0 collective-permute-done.2.refs_9_.group_taps_other
  5.7 0.0 collective-permute-done.3.group_other
  5.7 0.0 collective-permute-done.refs_7_.other
  5.7 0.0 collective-permute-done.1.refs_8_.group_weight_other
  5.7 0.0 copy-done.14
  5.7 0.0 copy-start.5
  5.7 0.9 %copy-done.5 = bf16[56,3,128]{2,0,1:T(8,128)(2,1)S(1)} copy-done((bf16[56,3,128]{2,0,1:T(8,128)(2,1)S(1)}, bf16[56,3,128]{2,0,1:T(8,128)(2,1)}, u32[]{:S(2)}) %copy-start.5) | copy-done | bytes 43032
  6.6 0.8 %copy-done.7 = bf16[56,3,64]{2,0,1:T(8,128)(2,1)S(1)} copy-done((bf16[56,3,64]{2,0,1:T(8,128)(2,1)S(1)}, bf16[56,3,64]{2,0,1:T(8,128)(2,1)}, u32[]{:S(2)}) %copy-start.7) | copy-done | bytes 21528
  7.3 0.9 %copy-done.9 = bf16[1,496,128]{2,1,0:T(8,128)(2,1)S(1)} copy-done((bf16[1,496,128]{2,1,0:T(8,128)(2,1)S(1)}, bf16[1,496,128]{2,1,0:T(8,128)(2,1)}, u32[]{:S(2)}) %copy-start.9) | copy-done | bytes 127000
  8.2 0.9 %copy-done.10 = bf16[1,496,128]{2,1,0:T(8,128)(2,1)S(1)} copy-done((bf16[1,496,128]{2,1,0:T(8,128)(2,1)S(1)}, bf16[1,496,128]{2,1,0:T(8,128)(2,1)}, u32[]{:S(2)}) %copy-start.10) | copy-done | bytes 127000
  9.2 1.6 %pack_windows.1 = (bf16[1,496,128]{2,1,0:T(8,128)(2,1)S(1)}, bf16[1,496,128]{2,1,0:T(8,128)(2,1)S(1)}, bf16[1,496,128]{2,1,0:T(8,128)(2,1)}, bf16[1,496,128]{2,1...) custom-call(s32[1,56]{1,0:T(1,128)S(1)} %copy-done.14, ...), custom_call_target="tpu_custom_call", output_to_operand_aliasing={{0}: (4, {}), {1}: (5, {}), {2}: (6, {}), {3}: (7, {}), {4}... | custom-call | bytes 500000 | tf_op jit(solution)/shard_map/pack_windows/pallas_call | solution.py:173
  10.7 3.8 %collective-permute-start.4 = (bf16[1,496,128]{2,1,0:T(8,128)(2,1)S(1)}, bf16[1,496,128]{2,1,0:T(8,128)(2,1)S(1)}, u32[]{:S(2)}, u32[]{:S(2)}) collective-permute-start(bf16[1,496,128]{2,1,0:T(8,128)(2,1)S(1)} %get-tuple-element.40), channel_id=1, source_target_pairs={{0,8},{2,10},{4,12},{6,14},{8,0},{10,2},{12,4},{14,6},{1,9},{3,11}... | collective-permute-start | bytes 380936 | tf_op jit(solution)/shard_map/ppermute | solution.py:644
  14.5 2.5 %collective-permute-start.5 = (bf16[1,496,128]{2,1,0:T(8,128)(2,1)S(1)}, bf16[1,496,128]{2,1,0:T(8,128)(2,1)S(1)}, u32[]{:S(2)}, u32[]{:S(2)}) collective-permute-start(bf16[1,496,128]{2,1,0:T(8,128)(2,1)S(1)} %get-tuple-element.41), channel_id=1, source_target_pairs={{0,6},{2,8},{4,10},{6,12},{8,14},{10,0},{12,2},{14,4},{1,7},{3,9},... | collective-permute-start | bytes 380936 | tf_op jit(solution)/shard_map/ppermute | solution.py:644
  17.0 1.3 %collective-permute-start.6 = (bf16[1,496,128]{2,1,0:T(8,128)(2,1)}, bf16[1,496,128]{2,1,0:T(8,128)(2,1)S(1)}, u32[]{:S(2)}, u32[]{:S(2)}) collective-permute-start(bf16[1,496,128]{2,1,0:T(8,128)(2,1)} %get-tuple-element.53), channel_id=1, source_target_pairs={{0,10},{2,12},{4,14},{6,0},{8,2},{10,4},{12,6},{14,8},{1,11},{3,13... | collective-permute-start | bytes 380936 | tf_op jit(solution)/shard_map/ppermute | solution.py:644
  18.3 1.6 %collective-permute-start.7 = (bf16[1,496,128]{2,1,0:T(8,128)(2,1)}, bf16[1,496,128]{2,1,0:T(8,128)(2,1)S(1)}, u32[]{:S(2)}, u32[]{:S(2)}) collective-permute-start(bf16[1,496,128]{2,1,0:T(8,128)(2,1)} %get-tuple-element.54), channel_id=1, source_target_pairs={{0,4},{2,6},{4,8},{6,10},{8,12},{10,14},{12,0},{14,2},{1,5},{3,7},... | collective-permute-start | bytes 380936 | tf_op jit(solution)/shard_map/ppermute | solution.py:644
  19.9 2.2 %collective-permute-start.8 = (bf16[1,496,128]{2,1,0:T(8,128)(2,1)}, bf16[1,496,128]{2,1,0:T(8,128)(2,1)S(1)}, u32[]{:S(2)}, u32[]{:S(2)}) collective-permute-start(bf16[1,496,128]{2,1,0:T(8,128)(2,1)} %get-tuple-element.55), channel_id=1, source_target_pairs={{0,12},{2,14},{4,0},{6,2},{8,4},{10,6},{12,8},{14,10},{1,13},{3,15... | collective-permute-start | bytes 380936 | tf_op jit(solution)/shard_map/ppermute | solution.py:644
  22.2 7.6 %collective-permute-done.4.refs_0_ = bf16[1,496,128]{2,1,0:T(8,128)(2,1)S(1)} collective-permute-done((bf16[1,496,128]{2,1,0:T(8,128)(2,1)S(1)}, bf16[1,496,128]{2,1,0:T(8,128)(2,1)S(1)}, u32[]{:S(2)}, u32[]{:S(2)}) %collective-permute-start.4) | collective-permute-done | bytes 127008 | tf_op jit(solution)/shard_map/ppermute | solution.py:644
  29.7 0.0 collective-permute-start.9
  29.7 1.2 %collective-permute-done.5.refs_1_ = bf16[1,496,128]{2,1,0:T(8,128)(2,1)S(1)} collective-permute-done((bf16[1,496,128]{2,1,0:T(8,128)(2,1)S(1)}, bf16[1,496,128]{2,1,0:T(8,128)(2,1)S(1)}, u32[]{:S(2)}, u32[]{:S(2)}) %collective-permute-start.5) | collective-permute-done | bytes 127008 | tf_op jit(solution)/shard_map/ppermute | solution.py:644
  30.9 3.6 %collective-permute-start.10 = (bf16[1,496,128]{2,1,0:T(8,128)(2,1)}, bf16[1,496,128]{2,1,0:T(8,128)(2,1)S(1)}, u32[]{:S(2)}, u32[]{:S(2)}) collective-permute-start(bf16[1,496,128]{2,1,0:T(8,128)(2,1)} %get-tuple-element.57), channel_id=1, source_target_pairs={{0,14},{2,0},{4,2},{6,4},{8,6},{10,8},{12,10},{14,12},{1,15},{3,1}... | collective-permute-start | bytes 380936 | tf_op jit(solution)/shard_map/ppermute | solution.py:644
  37.1 0.0 copy-start.12
  37.1 0.0 copy-start.13
  37.1 0.0 copy-start.15
  37.1 0.0 copy-done.3
  37.1 0.0 copy-done.4
  37.1 0.0 copy-done.1
  37.1 0.0 copy-done
  37.1 0.6 %copy-done.12 = f32[4,128]{1,0:T(4,128)S(1)} copy-done((f32[4,128]{1,0:T(4,128)S(1)}, f32[4,128]{1,0:T(4,128)}, u32[]{:S(2)}) %copy-start.12) | copy-done | bytes 2072
  37.7 0.0 copy-done.13
  37.7 1.2 %copy-done.2 = bf16[4096,128]{1,0:T(8,128)(2,1)S(1)} copy-done((bf16[4096,128]{1,0:T(8,128)(2,1)S(1)}, bf16[4096,128]{1,0:T(8,128)(2,1)}, u32[]{:S(2)}) %copy-start.2) | copy-done | bytes 1048600
  39.0 0.8 %copy-done.6 = bf16[56,3,128]{2,0,1:T(8,128)(2,1)S(1)} copy-done((bf16[56,3,128]{2,0,1:T(8,128)(2,1)S(1)}, bf16[56,3,128]{2,0,1:T(8,128)(2,1)}, u32[]{:S(2)}) %copy-start.6) | copy-done | bytes 43032
  39.8 0.8 %copy-done.8 = bf16[56,3,64]{2,0,1:T(8,128)(2,1)S(1)} copy-done((bf16[56,3,64]{2,0,1:T(8,128)(2,1)S(1)}, bf16[56,3,64]{2,0,1:T(8,128)(2,1)}, u32[]{:S(2)}) %copy-start.8) | copy-done | bytes 21528
  40.5 0.7 %copy-done.11 = bf16[4096,1]{0,1:T(2,128)(2,1)S(1)} copy-done((bf16[4096,1]{0,1:T(2,128)(2,1)S(1)}, bf16[4096,1]{0,1:T(2,128)(2,1)}, u32[]{:S(2)}) %copy-start.11) | copy-done | bytes 8216
  41.3 5.4 %advance_staying.1 = (s32[1,128]{1,0:T(1,128)S(1)}, f32[112,128]{1,0:T(8,128)S(1)}, f32[8,128]{1,0:T(8,128)S(1)}, f32[112,128]{1,0:T(8,128)S(1)}, f32[112,128]{1...) custom-call(s32[1,56]{1,0:T(1,128)S(1)} %copy-done.15, ...), custom_call_target="tpu_custom_call" | custom-call | flops 300000000 | bytes 6000000 | tf_op jit(solution)/shard_map/advance_staying/pallas_call | solution.py:417
  46.7 0.0 collective-permute-done.6.refs_2_
  46.7 0.0 collective-permute-done.7.refs_3_
  46.7 0.0 collective-permute-done.8.refs_4_
  46.7 0.0 collective-permute-done.9.refs_5_
  46.7 0.0 collective-permute-done.10.refs_6_
  46.8 3.2 %advance_arrived.1 = (bf16[2,56,128]{2,1,0:T(8,128)(2,1)}, bf16[3,56,128]{2,1,0:T(8,128)(2,1)}, bf16[3,56,64]{2,1,0:T(8,128)(2,1)}, bf16[56,64,128]{2,1,0:T(8,128)(2,1)}) custom-call(s32[1,128]{1,0:T(1,128)S(1)} %get-tuple-element.42.plan, s32[1]{0:T(128)S(6)} %copy.41.live, f32[1]{0:T(128)S(6)} %copy.40.skip_gain, ...), custom_call_target="tpu_custom_call", output_to_operand_aliasing={{3}: (16, {})} | custom-call | flops 10000000 | bytes 2000000 | tf_op jit(solution)/shard_map/advance_arrived/pallas_call | solution.py:602
  (15 shorter events, 0.0 us)
Async XLA Ops:
  0.6 5.0 %collective-permute-start.1 = (bf16[64,4096]{1,0:T(8,128)(2,1)}, bf16[64,4096]{1,0:T(8,128)(2,1)S(1)}, u32[]{:S(2)}, u32[]{:S(2)}) collective-permute-start(bf16[64,4096]{1,0:T(8,128)(2,1)} %bitcast.13), channel_id=1, source_target_pairs={{0,1},{1,0},{2,3},{3,2},{4,5},{5,4},{6,7},{7,6},{8,9},{9,8},{10,11... | collective-permute-start | bytes 1572872 | tf_op jit(solution)/shard_map/ppermute | solution.py:636
  1.1 0.7 %copy-start.16 = (f32[4,64]{1,0:T(4,128)S(1)}, f32[4,64]{1,0:T(4,128)}, u32[]{:S(2)}) copy-start(f32[4,64]{1,0:T(4,128)} %param.25) | copy-start | bytes 3076
  1.2 4.5 %collective-permute-start = (bf16[112,2048]{1,0:T(8,128)(2,1)}, bf16[112,2048]{1,0:T(8,128)(2,1)S(1)}, u32[]{:S(2)}, u32[]{:S(2)}) collective-permute-start(bf16[112,2048]{1,0:T(8,128)(2,1)} %bitcast.15), channel_id=1, source_target_pairs={{0,1},{1,0},{2,3},{3,2},{4,5},{5,4},{6,7},{7,6},{8,9},{9,8},{10,11... | collective-permute-start | bytes 1376264 | tf_op jit(solution)/shard_map/ppermute | solution.py:636
  1.2 0.7 %copy-start.17 = (f32[64]{0:T(128)S(1)}, f32[64]{0:T(128)}, u32[]{:S(2)}) copy-start(f32[64]{0:T(128)} %param.26) | copy-start | bytes 772
  1.2 4.4 %collective-permute-start.3 = (bf16[3,56,64]{2,1,0:T(8,128)(2,1)}, bf16[3,56,64]{2,1,0:T(8,128)(2,1)S(1)}, u32[]{:S(2)}, u32[]{:S(2)}) collective-permute-start(bf16[3,56,64]{2,1,0:T(8,128)(2,1)} %bitcast.20), channel_id=1, source_target_pairs={{0,1},{1,0},{2,3},{3,2},{4,5},{5,4},{6,7},{7,6},{8,9},{9,8},{10,11... | collective-permute-start | bytes 64520 | tf_op jit(solution)/shard_map/ppermute | solution.py:636
  1.7 4.0 %copy-start.14 = (s32[1,56]{1,0:T(1,128)S(1)}, s32[1,56]{1,0:T(1,128)}, u32[]{:S(2)}) copy-start(s32[1,56]{1,0:T(1,128)} %send.3) | copy-start | bytes 676
  1.9 3.7 %collective-permute-start.2 = (f32[5,64]{1,0:T(8,128)S(1)}, f32[5,64]{1,0:T(8,128)S(1)}, u32[]{:S(2)}, u32[]{:S(2)}) collective-permute-start(f32[5,64]{1,0:T(8,128)S(1)} %pad_maximum_fusion.group_taps), channel_id=1, source_target_pairs={{0,1},{1,0},{2,3},{3,2},{4,5},{5,4},{6,7},{7,6},{8,9},{9,8},{10,11... | collective-permute-start | bytes 3848 | tf_op jit(solution)/shard_map/ppermute | solution.py:636
  2.3 34.8 %copy-start.3 = (bf16[4096,64]{0,1:T(8,128)(2,1)S(1)}, bf16[4096,64]{0,1:T(8,128)(2,1)}, u32[]{:S(2)}) copy-start(bf16[4096,64]{0,1:T(8,128)(2,1)} %param.21) | copy-start | bytes 1572868
  2.3 34.8 %copy-start.4 = (bf16[2,56,2048]{2,1,0:T(8,128)(2,1)S(1)}, bf16[2,56,2048]{2,1,0:T(8,128)(2,1)}, u32[]{:S(2)}) copy-start(bf16[2,56,2048]{2,1,0:T(8,128)(2,1)} %param.18) | copy-start | bytes 1376260
  5.6 31.5 %copy-start.1 = (bf16[4096,128]{1,0:T(8,128)(2,1)S(1)}, bf16[4096,128]{1,0:T(8,128)(2,1)}, u32[]{:S(2)}) copy-start(bf16[4096,128]{1,0:T(8,128)(2,1)} %inner_weight.1) | copy-start | bytes 3145732
  5.7 0.9 %copy-start.5 = (bf16[56,3,128]{2,0,1:T(8,128)(2,1)S(1)}, bf16[56,3,128]{2,0,1:T(8,128)(2,1)}, u32[]{:S(2)}) copy-start(bf16[56,3,128]{2,0,1:T(8,128)(2,1)} %param.30) | copy-start | bytes 129028
  6.6 0.8 %copy-start.7 = (bf16[56,3,64]{2,0,1:T(8,128)(2,1)S(1)}, bf16[56,3,64]{2,0,1:T(8,128)(2,1)}, u32[]{:S(2)}) copy-start(bf16[56,3,64]{2,0,1:T(8,128)(2,1)} %param.31) | copy-start | bytes 64516
  7.3 0.9 %copy-start.9 = (bf16[1,496,128]{2,1,0:T(8,128)(2,1)S(1)}, bf16[1,496,128]{2,1,0:T(8,128)(2,1)}, u32[]{:S(2)}) copy-start(bf16[1,496,128]{2,1,0:T(8,128)(2,1)} %get-tuple-element.33.refs_0_) | copy-start | bytes 380932
  8.2 0.9 %copy-start.10 = (bf16[1,496,128]{2,1,0:T(8,128)(2,1)S(1)}, bf16[1,496,128]{2,1,0:T(8,128)(2,1)}, u32[]{:S(2)}) copy-start(bf16[1,496,128]{2,1,0:T(8,128)(2,1)} %get-tuple-element.34.refs_1_) | copy-start | bytes 380932
  9.2 28.0 %copy-start = (bf16[56,128,64]{1,2,0:T(8,128)(2,1)S(1)}, bf16[56,128,64]{1,2,0:T(8,128)(2,1)}, u32[]{:S(2)}) copy-start(bf16[56,128,64]{1,2,0:T(8,128)(2,1)} %param.32) | copy-start | bytes 2752516
  10.7 19.0 %collective-permute-start.4 = (bf16[1,496,128]{2,1,0:T(8,128)(2,1)S(1)}, bf16[1,496,128]{2,1,0:T(8,128)(2,1)S(1)}, u32[]{:S(2)}, u32[]{:S(2)}) collective-permute-start(bf16[1,496,128]{2,1,0:T(8,128)(2,1)S(1)} %get-tuple-element.40), channel_id=1, source_target_pairs={{0,8},{2,10},{4,12},{6,14},{8,0},{10,2},{12,4},{14,6},{1,9},{3,11}... | collective-permute-start | bytes 380936 | tf_op jit(solution)/shard_map/ppermute | solution.py:644
  14.5 16.4 %collective-permute-start.5 = (bf16[1,496,128]{2,1,0:T(8,128)(2,1)S(1)}, bf16[1,496,128]{2,1,0:T(8,128)(2,1)S(1)}, u32[]{:S(2)}, u32[]{:S(2)}) collective-permute-start(bf16[1,496,128]{2,1,0:T(8,128)(2,1)S(1)} %get-tuple-element.41), channel_id=1, source_target_pairs={{0,6},{2,8},{4,10},{6,12},{8,14},{10,0},{12,2},{14,4},{1,7},{3,9},... | collective-permute-start | bytes 380936 | tf_op jit(solution)/shard_map/ppermute | solution.py:644
  17.0 29.7 %collective-permute-start.6 = (bf16[1,496,128]{2,1,0:T(8,128)(2,1)}, bf16[1,496,128]{2,1,0:T(8,128)(2,1)S(1)}, u32[]{:S(2)}, u32[]{:S(2)}) collective-permute-start(bf16[1,496,128]{2,1,0:T(8,128)(2,1)} %get-tuple-element.53), channel_id=1, source_target_pairs={{0,10},{2,12},{4,14},{6,0},{8,2},{10,4},{12,6},{14,8},{1,11},{3,13... | collective-permute-start | bytes 380936 | tf_op jit(solution)/shard_map/ppermute | solution.py:644
  18.3 28.4 %collective-permute-start.7 = (bf16[1,496,128]{2,1,0:T(8,128)(2,1)}, bf16[1,496,128]{2,1,0:T(8,128)(2,1)S(1)}, u32[]{:S(2)}, u32[]{:S(2)}) collective-permute-start(bf16[1,496,128]{2,1,0:T(8,128)(2,1)} %get-tuple-element.54), channel_id=1, source_target_pairs={{0,4},{2,6},{4,8},{6,10},{8,12},{10,14},{12,0},{14,2},{1,5},{3,7},... | collective-permute-start | bytes 380936 | tf_op jit(solution)/shard_map/ppermute | solution.py:644
  19.9 26.8 %collective-permute-start.8 = (bf16[1,496,128]{2,1,0:T(8,128)(2,1)}, bf16[1,496,128]{2,1,0:T(8,128)(2,1)S(1)}, u32[]{:S(2)}, u32[]{:S(2)}) collective-permute-start(bf16[1,496,128]{2,1,0:T(8,128)(2,1)} %get-tuple-element.55), channel_id=1, source_target_pairs={{0,12},{2,14},{4,0},{6,2},{8,4},{10,6},{12,8},{14,10},{1,13},{3,15... | collective-permute-start | bytes 380936 | tf_op jit(solution)/shard_map/ppermute | solution.py:644
  29.7 17.0 %collective-permute-start.9 = (bf16[1,496,128]{2,1,0:T(8,128)(2,1)}, bf16[1,496,128]{2,1,0:T(8,128)(2,1)S(1)}, u32[]{:S(2)}, u32[]{:S(2)}) collective-permute-start(bf16[1,496,128]{2,1,0:T(8,128)(2,1)} %get-tuple-element.56), channel_id=1, source_target_pairs={{0,2},{2,4},{4,6},{6,8},{8,10},{10,12},{12,14},{14,0},{1,3},{3,5},... | collective-permute-start | bytes 380936 | tf_op jit(solution)/shard_map/ppermute | solution.py:644
  30.9 15.8 %collective-permute-start.10 = (bf16[1,496,128]{2,1,0:T(8,128)(2,1)}, bf16[1,496,128]{2,1,0:T(8,128)(2,1)S(1)}, u32[]{:S(2)}, u32[]{:S(2)}) collective-permute-start(bf16[1,496,128]{2,1,0:T(8,128)(2,1)} %get-tuple-element.57), channel_id=1, source_target_pairs={{0,14},{2,0},{4,2},{6,4},{8,6},{10,8},{12,10},{14,12},{1,15},{3,1}... | collective-permute-start | bytes 380936 | tf_op jit(solution)/shard_map/ppermute | solution.py:644
  37.1 0.7 %copy-start.12 = (f32[4,128]{1,0:T(4,128)S(1)}, f32[4,128]{1,0:T(4,128)}, u32[]{:S(2)}) copy-start(f32[4,128]{1,0:T(4,128)} %inner_taps.3) | copy-start | bytes 6148
  37.1 0.7 %copy-start.13 = (f32[128]{0:T(128)S(1)}, f32[128]{0:T(128)}, u32[]{:S(2)}) copy-start(f32[128]{0:T(128)} %param.24) | copy-start | bytes 1540
  37.1 0.7 %copy-start.15 = (s32[1,56]{1,0:T(1,128)S(1)}, s32[1,56]{1,0:T(1,128)}, u32[]{:S(2)}) copy-start(s32[1,56]{1,0:T(1,128)} %receive.1) | copy-start | bytes 676
  37.7 1.2 %copy-start.2 = (bf16[4096,128]{1,0:T(8,128)(2,1)S(1)}, bf16[4096,128]{1,0:T(8,128)(2,1)}, u32[]{:S(2)}) copy-start(bf16[4096,128]{1,0:T(8,128)(2,1)} %gate_weight.1) | copy-start | bytes 3145732
  39.0 0.8 %copy-start.6 = (bf16[56,3,128]{2,0,1:T(8,128)(2,1)S(1)}, bf16[56,3,128]{2,0,1:T(8,128)(2,1)}, u32[]{:S(2)}) copy-start(bf16[56,3,128]{2,0,1:T(8,128)(2,1)} %param.30) | copy-start | bytes 129028
  39.8 0.8 %copy-start.8 = (bf16[56,3,64]{2,0,1:T(8,128)(2,1)S(1)}, bf16[56,3,64]{2,0,1:T(8,128)(2,1)}, u32[]{:S(2)}) copy-start(bf16[56,3,64]{2,0,1:T(8,128)(2,1)} %param.31) | copy-start | bytes 64516
  40.5 0.7 %copy-start.11 = (bf16[4096,1]{0,1:T(2,128)(2,1)S(1)}, bf16[4096,1]{0,1:T(2,128)(2,1)}, u32[]{:S(2)}) copy-start(bf16[4096,1]{0,1:T(2,128)(2,1)} %param.22) | copy-start | bytes 24580
